TPU v7x, 256 devices: a whole 4x4x8 slice. The times are simulated.
256 devices in a mesh: seq: 64 (over z, y_lo, x), tp: 4 (over y_hi, core).
Axes of the slice: x: 4, y: 4 (y_hi: 2, y_lo: 2; y = y_hi * 2 + y_lo), z: 8, core: 2. Of those that a mesh axis runs over, the one named last changes fastest.
Arguments:
- latent: bfloat16 [64, 128, 4096], P('seq', None, 'tp'), may hold values from -6 to 6
- direction: bfloat16 [64, 128, 4096], P('seq', None, 'tp'), may hold values from -6 to 6
- concept: int32 [64], P('seq'), may hold values from 0 to 255
- timestep: int32 [64], replicated, may hold values from 0 to 999
- concept_table: bfloat16 [256, 4096], P(None, 'tp'), may hold values from -1.5 to 1.5
- w_query: bfloat16 [4096, 2048], P(None, 'tp'), may hold values from -2 to 2
- w_key: bfloat16 [4096, 2048], P(None, 'tp'), may hold values from -2 to 2
Outputs:
- score_field: bfloat16 [64, 128, 4096], P('seq', None, 'tp')
- table_grad: float32 [256, 4096], P(None, ('seq', 'tp'))
All inputs are finite; a program needn't handle non-finite values.
Results may differ from a plain program's by a relative error of at most 0.015.
Values may be sent and summed in bfloat16 or wider, within the bound.
No kernel may reach another device: no remote copies, remote signals or barrier semaphores. Data moves between devices by JAX's collectives and lax.ppermute only.
A program may use at most 64 MiB of HBM per device.

v0:
```python
import math

import jax
import jax.numpy as jnp
from jax import lax
from jax.sharding import PartitionSpec as P

HD = 128
CONCEPTS = 256
STEPS = 1000


EPS = 1e-06


def normalize(values, tangent):
    mean_sq = jnp.mean(values * values, axis=-1, keepdims=True)
    inv_rms = lax.rsqrt(mean_sq + EPS)
    normed = values * inv_rms
    normed_tan = inv_rms * (tangent - normed * jnp.mean(normed * tangent, axis=-1, keepdims=True))
    return (normed, normed_tan, inv_rms)


def energy_cotangents(query_rows, key_rows, query_tan, key_tan, inv_temp):
    query_f = query_rows.astype(jnp.float32)
    key_f = key_rows.astype(jnp.float32)
    qtan_f = query_tan.astype(jnp.float32)
    ktan_f = key_tan.astype(jnp.float32)
    temp_b = inv_temp[None, None, :, None]
    scores = jnp.einsum("fphd,gphd->phfg", query_f, key_f) * temp_b
    top = jnp.max(scores, axis=-1, keepdims=True)
    weights = jnp.exp(scores - top)
    weights = weights / jnp.sum(weights, axis=-1, keepdims=True)
    tangent_dot = jnp.einsum("fphd,gphd->phfg", qtan_f, key_f) + jnp.einsum(
        "fphd,gphd->phfg", query_f, ktan_f
    )
    mean_tan = jnp.sum(weights * tangent_dot, axis=-1, keepdims=True)
    curvature = -temp_b * weights * (tangent_dot - mean_tan)
    grad_query = -jnp.einsum("phfg,gphd->fphd", weights, key_f)
    grad_key = -jnp.einsum("phfg,fphd->gphd", weights, query_f)
    adj_query = jnp.einsum("phfg,gphd->fphd", curvature, key_f) - jnp.einsum(
        "phfg,gphd->fphd", weights, ktan_f
    )
    adj_key = jnp.einsum("phfg,fphd->gphd", curvature, query_f) - jnp.einsum(
        "phfg,fphd->gphd", weights, qtan_f
    )
    return (
        adj_query.astype(jnp.bfloat16),
        adj_key.astype(jnp.bfloat16),
        grad_query.astype(jnp.bfloat16),
        grad_key.astype(jnp.bfloat16),
    )


def project(inputs, weight):
    flat = inputs.reshape(-1, inputs.shape[-1])
    out = jnp.dot(flat, weight, preferred_element_type=jnp.float32).astype(jnp.bfloat16)
    return out.reshape(inputs.shape[0], inputs.shape[1], -1, HD)


def project_back(first, first_w, second, second_w):
    lead = first.shape[0] * first.shape[1]
    part_one = jnp.dot(first.reshape(lead, -1), first_w.T, preferred_element_type=jnp.float32)
    part_two = jnp.dot(second.reshape(lead, -1), second_w.T, preferred_element_type=jnp.float32)
    return (part_one + part_two).reshape(first.shape[0], first.shape[1], -1)


def body(latent, direction, concept, timestep, concept_table, w_query, w_key):
    full_latent, full_dir, full_table = (
        lax.all_gather(latent, "tp", axis=2, tiled=True),
        lax.all_gather(direction, "tp", axis=2, tiled=True),
        lax.all_gather(concept_table, "tp", axis=1, tiled=True),
    )
    width = full_latent.shape[2]
    local_width = latent.shape[2]
    values = full_latent.astype(jnp.float32)
    tangent = full_dir.astype(jnp.float32)
    normed, normed_tan, inv_rms = normalize(values, tangent)
    onehot = (concept[:, None] == jnp.arange(CONCEPTS, dtype=jnp.int32)[None, :]).astype(
        jnp.float32
    )
    modul = 1.0 + jnp.dot(onehot, full_table.astype(jnp.float32), precision=lax.Precision.HIGHEST)
    hidden = (normed * modul[:, None, :]).astype(jnp.bfloat16)
    hidden_tan = (normed_tan * modul[:, None, :]).astype(jnp.bfloat16)
    query_rows = project(hidden, w_query)
    key_rows = project(hidden, w_key)
    query_tan = project(hidden_tan, w_query)
    key_tan = project(hidden_tan, w_key)
    inv_temp = (0.25 + 1.75 * timestep.astype(jnp.float32) / STEPS) / math.sqrt(HD)
    results = energy_cotangents(
        lax.all_to_all(query_rows, "seq", split_axis=1, concat_axis=0, tiled=True),
        lax.all_to_all(key_rows, "seq", split_axis=1, concat_axis=0, tiled=True),
        lax.all_to_all(query_tan, "seq", split_axis=1, concat_axis=0, tiled=True),
        lax.all_to_all(key_tan, "seq", split_axis=1, concat_axis=0, tiled=True),
        inv_temp,
    )
    adj_query = lax.all_to_all(results[0], "seq", split_axis=0, concat_axis=1, tiled=True)
    adj_key = lax.all_to_all(results[1], "seq", split_axis=0, concat_axis=1, tiled=True)
    grad_query = lax.all_to_all(results[2], "seq", split_axis=0, concat_axis=1, tiled=True)
    grad_key = lax.all_to_all(results[3], "seq", split_axis=0, concat_axis=1, tiled=True)
    units = project_back(grad_query, w_query, grad_key, w_key)
    drift = project_back(adj_query, w_query, adj_key, w_key)
    terms = jnp.sum(normed * drift + normed_tan * units, axis=1)
    seq_count = lax.axis_size("seq")
    tp_count = lax.axis_size("tp")
    column_block = width // (seq_count * tp_count)
    frame_count = terms.shape[0]
    reordered = terms.reshape(frame_count, seq_count, tp_count, column_block)
    reordered = jnp.transpose(reordered, (0, 2, 1, 3)).reshape(frame_count, width)
    own_terms = lax.psum_scatter(reordered, "tp", scatter_dimension=1, tiled=True)
    all_frames = lax.all_to_all(own_terms, "seq", split_axis=1, concat_axis=0, tiled=True)
    all_concepts = lax.all_gather(concept, "seq", axis=0, tiled=True)
    all_onehot = (all_concepts[:, None] == jnp.arange(CONCEPTS, dtype=jnp.int32)[None, :]).astype(
        jnp.float32
    )
    table_grad = jnp.dot(all_onehot.T, all_frames, precision=lax.Precision.HIGHEST)
    start = lax.axis_index("tp") * local_width
    summed = lax.psum(units, "tp")
    gain = modul[:, None, :] * summed
    full_score = inv_rms * (gain - normed * jnp.mean(gain * normed, axis=-1, keepdims=True))
    score_field = lax.dynamic_slice_in_dim(full_score, start, local_width, 2).astype(jnp.bfloat16)
    return (score_field, table_grad)


def solution(mesh):
    in_specs = (
        P("seq", None, "tp"),
        P("seq", None, "tp"),
        P("seq"),
        P(),
        P(None, "tp"),
        P(None, "tp"),
        P(None, "tp"),
    )
    out_specs = (P("seq", None, "tp"), P(None, ("seq", "tp")))
    return jax.shard_map(body, mesh=mesh, in_specs=in_specs, out_specs=out_specs, check_vma=False)
```

profile of v0, /device:TPU:8, one launch (start us, length us, event | category | flops | bytes accessed | tf_op | source)
XLA Modules:
  0.0 373.3 jit_solution(4697385422711323578)
XLA Ops:
  7.2 0.7 all-gather.4.cloned.1.call-update
  7.9 0.7 all-gather.6.cloned.1.call-update
  9.3 25.9 %all-gather.4.cloned.1.call-done = bf16[1,128,4096]{2,1,0:T(8,128)(2,1)} async-done(((bf16[1,128,1024]{2,1,0:T(8,128)(2,1)}), bf16[1,128,4096]{2,1,0:T(8,128)(2,1)}) %all-gather.4.cloned.1.call-update) | async-done | bytes 1048592 | tf_op jit(solution)/shard_map/all_gather | solution.py:70
  35.2 1.6 fusion.4
  36.8 28.9 %all-gather.6.cloned.1.call-done = bf16[256,4096]{1,0:T(8,128)(2,1)} async-done(((bf16[256,1024]{1,0:T(8,128)(2,1)}), bf16[256,4096]{1,0:T(8,128)(2,1)}) %all-gather.6.cloned.1.call-update) | async-done | bytes 2097168 | tf_op jit(solution)/shard_map/all_gather | solution.py:72
  65.6 2.0 fusion.61
  67.6 3.0 convolution_convert_fusion.3
  70.6 0.7 reshape.136
  71.3 11.4 %all-to-all-start = ((bf16[1,128,4,128]{3,2,0,1:T(4,128)(2,1)}), bf16[1,128,4,128]{3,2,0,1:T(4,128)(2,1)S(1)}, u32[]{:S(2)}, u32[]{:S(2)}) async-start(bf16[1,128,4,128]{3,2,0,1:T(4,128)(2,1)} %bitcast.3), calls=%async_computation | async-start | bytes 262144 | tf_op jit(solution)/shard_map/all_to_all | solution.py:92
  82.8 3.0 convolution_convert_fusion.2
  85.7 0.7 reshape.137
  86.4 7.1 %all-to-all-done = bf16[1,128,4,128]{3,2,0,1:T(4,128)(2,1)S(1)} async-done(((bf16[1,128,4,128]{3,2,0,1:T(4,128)(2,1)}), bf16[1,128,4,128]{3,2,0,1:T(4,128)(2,1)S(1)}, u32[]{:S(2)}, u32[]{:S(2)}) %all-to-all-start) | async-done | bytes 131104 | tf_op jit(solution)/shard_map/all_to_all | solution.py:92
  93.5 5.0 %all-to-all-start.1 = ((bf16[1,128,4,128]{3,2,0,1:T(4,128)(2,1)}), bf16[1,128,4,128]{3,2,0,1:T(4,128)(2,1)S(1)}, u32[]{:S(2)}, u32[]{:S(2)}) async-start(bf16[1,128,4,128]{3,2,0,1:T(4,128)(2,1)} %bitcast.5), calls=%async_computation.1 | async-start | bytes 262144 | tf_op jit(solution)/shard_map/all_to_all | solution.py:91
  98.5 0.7 all-gather.8.cloned.1.call-update
  99.2 0.5 fusion.51
  99.8 9.2 %all-to-all-done.1 = bf16[1,128,4,128]{3,2,0,1:T(4,128)(2,1)S(1)} async-done(((bf16[1,128,4,128]{3,2,0,1:T(4,128)(2,1)}), bf16[1,128,4,128]{3,2,0,1:T(4,128)(2,1)S(1)}, u32[]{:S(2)}, u32[]{:S(2)}) %all-to-all-start.1) | async-done | bytes 131104 | tf_op jit(solution)/shard_map/all_to_all | solution.py:91
  109.0 0.2 fusion.60
  109.2 0.1 fusion.23
  109.3 0.2 fusion.15
  109.5 0.8 copy.44
  110.3 5.1 %all-to-all-start.2 = ((bf16[64,2,4,128]{3,2,1,0:T(4,128)(2,1)}), bf16[64,2,4,128]{3,2,1,0:T(4,128)(2,1)S(1)}, u32[]{:S(2)}, u32[]{:S(2)}) async-start(bf16[64,2,4,128]{3,2,1,0:T(4,128)(2,1)} %copy.44), calls=%async_computation.2 | async-start | bytes 262144 | tf_op jit(solution)/shard_map/all_to_all | solution.py:99
  115.3 0.2 fusion.14
  115.5 0.8 copy.46
  116.3 9.5 %all-to-all-done.2 = bf16[64,2,4,128]{3,2,1,0:T(4,128)(2,1)S(1)} async-done(((bf16[64,2,4,128]{3,2,1,0:T(4,128)(2,1)}), bf16[64,2,4,128]{3,2,1,0:T(4,128)(2,1)S(1)}, u32[]{:S(2)}, u32[]{:S(2)}) %all-to-all-start.2) | async-done | bytes 131104 | tf_op jit(solution)/shard_map/all_to_all | solution.py:99
  125.8 5.9 %all-to-all-start.3 = ((bf16[64,2,4,128]{3,2,1,0:T(4,128)(2,1)}), bf16[64,2,4,128]{3,2,1,0:T(4,128)(2,1)}, u32[]{:S(2)}, u32[]{:S(2)}) async-start(bf16[64,2,4,128]{3,2,1,0:T(4,128)(2,1)} %copy.46), calls=%async_computation.3 | async-start | bytes 262144 | tf_op jit(solution)/shard_map/all_to_all | solution.py:100
  131.7 3.7 %fusion.31 = f32[128,4096]{1,0:T(8,128)S(1)} fusion(bf16[4096,512]{1,0:T(8,128)(2,1)} %param.12, bf16[16,8,4,128]{3,2,1,0:T(4,128)(2,1)} %bitcast.88), kind=kOutput, calls=%fused_computation.55 | convolution fusion | flops 536870912 | bytes 6422528 | tf_op jit(solution)/shard_map/dot_general | solution.py:63
  135.5 6.5 %all-to-all-done.3 = bf16[64,2,4,128]{3,2,1,0:T(4,128)(2,1)} async-done(((bf16[64,2,4,128]{3,2,1,0:T(4,128)(2,1)}), bf16[64,2,4,128]{3,2,1,0:T(4,128)(2,1)}, u32[]{:S(2)}, u32[]{:S(2)}) %all-to-all-start.3) | async-done | bytes 131104 | tf_op jit(solution)/shard_map/all_to_all | solution.py:100
  142.0 5.1 %fusion.3 = f32[1,128,4096]{2,1,0:T(8,128)} fusion(f32[128,4096]{1,0:T(8,128)S(1)} %fusion.31, bf16[4096,512]{1,0:T(8,128)(2,1)} %param.13, bf16[16,8,4,128]{3,2,1,0:T(4,128)(2,1)} %bitcast.28), kind=kOutput, calls=%fused_computation.5 | convolution fusion | flops 537395200 | bytes 8519680 | tf_op jit(solution)/shard_map/dot_general | solution.py:64
  147.2 57.8 %all-reduce.3.cloned.1.call-done = f32[1,128,4096]{2,1,0:T(8,128)} async-done(((f32[1,128,4096]{2,1,0:T(8,128)}), f32[1,128,4096]{2,1,0:T(8,128)}) %all-reduce.3.cloned.1.call-update) | async-done | bytes 2097168 | tf_op jit(solution)/shard_map/psum | solution.py:118
  205.0 5.2 %fusion.5 = (f32[128]{0:T(128)S(1)}, f32[128]{0:T(128)}, f32[1,128,4096]{2,1,0:T(8,128)}, f32[1,128,4096]{2,1,0:T(8,128)}) fusion(bf16[1,128,4096]{2,1,0:T(8,128)(2,1)} %all-gather.8.cloned.1.call-done, bf16[1,128,4096]{2,1,0:T(8,128)(2,1)S(1)} %copy-done.2, f32[128]{0:T(128)S(1)} %copy-done.11, f32[1,128,4096]{2,1,0:T(8,128)} %all-reduce.3.cloned.1.call-done, ...), kind=kLoop, calls=%fused_computation.11 | loop fusion | flops 4194048 | bytes 8406528 | tf_op jit(solution)/shard_map/reduce_sum | solution.py:20
  210.1 0.8 convolution_convert_fusion.1
  210.9 0.7 reshape.142
  211.6 11.4 %all-to-all-start.4 = ((bf16[1,128,4,128]{3,2,0,1:T(4,128)(2,1)}), bf16[1,128,4,128]{3,2,0,1:T(4,128)(2,1)S(1)}, u32[]{:S(2)}, u32[]{:S(2)}) async-start(bf16[1,128,4,128]{3,2,0,1:T(4,128)(2,1)} %bitcast.12), calls=%async_computation.4 | async-start | bytes 262144 | tf_op jit(solution)/shard_map/all_to_all | solution.py:93
  223.2 3.0 convolution_convert_fusion
  226.2 0.7 reshape.143
  226.9 6.9 %all-to-all-done.4 = bf16[1,128,4,128]{3,2,0,1:T(4,128)(2,1)S(1)} async-done(((bf16[1,128,4,128]{3,2,0,1:T(4,128)(2,1)}), bf16[1,128,4,128]{3,2,0,1:T(4,128)(2,1)S(1)}, u32[]{:S(2)}, u32[]{:S(2)}) %all-to-all-start.4) | async-done | bytes 131104 | tf_op jit(solution)/shard_map/all_to_all | solution.py:93
  233.8 5.2 %all-to-all-start.5 = ((bf16[1,128,4,128]{3,2,0,1:T(4,128)(2,1)}), bf16[1,128,4,128]{3,2,0,1:T(4,128)(2,1)S(1)}, u32[]{:S(2)}, u32[]{:S(2)}) async-start(bf16[1,128,4,128]{3,2,0,1:T(4,128)(2,1)} %bitcast.14), calls=%async_computation.5 | async-start | bytes 262144 | tf_op jit(solution)/shard_map/all_to_all | solution.py:94
  239.0 0.6 dynamic-slice
  239.6 0.8 dynamic-update-slice
  240.3 22.7 %all-reduce = s32[64]{0:T(128)S(1)} all-reduce(s32[64]{0:T(128)S(1)} %dynamic-update-slice), channel_id=1, replica_groups=mesh['seq'=64,'tp'=4] {'seq'}, use_global_device_ids=true, to_apply=%add | all-reduce | flops 64 | bytes 512
  263.0 0.2 fusion.37
  263.3 0.2 multiply_reduce_fusion.1
  263.5 0.3 fusion.40
  263.8 0.2 fusion.13
  264.0 0.8 copy.59
  264.8 7.0 %all-to-all-start.6 = ((bf16[64,2,4,128]{3,2,1,0:T(4,128)(2,1)}), bf16[64,2,4,128]{3,2,1,0:T(4,128)(2,1)S(1)}, u32[]{:S(2)}, u32[]{:S(2)}) async-start(bf16[64,2,4,128]{3,2,1,0:T(4,128)(2,1)} %copy.59), calls=%async_computation.6 | async-start | bytes 262144 | tf_op jit(solution)/shard_map/all_to_all | solution.py:97
  271.8 0.2 fusion.44
  272.0 0.2 fusion.12
  272.2 0.8 copy.62
  273.0 9.2 %all-to-all-done.6 = bf16[64,2,4,128]{3,2,1,0:T(4,128)(2,1)S(1)} async-done(((bf16[64,2,4,128]{3,2,1,0:T(4,128)(2,1)}), bf16[64,2,4,128]{3,2,1,0:T(4,128)(2,1)S(1)}, u32[]{:S(2)}, u32[]{:S(2)}) %all-to-all-start.6) | async-done | bytes 131104 | tf_op jit(solution)/shard_map/all_to_all | solution.py:97
  282.2 5.1 %all-to-all-start.7 = ((bf16[64,2,4,128]{3,2,1,0:T(4,128)(2,1)}), bf16[64,2,4,128]{3,2,1,0:T(4,128)(2,1)S(1)}, u32[]{:S(2)}, u32[]{:S(2)}) async-start(bf16[64,2,4,128]{3,2,1,0:T(4,128)(2,1)} %copy.62), calls=%async_computation.7 | async-start | bytes 262144 | tf_op jit(solution)/shard_map/all_to_all | solution.py:98
  287.3 0.0 reduce-scatter.4.cloned.1.call-start
  287.3 5.3 %fusion.26 = f32[128,4096]{1,0:T(8,128)} fusion(bf16[4096,512]{1,0:T(8,128)(2,1)} %param.12, bf16[16,8,4,128]{3,2,1,0:T(4,128)(2,1)} %bitcast.87), kind=kOutput, calls=%fused_computation.50 | convolution fusion | flops 536870912 | bytes 6422528 | tf_op jit(solution)/shard_map/dot_general | solution.py:63
  292.6 5.1 %all-to-all-done.7 = bf16[64,2,4,128]{3,2,1,0:T(4,128)(2,1)S(1)} async-done(((bf16[64,2,4,128]{3,2,1,0:T(4,128)(2,1)}), bf16[64,2,4,128]{3,2,1,0:T(4,128)(2,1)S(1)}, u32[]{:S(2)}, u32[]{:S(2)}) %all-to-all-start.7) | async-done | bytes 131104 | tf_op jit(solution)/shard_map/all_to_all | solution.py:98
  297.7 4.7 %fusion.7 = f32[4096]{0:T(1024)S(1)} fusion(f32[1,128,4096]{2,1,0:T(8,128)S(1)} %copy-done, bf16[1,128,4096]{2,1,0:T(8,128)(2,1)} %all-gather.8.cloned.1.call-done, f32[128,4096]{1,0:T(8,128)} %fusion.26, bf16[4096,512]{1,0:T(8,128)(2,1)} %param.13, bf16[1,128,4096]{2,1,0:T(8,128)(2,1)S(1)} %copy-done.2, f32[128]{0:T(128)S(1)} %copy-done.17, ...), kind=kOutput, calls=%fused_computation.16 | convolution fusion | flops 542633984 | bytes 10634240 | tf_op jit(solution)/shard_map/dot_general | solution.py:64
  302.4 0.1 reshape.147
  302.6 2.5 reshape.158
  305.1 37.8 %reduce-scatter.4.cloned.1.call-done = f32[1024,1]{1,0:T(8,128)} async-done(((f32[4096,1]{1,0:T(8,128)}), f32[1024,1]{1,0:T(8,128)}) %reduce-scatter.4.cloned.1.call-update) | async-done | bytes 4112
  343.0 1.2 bitcast_reduce_fusion
  344.2 0.7 all_to_all.43
  344.9 11.4 %all-to-all-start.8 = ((f32[1,64,16]{2,0,1:T(1,128)}), f32[1,64,16]{2,0,1:T(1,128)S(1)}, u32[]{:S(2)}, u32[]{:S(2)}) async-start(f32[1,64,16]{2,0,1:T(1,128)} %bitcast.20), calls=%async_computation.8 | async-start | bytes 65536 | tf_op jit(solution)/shard_map/all_to_all | solution.py:111
  356.4 2.1 fusion.19
  358.4 7.5 %all-to-all-done.8 = f32[1,64,16]{2,0,1:T(1,128)S(1)} async-done(((f32[1,64,16]{2,0,1:T(1,128)}), f32[1,64,16]{2,0,1:T(1,128)S(1)}, u32[]{:S(2)}, u32[]{:S(2)}) %all-to-all-start.8) | async-done | bytes 4128 | tf_op jit(solution)/shard_map/all_to_all | solution.py:111
  365.9 0.8 fusion.49
  (62 shorter events, 0.4 us)
Async XLA Ops:
  7.2 28.0 %all-gather.4.cloned.1.call-start = ((), (), s32[]{:S(2)}) async-start(), calls=%async_computation.10 | async-start | bytes 1310720 | tf_op jit(solution)/shard_map/all_gather | solution.py:70
  7.9 57.7 %all-gather.6.cloned.1.call-start = ((), (), s32[]{:S(2)}) async-start(), calls=%async_computation.11 | async-start | bytes 2621440 | tf_op jit(solution)/shard_map/all_gather | solution.py:72
  35.2 32.5 %copy-start.2 = (bf16[1,128,4096]{2,1,0:T(8,128)(2,1)S(1)}, bf16[1,128,4096]{2,1,0:T(8,128)(2,1)}, u32[]{:S(2)}) copy-start(bf16[1,128,4096]{2,1,0:T(8,128)(2,1)} %all-gather.4.cloned.1.call-done) | copy-start | bytes 3145732
  36.8 45.9 %copy-start.10 = (f32[128]{0:T(128)}, f32[128]{0:T(128)S(1)}, u32[]{:S(2)}) copy-start(f32[128]{0:T(128)S(1)} %add_rsqrt_fusion) | copy-start | bytes 1540
  71.3 22.2 %all-to-all-start = ((bf16[1,128,4,128]{3,2,0,1:T(4,128)(2,1)}), bf16[1,128,4,128]{3,2,0,1:T(4,128)(2,1)S(1)}, u32[]{:S(2)}, u32[]{:S(2)}) async-start(bf16[1,128,4,128]{3,2,0,1:T(4,128)(2,1)} %bitcast.3), calls=%async_computation | async-start | bytes 262144 | tf_op jit(solution)/shard_map/all_to_all | solution.py:92
  82.7 16.5 %copy-start.18 = (s32[64]{0:T(128)S(1)}, s32[64]{0:T(128)}, u32[]{:S(2)}) copy-start(s32[64]{0:T(128)} %param.10) | copy-start | bytes 772
  93.5 15.4 %all-to-all-start.1 = ((bf16[1,128,4,128]{3,2,0,1:T(4,128)(2,1)}), bf16[1,128,4,128]{3,2,0,1:T(4,128)(2,1)S(1)}, u32[]{:S(2)}, u32[]{:S(2)}) async-start(bf16[1,128,4,128]{3,2,0,1:T(4,128)(2,1)} %bitcast.5), calls=%async_computation.1 | async-start | bytes 262144 | tf_op jit(solution)/shard_map/all_to_all | solution.py:91
  98.5 48.7 %all-gather.8.cloned.1.call-start = ((), (), s32[]{:S(2)}) async-start(), calls=%async_computation.13 | async-start | bytes 1310720 | tf_op jit(solution)/shard_map/all_gather | solution.py:71
  108.9 16.9 %copy-start.4 = (bf16[1,128,4,128]{3,1,2,0:T(8,128)(2,1)}, bf16[1,128,4,128]{3,1,2,0:T(8,128)(2,1)S(1)}, u32[]{:S(2)}) copy-start(bf16[1,128,4,128]{3,1,2,0:T(8,128)(2,1)S(1)} %copy.39) | copy-start | bytes 393220
  109.2 22.5 %copy-start.8 = (f32[2,4,64]{2,1,0:T(4,128)}, f32[2,4,64]{2,1,0:T(4,128)S(1)}, u32[]{:S(2)}) copy-start(f32[2,4,64]{2,1,0:T(4,128)S(1)} %get-tuple-element.8) | copy-start | bytes 6148
  109.3 22.5 %copy-start.13 = (f32[2,4,64]{2,1,0:T(4,128)}, f32[2,4,64]{2,1,0:T(4,128)S(1)}, u32[]{:S(2)}) copy-start(f32[2,4,64]{2,1,0:T(4,128)S(1)} %fusion.23) | copy-start | bytes 6148
  110.3 15.5 %all-to-all-start.2 = ((bf16[64,2,4,128]{3,2,1,0:T(4,128)(2,1)}), bf16[64,2,4,128]{3,2,1,0:T(4,128)(2,1)S(1)}, u32[]{:S(2)}, u32[]{:S(2)}) async-start(bf16[64,2,4,128]{3,2,1,0:T(4,128)(2,1)} %copy.44), calls=%async_computation.2 | async-start | bytes 262144 | tf_op jit(solution)/shard_map/all_to_all | solution.py:99
  125.8 5.9 %copy-start.7 = (bf16[64,2,4,128]{3,2,1,0:T(4,128)(2,1)}, bf16[64,2,4,128]{3,2,1,0:T(4,128)(2,1)S(1)}, u32[]{:S(2)}) copy-start(bf16[64,2,4,128]{3,2,1,0:T(4,128)(2,1)S(1)} %all-to-all-done.2) | copy-start | bytes 393220
  125.8 16.2 %all-to-all-start.3 = ((bf16[64,2,4,128]{3,2,1,0:T(4,128)(2,1)}), bf16[64,2,4,128]{3,2,1,0:T(4,128)(2,1)}, u32[]{:S(2)}, u32[]{:S(2)}) async-start(bf16[64,2,4,128]{3,2,1,0:T(4,128)(2,1)} %copy.46), calls=%async_computation.3 | async-start | bytes 262144 | tf_op jit(solution)/shard_map/all_to_all | solution.py:100
  131.7 73.3 %all-reduce.3.cloned.1.call-start = ((), (), s32[]{:S(2)}) async-start(), calls=%async_computation.12 | async-start | bytes 4194304 | tf_op jit(solution)/shard_map/psum | solution.py:118
  147.1 57.8 %copy-start.11 = (f32[128]{0:T(128)S(1)}, f32[128]{0:T(128)}, u32[]{:S(2)}) copy-start(f32[128]{0:T(128)} %copy-done.10) | copy-start | bytes 1540
  147.2 62.9 %copy-start.3 = (bf16[1,128,4096]{2,1,0:T(8,128)(2,1)S(1)}, bf16[1,128,4096]{2,1,0:T(8,128)(2,1)}, u32[]{:S(2)}) copy-start(bf16[1,128,4096]{2,1,0:T(8,128)(2,1)} %all-gather.8.cloned.1.call-done) | copy-start | bytes 3145732
  205.0 5.2 %copy-start.1 = (bf16[4096,512]{1,0:T(8,128)(2,1)S(1)}, bf16[4096,512]{1,0:T(8,128)(2,1)}, u32[]{:S(2)}) copy-start(bf16[4096,512]{1,0:T(8,128)(2,1)} %param.12) | copy-start | bytes 12582916
  210.1 13.0 %copy-start.16 = (f32[128]{0:T(128)}, f32[128]{0:T(128)S(1)}, u32[]{:S(2)}) copy-start(f32[128]{0:T(128)S(1)} %broadcast_multiply_fusion.1) | copy-start | bytes 1540
  211.6 22.1 %all-to-all-start.4 = ((bf16[1,128,4,128]{3,2,0,1:T(4,128)(2,1)}), bf16[1,128,4,128]{3,2,0,1:T(4,128)(2,1)S(1)}, u32[]{:S(2)}, u32[]{:S(2)}) async-start(bf16[1,128,4,128]{3,2,0,1:T(4,128)(2,1)} %bitcast.12), calls=%async_computation.4 | async-start | bytes 262144 | tf_op jit(solution)/shard_map/all_to_all | solution.py:93
  223.1 15.9 %copy-start.19 = (u32[256]{0:T(256)S(1)}, u32[256]{0:T(256)}, u32[]{:S(2)}) copy-start(u32[256]{0:T(256)} %constant.38) | copy-start | bytes 3076
  223.1 40.1 %copy-start.5 = (bf16[1,128,4,128]{3,1,2,0:T(8,128)(2,1)S(1)}, bf16[1,128,4,128]{3,1,2,0:T(8,128)(2,1)}, u32[]{:S(2)}) copy-start(bf16[1,128,4,128]{3,1,2,0:T(8,128)(2,1)} %copy-done.4) | copy-start | bytes 393220
  223.1 40.1 %copy-start.9 = (f32[2,4,64]{2,1,0:T(4,128)S(1)}, f32[2,4,64]{2,1,0:T(4,128)}, u32[]{:S(2)}) copy-start(f32[2,4,64]{2,1,0:T(4,128)} %copy-done.8) | copy-start | bytes 6148
  223.1 40.1 %copy-start.14 = (f32[2,4,64]{2,1,0:T(4,128)S(1)}, f32[2,4,64]{2,1,0:T(4,128)}, u32[]{:S(2)}) copy-start(f32[2,4,64]{2,1,0:T(4,128)} %copy-done.13) | copy-start | bytes 6148
  226.2 37.3 %copy-start.20 = (f32[64]{0:T(128)S(1)}, f32[64]{0:T(128)}, u32[]{:S(2)}) copy-start(f32[64]{0:T(128)} %get-tuple-element.6) | copy-start | bytes 772
  233.8 29.4 %all-to-all-start.5 = ((bf16[1,128,4,128]{3,2,0,1:T(4,128)(2,1)}), bf16[1,128,4,128]{3,2,0,1:T(4,128)(2,1)S(1)}, u32[]{:S(2)}, u32[]{:S(2)}) async-start(bf16[1,128,4,128]{3,2,0,1:T(4,128)(2,1)} %bitcast.14), calls=%async_computation.5 | async-start | bytes 262144 | tf_op jit(solution)/shard_map/all_to_all | solution.py:94
  264.8 17.4 %all-to-all-start.6 = ((bf16[64,2,4,128]{3,2,1,0:T(4,128)(2,1)}), bf16[64,2,4,128]{3,2,1,0:T(4,128)(2,1)S(1)}, u32[]{:S(2)}, u32[]{:S(2)}) async-start(bf16[64,2,4,128]{3,2,1,0:T(4,128)(2,1)} %copy.59), calls=%async_computation.6 | async-start | bytes 262144 | tf_op jit(solution)/shard_map/all_to_all | solution.py:97
  282.2 5.1 %copy-start.6 = (bf16[64,2,4,128]{3,2,1,0:T(4,128)(2,1)}, bf16[64,2,4,128]{3,2,1,0:T(4,128)(2,1)S(1)}, u32[]{:S(2)}) copy-start(bf16[64,2,4,128]{3,2,1,0:T(4,128)(2,1)S(1)} %all-to-all-done.6) | copy-start | bytes 393220
  282.2 15.5 %all-to-all-start.7 = ((bf16[64,2,4,128]{3,2,1,0:T(4,128)(2,1)}), bf16[64,2,4,128]{3,2,1,0:T(4,128)(2,1)S(1)}, u32[]{:S(2)}, u32[]{:S(2)}) async-start(bf16[64,2,4,128]{3,2,1,0:T(4,128)(2,1)} %copy.62), calls=%async_computation.7 | async-start | bytes 262144 | tf_op jit(solution)/shard_map/all_to_all | solution.py:98
  287.3 55.7 %reduce-scatter.4.cloned.1.call-start = ((), (), s32[]{:S(2)}) async-start(), calls=%async_computation.14 | async-start | bytes 2621440
  287.3 10.4 %copy-start = (f32[1,128,4096]{2,1,0:T(8,128)S(1)}, f32[1,128,4096]{2,1,0:T(8,128)}, u32[]{:S(2)}) copy-start(f32[1,128,4096]{2,1,0:T(8,128)} %fusion.3) | copy-start | bytes 6291460
  287.3 10.4 %copy-start.12 = (f32[128]{0:T(128)S(1)}, f32[128]{0:T(128)}, u32[]{:S(2)}) copy-start(f32[128]{0:T(128)} %copy-done.10) | copy-start | bytes 1540
  287.3 10.4 %copy-start.17 = (f32[128]{0:T(128)S(1)}, f32[128]{0:T(128)}, u32[]{:S(2)}) copy-start(f32[128]{0:T(128)} %copy-done.16) | copy-start | bytes 1540
  302.6 2.5 copy-start.15
  344.9 21.0 %all-to-all-start.8 = ((f32[1,64,16]{2,0,1:T(1,128)}), f32[1,64,16]{2,0,1:T(1,128)S(1)}, u32[]{:S(2)}, u32[]{:S(2)}) async-start(f32[1,64,16]{2,0,1:T(1,128)} %bitcast.20), calls=%async_computation.8 | async-start | bytes 65536 | tf_op jit(solution)/shard_map/all_to_all | solution.py:111
Sparse Core Ops, SparseCore 0:
  9.8 25.3 all-gather.3
  37.0 28.6 all-gather.5
  101.1 23.7 all-gather.7
  147.3 57.6 all-reduce.2
  305.2 37.6 reduce-scatter.3
where the time goes:
time: 374 us; the launch traced here: 373 us
  waiting for transfers between devices  213 us (57%)
  starting transfers between devices  67.7 us (18%)
  matrix products  33.3 us (9%)
  blocking collectives  22.7 us (6%)
  between operations  14.9 us (4%)
  local copies, waits for them, and re-layouts  11.9 us (3%)
  other arithmetic  9.44 us (3%)
    psum x1, waiting for transfers between devices, body(): summed = lax.psum(units, 'tp')  57.8 us
    unnamed x6, waiting for transfers between devices  39.9 us
    all_gather x1, waiting for transfers between devices, body(): lax.all_gather(concept_table, 'tp', axis=1, tiled=True)  28.9 us
    all_gather x1, waiting for transfers between devices, body(): lax.all_gather(latent, 'tp', axis=2, tiled=True)  25.9 us
    unnamed x1, blocking collectives  22.7 us
    all_to_all x1, starting transfers between devices, body(): lax.all_to_all(own_terms, 'seq', split_axis=1, concat_axis=0, tiled=True)  11.4 us
    all_to_all x1, starting transfers between devices, body(): lax.all_to_all(query_tan, 'seq', split_axis=1, concat_axis=0, tiled=True)  11.4 us
    all_to_all x1, starting transfers between devices, body(): lax.all_to_all(key_rows, 'seq', split_axis=1, concat_axis=0, tiled=True)  11.4 us
  transfers between devices with their start and end apart: 14, of which 12 were waited for; matrix products, arithmetic and copies ran while one was open for 8% of the time, Pallas kernels for 0%

commit v1 on v0

v1 whole, which is shorter than its diff:
```python
import functools
import math

import jax
import jax.numpy as jnp
from jax import lax
from jax.experimental import pallas as pl
from jax.experimental.pallas import tpu as pltpu
from jax.sharding import PartitionSpec as P

D = 4096
HD = 128
CONCEPTS = 256
STEPS = 1000
EPS = 1e-06
F = 64
W = 1024
ROWS = 208

BF = jnp.bfloat16
F32 = jnp.float32
NT = (((1,), (1,)), ((), ()))
TN = (((0,), (0,)), ((), ()))


def nt(a, b):
    return lax.dot_general(a, b, NT, preferred_element_type=F32)


def main_kernel(me_ref, c0, c1, c2, c3, t0, t1, t2, t3, concept_ref, temp_ref, wq_ref, wk_ref,
                rs_ref, stat_ref, w_s, mod_s, h_s, acc_s, g_s, sems):
    parts = (c0, c1, c2, c3)
    tables = (t0, t1, t2, t3)
    me = me_ref[0]
    copies = []
    for k in range(4):
        rows = pl.ds(pl.multiple_of((me ^ k) * W, W), W)
        a = pltpu.make_async_copy(wq_ref.at[rows], w_s.at[k, :, pl.ds(0, 512)], sems.at[2 * k])
        b = pltpu.make_async_copy(wk_ref.at[rows], w_s.at[k, :, pl.ds(512, 512)], sems.at[2 * k + 1])
        a.start()
        b.start()
        copies.append((a, b))
    onehot = (concept_ref[...] == lax.broadcasted_iota(jnp.int32, (F, CONCEPTS), 1)).astype(BF)
    sq = jnp.zeros((2, F, 128), F32)
    sd = jnp.zeros((2, F, 128), F32)
    for k in range(4):
        mod_s[k] = 1.0 + jnp.dot(onehot, tables[k][...], preferred_element_type=F32)
        for j in range(8):
            lanes = pl.ds(128 * j, 128)
            x = parts[k][0:2, :, lanes].astype(F32)
            d = parts[k][2:4, :, lanes].astype(F32)
            sq = sq + x * x
            sd = sd + x * d
    inv = lax.rsqrt(jnp.sum(sq, axis=-1, keepdims=True) / D + EPS)
    mean = inv * (jnp.sum(sd, axis=-1, keepdims=True) / D)
    inv2 = inv.reshape(2 * F, 1)
    mean2 = mean.reshape(2 * F, 1)

    def normed_of(k, lanes):
        x = parts[k][0:2, :, lanes].astype(F32).reshape(2 * F, -1)
        d = parts[k][2:4, :, lanes].astype(F32).reshape(2 * F, -1)
        n = x * inv2
        return n, inv2 * (d - n * mean2)

    for k in range(4):
        for j in range(4):
            lanes = pl.ds(256 * j, 256)
            n, nd = normed_of(k, lanes)
            m = mod_s[k, :, lanes]
            m = jnp.concatenate([m, m], axis=0)
            h_s[k, 0:128, lanes] = (n * m).astype(BF)
            h_s[k, 128:256, lanes] = (nd * m).astype(BF)
    for k in range(4):
        copies[k][0].wait()
        copies[k][1].wait()

    acc_s[...] = jnp.zeros_like(acc_s)

    def forward(k, carry):
        acc_s[...] += jnp.dot(h_s[k], w_s[k], preferred_element_type=F32)
        return carry

    lax.fori_loop(0, 4, forward, 0)

    temp = temp_ref[...]
    scal = jnp.zeros((2 * F, 128), F32)
    scals = []
    for p in range(2):
        part = jnp.zeros((F, HD), F32)
        for h in range(4):
            ql, kl = pl.ds(128 * h, 128), pl.ds(512 + 128 * h, 128)
            r0, r1 = pl.ds(64 * p, 64), pl.ds(128 + 64 * p, 64)
            q, qt = acc_s[r0, ql].astype(BF), acc_s[r1, ql].astype(BF)
            kk, kt = acc_s[r0, kl].astype(BF), acc_s[r1, kl].astype(BF)
            prod = nt(jnp.concatenate([q, qt], axis=0), jnp.concatenate([kk, kt], axis=0))
            scores = prod[0:64, 0:64] * temp
            tdot = prod[64:128, 0:64] + prod[0:64, 64:128]
            e = jnp.exp(scores - jnp.max(scores, axis=-1, keepdims=True))
            w = e / jnp.sum(e, axis=-1, keepdims=True)
            cur = -temp * w * (tdot - jnp.sum(w * tdot, axis=-1, keepdims=True))
            wc = jnp.concatenate([w, cur], axis=0).astype(BF)
            wct = jnp.concatenate([w, cur], axis=1).T.astype(BF)
            back_q = jnp.dot(wc, jnp.concatenate([kk, kt], axis=1), preferred_element_type=F32)
            back_k = jnp.dot(wct, jnp.concatenate([q, qt], axis=1), preferred_element_type=F32)
            gq, aq = -back_q[0:64, 0:128], back_q[64:128, 0:128] - back_q[0:64, 128:256]
            gk, ak = -back_k[0:64, 0:128], back_k[64:128, 0:128] - back_k[0:64, 128:256]
            gqb, gkb = gq.astype(BF), gk.astype(BF)
            g_s[r0, ql] = gqb
            g_s[r1, ql] = aq.astype(BF)
            g_s[r0, kl] = gkb
            g_s[r1, kl] = ak.astype(BF)
            part = part + gqb.astype(F32) * q.astype(F32) + gkb.astype(F32) * kk.astype(F32)
        scals.append(jnp.sum(part, axis=-1, keepdims=True))
    scal = jnp.concatenate(scals, axis=0)
    eye = lax.broadcasted_iota(jnp.int32, (128, 128), 0) == lax.broadcasted_iota(jnp.int32, (128, 128), 1)
    srow = jnp.sum(jnp.where(eye, scal, 0.0), axis=0, keepdims=True)
    hi = srow.astype(BF).astype(F32)
    lo = srow - hi
    sub = lax.broadcasted_iota(jnp.int32, (16, 128), 0)
    stats = jnp.where(sub == 0, hi, jnp.where(sub == 1, lo, 0.0))
    lane = lax.broadcasted_iota(jnp.int32, (2 * F, 128), 1)
    stat_ref[...] = jnp.where(lane == 0, inv2, 0.0)

    rr = lax.broadcasted_iota(jnp.int32, (256, 512), 0)
    cc = lax.broadcasted_iota(jnp.int32, (256, 512), 1)
    source = ((rr >> 3) & 7) * 64 + (rr >> 6) * 16 + (rr & 7)
    perm_a = (cc == source).astype(BF)
    perm_b = (cc == source + 8).astype(BF)
    for k in range(4):
        rs_ref[k, 192:208, :] = jnp.concatenate([stats] + [jnp.zeros((16, 896), F32)], axis=1).astype(BF)
    for k in range(4):
        for j in range(2):
            lanes = pl.ds(512 * j, 512)
            back = nt(g_s[...], w_s[k, 512 * j:512 * j + 512, :])
            units, drift = back[0:128], back[128:256]
            rs_ref[k, 0:128, lanes] = units.astype(BF)
            n, nd = normed_of(k, lanes)
            terms = n * drift + nd * units
            terms = (terms[0:64] + terms[64:128]).astype(BF)
            moved = jnp.concatenate([nt(perm_a, terms), nt(perm_b, terms)], axis=1).astype(BF)
            spot = pl.ds(pl.multiple_of(((me ^ k) * 2 + j) * 128, 128), 128)
            for t in range(4):
                rs_ref[me ^ t, 128:192, spot] = moved[64 * t:64 * t + 64]


def main_call(me, parts, tables, concept, temp, wq, wk):
    vm = pl.BlockSpec(memory_space=pltpu.VMEM)
    sm = pl.BlockSpec(memory_space=pltpu.SMEM)
    hb = pl.BlockSpec(memory_space=pl.ANY)
    return pl.pallas_call(
        main_kernel,
        out_shape=(jax.ShapeDtypeStruct((4, ROWS, W), BF), jax.ShapeDtypeStruct((2 * F, 128), F32)),
        in_specs=[sm] + [vm] * 10 + [hb, hb],
        out_specs=(vm, vm),
        scratch_shapes=[
            pltpu.VMEM((4, W, W), BF),
            pltpu.VMEM((4, F, W), F32),
            pltpu.VMEM((4, 256, W), BF),
            pltpu.VMEM((256, W), F32),
            pltpu.VMEM((256, W), BF),
            pltpu.SemaphoreType.DMA((8,)),
        ],
        compiler_params=pltpu.CompilerParams(vmem_limit_bytes=48 * 1024 * 1024),
        name="attend",
    )(me, *parts, *tables, concept, temp, wq, wk)


def merge_kernel(a_ref, b_ref, o_ref):
    o_ref[0:192, :] = (a_ref[0:192, :].astype(F32) + b_ref[0:192, :].astype(F32)).astype(BF)
    o_ref[192:208, :] = jnp.concatenate(
        [a_ref[192:208, 0:128], b_ref[192:208, 0:128], a_ref[192:208, 256:1024]], axis=1)


def final_kernel(a_ref, b_ref, c_ref, x_ref, table_ref, concept_ref, stat_ref, score_ref, terms_ref):
    total = (a_ref[0:192, :].astype(F32) + b_ref[0:192, :].astype(F32)) + c_ref[0:192, :].astype(F32)
    terms_ref[...] = total[128:192].astype(BF)
    units = total[0:128]
    srow = jnp.zeros((1, 128), F32)
    for ref, lane in ((a_ref, 0), (b_ref, 0), (c_ref, 0), (c_ref, 128)):
        part = ref[192:208, lane:lane + 128].astype(F32)
        srow = srow + (part[0:1] + part[1:2])
    eye = lax.broadcasted_iota(jnp.int32, (128, 128), 0) == lax.broadcasted_iota(jnp.int32, (128, 128), 1)
    mean = jnp.sum(jnp.where(eye, srow, 0.0), axis=1, keepdims=True) / D
    inv = jnp.sum(stat_ref[...], axis=1, keepdims=True)
    onehot = (concept_ref[...] == lax.broadcasted_iota(jnp.int32, (F, CONCEPTS), 1)).astype(BF)
    mod = 1.0 + jnp.dot(onehot, table_ref[...], preferred_element_type=F32)
    mod = jnp.concatenate([mod, mod], axis=0)
    x = x_ref[0:2].astype(F32).reshape(2 * F, W)
    score_ref[...] = (inv * (mod * units - (x * inv) * mean)).astype(BF).reshape(2, F, W)


def body(latent, direction, concept, timestep, concept_table, w_query, w_key):
    tp = lax.axis_index("tp")
    y_hi = tp >> 1
    cross = []
    for s in range(64):
        for t in range(4):
            cross.append((4 * s + t, 4 * (s ^ 4) + (t ^ 2)))
    core = [(t, t ^ 1) for t in range(4)]
    swap_core = lambda v: lax.ppermute(v, "tp", core)
    swap_chip = lambda v: lax.ppermute(v, ("seq", "tp"), cross)

    def flip(v):
        v = v.reshape((8, 2, 4) + v.shape[1:])
        v = jnp.where(y_hi == 1, v[:, ::-1], v)
        return v.reshape((64,) + v.shape[3:])

    mine = jnp.concatenate([latent.reshape(F, 2, W), direction.reshape(F, 2, W)], axis=1)
    ident = jnp.broadcast_to(concept.astype(BF).reshape(1, 1, 1), (F, 4, 128))
    sent = jnp.concatenate([flip(mine), ident], axis=2)
    got = lax.all_to_all(sent, "seq", split_axis=0, concat_axis=0, tiled=True)
    ids = got[:, 0, W:W + 1].astype(jnp.int32)
    own = jnp.transpose(got[:, :, :W], (1, 0, 2))

    t_own = concept_table
    t_core = swap_core(t_own)
    t_chip = swap_chip(t_own)
    t_both = swap_core(t_chip)

    chip = swap_chip(own)
    near = swap_core(own)
    both = swap_core(chip)

    temp = ((0.25 + 1.75 * timestep.astype(F32) / STEPS) / math.sqrt(HD)).reshape(F, 1)
    parts, stat = main_call(
        tp.reshape(1).astype(jnp.int32), (own, near, chip, both), (t_own, t_core, t_chip, t_both), ids, temp, w_query, w_key)

    vm = pl.BlockSpec(memory_space=pltpu.VMEM)
    far = swap_core(parts[3])
    summed = pl.pallas_call(
        merge_kernel, out_shape=jax.ShapeDtypeStruct((ROWS, W), BF), in_specs=[vm] * 2, out_specs=vm, name="merge",
    )(parts[2], far)
    arrived = swap_chip(summed)
    beside = swap_core(parts[1])
    score, terms = pl.pallas_call(
        final_kernel,
        out_shape=(jax.ShapeDtypeStruct((2, F, W), BF), jax.ShapeDtypeStruct((F, W), BF)),
        in_specs=[vm] * 7, out_specs=(vm, vm), name="finish",
    )(parts[0], beside, arrived, own, t_own, ids, stat)

    score_rows = jnp.transpose(score, (1, 0, 2)).reshape(F, 16, 128)
    term_rows = jnp.transpose(terms.reshape(8, 8, 8, 128), (2, 0, 1, 3)).reshape(F, 8, 128)
    back = lax.all_to_all(
        jnp.concatenate([score_rows, term_rows], axis=1), "seq", split_axis=0, concat_axis=0, tiled=True)
    score_field = flip(back[:, :16].reshape(F, 2, W)).reshape(1, 128, W)
    frames = jnp.sum(back[:, 16:].astype(F32), axis=0).reshape(8, 2, F)
    frames = jnp.transpose(frames, (2, 1, 0)).reshape(F, 16)
    onehot = (ids == jnp.arange(CONCEPTS, dtype=jnp.int32)[None, :]).astype(F32)
    table_grad = jnp.dot(onehot.T, frames, precision=lax.Precision.HIGHEST)
    return (score_field, table_grad)


def solution(mesh):
    in_specs = (
        P("seq", None, "tp"),
        P("seq", None, "tp"),
        P("seq"),
        P(),
        P(None, "tp"),
        P(None, "tp"),
        P(None, "tp"),
    )
    out_specs = (P("seq", None, "tp"), P(None, ("seq", "tp")))
    return jax.shard_map(body, mesh=mesh, in_specs=in_specs, out_specs=out_specs, check_vma=False)
```

time: 374 us -> 120 us (0.32)
  waiting for transfers between devices: 213 us -> 53.1 us
  starting transfers between devices: 67.7 us -> 27.5 us
  matrix products: 33.3 us -> 0.82 us
  blocking collectives: 22.7 us -> 0 us
  Pallas kernels: 0 us -> 20.9 us
  between operations: 14.9 us -> 1.54 us
  other arithmetic: 9.44 us -> 4.93 us
    psum x1 -> x0, waiting for transfers between devices: 57.8 us -> none  [body(): summed = lax.psum(units, 'tp')]
    all_gather x3 -> x0, waiting for transfers between devices: 54.7 us -> none  [the longest x1 28.9 us: body(): lax.all_gather(concept_table, 'tp', axis=1, tiled=True)]
    all_to_all x9 -> x2, starting transfers between devices: 67.5 us -> 22.5 us  [the longest x1 12.9 us: body(): got = lax.all_to_all(sent, 'seq', split_axis=0, concat_axis=0, tiled=True)]
    unnamed x6 -> x0, waiting for transfers between devices: 39.9 us -> none
    dot_general x19 -> x1, matrix products: 33.3 us -> 0.82 us  [body(): table_grad = jnp.dot(onehot.T, frames, precision=lax.Precision.HIGHEST)]
    all_to_all x9 -> x2, waiting for transfers between devices: 61 us -> 30.3 us  [the longest x1 17.6 us: body(): got = lax.all_to_all(sent, 'seq', split_axis=0, concat_axis=0, tiled=True)]
    ppermute x0 -> x9, waiting for transfers between devices: none -> 22.8 us  [the longest x3 20.5 us: body(): swap_chip = lambda v: lax.ppermute(v, ('seq', 'tp'), cross)]
    unnamed x1 -> x0, blocking collectives: 22.7 us -> none
  transfers between devices with their start and end apart: 14 -> 11, of which waited for: 12 -> 6; matrix products, arithmetic and copies ran while one was open for 8% -> 3% of each run, Pallas kernels for 0% -> 2%
where the time goes in v1:
time: 120 us; the launch traced here: 119 us
  waiting for transfers between devices  53.1 us (44%)
  starting transfers between devices  27.5 us (23%)
  Pallas kernels  20.9 us (17%)
  local copies, waits for them, and re-layouts  10.3 us (9%)
  other arithmetic  4.93 us (4%)
  between operations  1.54 us (1%)
    ppermute x3, waiting for transfers between devices, body(): swap_chip = lambda v: lax.ppermute(v, ('seq', 'tp'), cross)  20.5 us
    all_to_all x1, waiting for transfers between devices, body(): got = lax.all_to_all(sent, 'seq', split_axis=0, concat_axis=0, tiled=True)  17.6 us
    pallas_call x1, Pallas kernels, main_call(): pl.pallas_call(main_kernel, out_shape=(jax.ShapeDtypeStruct((4, ROWS, W),...  16.2 us
    all_to_all x1, starting transfers between devices, body(): got = lax.all_to_all(sent, 'seq', split_axis=0, concat_axis=0, tiled=True)  12.9 us
    all_to_all x1, waiting for transfers between devices, body(): lax.all_to_all(jnp.concatenate([score_rows, term_rows], axis=1), 'seq', s...  12.7 us
    all_to_all x1, starting transfers between devices, body(): lax.all_to_all(jnp.concatenate([score_rows, term_rows], axis=1), 'seq', s...  9.58 us
    ppermute x3, starting transfers between devices, body(): swap_chip = lambda v: lax.ppermute(v, ('seq', 'tp'), cross)  3.99 us
    convert_element_type x2, other arithmetic, body(): ids = got[:, 0, W:W + 1].astype(jnp.int32)  2.94 us
  transfers between devices with their start and end apart: 11, of which 6 were waited for; matrix products, arithmetic and copies ran while one was open for 3% of the time, Pallas kernels for 2%

profile of v1, /device:TPU:8, one launch (start us, length us, event | category | flops | bytes accessed | tf_op | source)
XLA Modules:
  0.0 119.1 jit_solution(14713114165202079416)
XLA Ops:
  0.6 0.0 copy-start.1
  0.6 0.0 copy-start.8
  1.4 1.0 concatenate.14
  2.4 1.1 concatenate.15
  3.5 0.5 pad_maximum_fusion
  4.0 0.3 reverse_select_fusion
  4.3 1.0 concatenate.17
  5.3 12.9 %all-to-all-start = ((bf16[64,4,1152]{2,1,0:T(4,128)(2,1)}), bf16[64,4,1152]{2,1,0:T(4,128)(2,1)S(1)}, u32[]{:S(2)}, u32[]{:S(2)}) async-start(bf16[64,4,1152]{2,1,0:T(4,128)(2,1)} %concatenate.17), calls=%async_computation | async-start | bytes 1179648 | tf_op jit(solution)/shard_map/all_to_all | solution.py:211
  18.3 0.0 copy-done.1
  18.3 1.4 %collective-permute-start.4 = (bf16[256,1024]{1,0:T(8,128)(2,1)S(1)}, bf16[256,1024]{1,0:T(8,128)(2,1)S(1)}, u32[]{:S(2)}, u32[]{:S(2)}) collective-permute-start(bf16[256,1024]{1,0:T(8,128)(2,1)S(1)} %copy-done.1), channel_id=1, source_target_pairs={{0,18},{1,19},{2,16},{3,17},{4,22},{5,23},{6,20},{7,21},{8,26},{9,... | collective-permute-start | bytes 1572872 | tf_op jit(solution)/shard_map/ppermute | solution.py:201
  19.7 17.6 %all-to-all-done = bf16[64,4,1152]{2,1,0:T(4,128)(2,1)S(1)} async-done(((bf16[64,4,1152]{2,1,0:T(4,128)(2,1)}), bf16[64,4,1152]{2,1,0:T(4,128)(2,1)S(1)}, u32[]{:S(2)}, u32[]{:S(2)}) %all-to-all-start) | async-done | bytes 589856 | tf_op jit(solution)/shard_map/all_to_all | solution.py:211
  37.3 0.0 copy-start.4
  37.3 0.8 copy-done.4
  38.1 0.2 slice.32
  38.3 0.2 copy.42
  38.5 0.0 copy-start
  38.5 1.8 %collective-permute-start.1 = (bf16[4,64,1024]{2,1,0:T(8,128)(2,1)S(1)}, bf16[4,64,1024]{2,1,0:T(8,128)(2,1)S(1)}, u32[]{:S(2)}, u32[]{:S(2)}) collective-permute-start(bf16[4,64,1024]{2,1,0:T(8,128)(2,1)S(1)} %bitcast.27), channel_id=1, source_target_pairs={{0,18},{1,19},{2,16},{3,17},{4,22},{5,23},{6,20},{7,21},{8,26},{9,... | collective-permute-start | bytes 1572872 | tf_op jit(solution)/shard_map/ppermute | solution.py:201
  40.2 0.0 collective-permute-start.3
  40.2 0.0 collective-permute-done.4.t2
  40.2 0.5 collective-permute-start.5
  40.7 0.0 collective-permute-start
  40.7 9.3 %collective-permute-done.1.c2 = bf16[4,64,1024]{2,1,0:T(8,128)(2,1)S(1)} collective-permute-done((bf16[4,64,1024]{2,1,0:T(8,128)(2,1)S(1)}, bf16[4,64,1024]{2,1,0:T(8,128)(2,1)S(1)}, u32[]{:S(2)}, u32[]{:S(2)}) %collective-permute-start.1) | collective-permute-done | bytes 524320 | tf_op jit(solution)/shard_map/ppermute | solution.py:201
  50.1 0.0 collective-permute-start.2
  50.1 0.0 copy-done.8
  50.1 0.1 copy.31.temp_ref
  50.2 0.9 slice_convert_fusion
  51.1 0.0 copy-start.2
  51.1 0.0 collective-permute-done.3.t1
  51.1 0.0 collective-permute-done.5.t3
  51.1 0.0 collective-permute-done.c1
  51.1 1.0 collective-permute-done.2.c3
  52.1 16.2 %attend.1 = (bf16[4,208,1024]{2,1,0:T(8,128)(2,1)S(1)}, f32[128,128]{1,0:T(8,128)S(1)}) custom-call(s32[1]{0:T(128)} %bitcast.me_ref, bf16[4,64,1024]{2,1,0:T(8,128)(2,1)S(1)} %bitcast.29, bf16[4,64,1024]{2,1,0:T(8,128)(2,1)} %collective-permute-done.c1, bf16[4,64,1024]{2,1,0:T(8,128)(2,1)S(1)} %collective-permute-done.1.c2, ...), custom_call_target="tpu_custom_call" | custom-call | tf_op jit(solution)/shard_map/attend/pallas_call | solution.py:150
  68.3 0.0 copy-done
  68.3 0.0 copy-done.2
  68.3 0.0 copy-start.3
  68.3 1.1 slice_bitcast_fusion
  69.4 0.0 copy-done.3
  69.4 0.1 collective-permute-start.7
  69.6 0.4 collective-permute-start.6
  70.0 1.3 %collective-permute-done.7.b_ref = bf16[208,1024]{1,0:T(8,128)(2,1)S(1)} collective-permute-done((bf16[208,1024]{1,0:T(8,128)(2,1)S(1)}, bf16[208,1024]{1,0:T(8,128)(2,1)S(1)}, u32[]{:S(2)}, u32[]{:S(2)}) %collective-permute-start.7) | collective-permute-done | bytes 426016 | tf_op jit(solution)/shard_map/ppermute | solution.py:200
  71.2 0.0 copy-start.7
  71.2 0.8 copy-done.7
  72.0 2.0 %merge.1 = bf16[208,1024]{1,0:T(8,128)(2,1)} custom-call(bf16[208,1024]{1,0:T(8,128)(2,1)} %get-tuple-element.11.a_ref, bf16[208,1024]{1,0:T(8,128)(2,1)} %copy-done.7), custom_call_target="tpu_custom_call" | custom-call | tf_op jit(solution)/shard_map/merge/pallas_call | solution.py:230
  74.0 0.9 collective-permute-start.8
  74.8 0.0 collective-permute-done.6.b_ref
  74.8 0.0 copy-start.5
  74.8 11.2 %collective-permute-done.8.c_ref = bf16[208,1024]{1,0:T(8,128)(2,1)S(1)} collective-permute-done((bf16[208,1024]{1,0:T(8,128)(2,1)}, bf16[208,1024]{1,0:T(8,128)(2,1)S(1)}, u32[]{:S(2)}, u32[]{:S(2)}) %collective-permute-start.8) | collective-permute-done | bytes 426016 | tf_op jit(solution)/shard_map/ppermute | solution.py:201
  86.0 0.0 copy-start.6
  86.0 0.0 copy-done.5
  86.0 0.8 copy-done.6
  86.8 2.7 %finish.1 = (bf16[2,64,1024]{2,1,0:T(8,128)(2,1)}, bf16[64,1024]{1,0:T(8,128)(2,1)}) custom-call(bf16[208,1024]{1,0:T(8,128)(2,1)} %get-tuple-element.13.a_ref, bf16[208,1024]{1,0:T(8,128)(2,1)} %copy-done.5, bf16[208,1024]{1,0:T(8,128)(2,1)} %copy-done.6, bf16[4,64,1024]{2,1,0:T(8,128)(2,1)} %bitcast.30, bf16[256,1024]{1,0:T(8,128)(2,1)} %table_ref.1, ...), custom_call_target="tpu_custom_call" | custom-call | tf_op jit(solution)/shard_map/finish/pallas_call | solution.py:235
  89.5 1.2 %copy.33 = bf16[64,2,1024]{2,1,0:T(2,128)(2,1)S(1)} copy(bf16[64,2,1024]{2,0,1:T(8,128)(2,1)} %bitcast.35) | data formatting | bytes 524288 | tf_op jit(solution)/shard_map/transpose | solution.py:241
  90.7 0.2 reshape.57
  90.9 0.9 copy.34
  91.8 0.8 pad_maximum_fusion.1
  92.6 9.6 %all-to-all-start.1 = ((bf16[64,24,128]{2,1,0:T(8,128)(2,1)}), bf16[64,24,128]{2,1,0:T(8,128)(2,1)S(1)}, u32[]{:S(2)}, u32[]{:S(2)}) async-start(bf16[64,24,128]{2,1,0:T(8,128)(2,1)} %pad_maximum_fusion.1), calls=%async_computation.1 | async-start | bytes 786432 | tf_op jit(solution)/shard_map/all_to_all | solution.py:243
  102.2 2.1 %fusion.4 = s32[64]{0:T(128)S(1)} fusion(bf16[64,4,1152]{2,1,0:T(4,128)(2,1)} %copy-done.4), kind=kLoop, calls=%fused_computation.17 | loop fusion | flops 64 | bytes 384 | tf_op jit(solution)/shard_map/convert_element_type | solution.py:212
  104.3 12.7 %all-to-all-done.1 = bf16[64,24,128]{2,1,0:T(8,128)(2,1)S(1)} async-done(((bf16[64,24,128]{2,1,0:T(8,128)(2,1)}), bf16[64,24,128]{2,1,0:T(8,128)(2,1)S(1)}, u32[]{:S(2)}, u32[]{:S(2)}) %all-to-all-start.1) | async-done | bytes 393248 | tf_op jit(solution)/shard_map/all_to_all | solution.py:243
  117.0 0.1 reshape_reshape.6
  117.1 0.3 broadcast_select_fusion
  117.4 0.8 reshape_reshape.7
  118.2 0.1 convert_reduce_fusion
  118.2 0.1 reshape.60
  118.3 0.8 fusion
  (2 shorter events, 0.0 us)
Async XLA Ops:
  0.6 17.7 %copy-start.1 = (bf16[256,1024]{1,0:T(8,128)(2,1)S(1)}, bf16[256,1024]{1,0:T(8,128)(2,1)}, u32[]{:S(2)}) copy-start(bf16[256,1024]{1,0:T(8,128)(2,1)} %table_ref.1) | copy-start | bytes 1572868
  0.6 49.4 %copy-start.8 = (s32[64]{0:T(128)S(1)}, s32[64]{0:T(128)}, u32[]{:S(2)}) copy-start(s32[64]{0:T(128)} %param.10) | copy-start | bytes 772
  5.3 31.9 %all-to-all-start = ((bf16[64,4,1152]{2,1,0:T(4,128)(2,1)}), bf16[64,4,1152]{2,1,0:T(4,128)(2,1)S(1)}, u32[]{:S(2)}, u32[]{:S(2)}) async-start(bf16[64,4,1152]{2,1,0:T(4,128)(2,1)} %concatenate.17), calls=%async_computation | async-start | bytes 1179648 | tf_op jit(solution)/shard_map/all_to_all | solution.py:211
  18.3 21.9 %collective-permute-start.4 = (bf16[256,1024]{1,0:T(8,128)(2,1)S(1)}, bf16[256,1024]{1,0:T(8,128)(2,1)S(1)}, u32[]{:S(2)}, u32[]{:S(2)}) collective-permute-start(bf16[256,1024]{1,0:T(8,128)(2,1)S(1)} %copy-done.1), channel_id=1, source_target_pairs={{0,18},{1,19},{2,16},{3,17},{4,22},{5,23},{6,20},{7,21},{8,26},{9,... | collective-permute-start | bytes 1572872 | tf_op jit(solution)/shard_map/ppermute | solution.py:201
  37.3 0.8 copy-start.4
  38.5 29.9 %copy-start = (bf16[64,4,1024]{2,0,1:T(8,128)(2,1)}, bf16[64,4,1024]{2,0,1:T(8,128)(2,1)S(1)}, u32[]{:S(2)}) copy-start(bf16[64,4,1024]{2,0,1:T(8,128)(2,1)S(1)} %copy.42) | copy-start | bytes 1572868
  38.5 11.6 %collective-permute-start.1 = (bf16[4,64,1024]{2,1,0:T(8,128)(2,1)S(1)}, bf16[4,64,1024]{2,1,0:T(8,128)(2,1)S(1)}, u32[]{:S(2)}, u32[]{:S(2)}) collective-permute-start(bf16[4,64,1024]{2,1,0:T(8,128)(2,1)S(1)} %bitcast.27), channel_id=1, source_target_pairs={{0,18},{1,19},{2,16},{3,17},{4,22},{5,23},{6,20},{7,21},{8,26},{9,... | collective-permute-start | bytes 1572872 | tf_op jit(solution)/shard_map/ppermute | solution.py:201
  40.2 10.8 %collective-permute-start.3 = (bf16[256,1024]{1,0:T(8,128)(2,1)S(1)}, bf16[256,1024]{1,0:T(8,128)(2,1)S(1)}, u32[]{:S(2)}, u32[]{:S(2)}) collective-permute-start(bf16[256,1024]{1,0:T(8,128)(2,1)S(1)} %copy-done.1), channel_id=1, source_target_pairs={{0,1},{1,0},{2,3},{3,2},{4,5},{5,4},{6,7},{7,6},{8,9},{9,8},{10,11... | collective-permute-start | bytes 1572872 | tf_op jit(solution)/shard_map/ppermute | solution.py:200
  40.2 10.9 %collective-permute-start.5 = (bf16[256,1024]{1,0:T(8,128)(2,1)S(1)}, bf16[256,1024]{1,0:T(8,128)(2,1)S(1)}, u32[]{:S(2)}, u32[]{:S(2)}) collective-permute-start(bf16[256,1024]{1,0:T(8,128)(2,1)S(1)} %collective-permute-done.4.t2), channel_id=1, source_target_pairs={{0,1},{1,0},{2,3},{3,2},{4,5},{5,4},{6,7},{7,6},{8,9},{9,8},{10,11... | collective-permute-start | bytes 1572872 | tf_op jit(solution)/shard_map/ppermute | solution.py:200
  40.7 10.4 %collective-permute-start = (bf16[4,64,1024]{2,1,0:T(8,128)(2,1)S(1)}, bf16[4,64,1024]{2,1,0:T(8,128)(2,1)}, u32[]{:S(2)}, u32[]{:S(2)}) collective-permute-start(bf16[4,64,1024]{2,1,0:T(8,128)(2,1)S(1)} %bitcast.28), channel_id=1, source_target_pairs={{0,1},{1,0},{2,3},{3,2},{4,5},{5,4},{6,7},{7,6},{8,9},{9,8},{10,11... | collective-permute-start | bytes 1572872 | tf_op jit(solution)/shard_map/ppermute | solution.py:200
  50.1 2.0 %collective-permute-start.2 = (bf16[4,64,1024]{2,1,0:T(8,128)(2,1)S(1)}, bf16[4,64,1024]{2,1,0:T(8,128)(2,1)}, u32[]{:S(2)}, u32[]{:S(2)}) collective-permute-start(bf16[4,64,1024]{2,1,0:T(8,128)(2,1)S(1)} %collective-permute-done.1.c2), channel_id=1, source_target_pairs={{0,1},{1,0},{2,3},{3,2},{4,5},{5,4},{6,7},{7,6},{8,9},{9,8},{10,11... | collective-permute-start | bytes 1572872 | tf_op jit(solution)/shard_map/ppermute | solution.py:200
  51.1 17.3 %copy-start.2 = (s32[64,1,1]{2,1,0:T(1,128)}, s32[64,1,1]{2,1,0:T(1,128)S(1)}, u32[]{:S(2)}) copy-start(s32[64,1,1]{2,1,0:T(1,128)S(1)} %slice_convert_fusion) | copy-start | bytes 772
  68.3 1.1 copy-start.3
  69.4 1.8 %collective-permute-start.7 = (bf16[208,1024]{1,0:T(8,128)(2,1)S(1)}, bf16[208,1024]{1,0:T(8,128)(2,1)S(1)}, u32[]{:S(2)}, u32[]{:S(2)}) collective-permute-start(bf16[208,1024]{1,0:T(8,128)(2,1)S(1)} %get-tuple-element.10), channel_id=1, source_target_pairs={{0,1},{1,0},{2,3},{3,2},{4,5},{5,4},{6,7},{7,6},{8,9},{9,8},{10,11... | collective-permute-start | bytes 1277960 | tf_op jit(solution)/shard_map/ppermute | solution.py:200
  69.6 5.3 %collective-permute-start.6 = (bf16[208,1024]{1,0:T(8,128)(2,1)S(1)}, bf16[208,1024]{1,0:T(8,128)(2,1)S(1)}, u32[]{:S(2)}, u32[]{:S(2)}) collective-permute-start(bf16[208,1024]{1,0:T(8,128)(2,1)S(1)} %get-tuple-element.12), channel_id=1, source_target_pairs={{0,1},{1,0},{2,3},{3,2},{4,5},{5,4},{6,7},{7,6},{8,9},{9,8},{10,11... | collective-permute-start | bytes 1277960 | tf_op jit(solution)/shard_map/ppermute | solution.py:200
  71.2 0.8 copy-start.7
  74.0 12.1 %collective-permute-start.8 = (bf16[208,1024]{1,0:T(8,128)(2,1)}, bf16[208,1024]{1,0:T(8,128)(2,1)S(1)}, u32[]{:S(2)}, u32[]{:S(2)}) collective-permute-start(bf16[208,1024]{1,0:T(8,128)(2,1)} %merge.1), channel_id=1, source_target_pairs={{0,18},{1,19},{2,16},{3,17},{4,22},{5,23},{6,20},{7,21},{8,26},{9,... | collective-permute-start | bytes 1277960 | tf_op jit(solution)/shard_map/ppermute | solution.py:201
  74.8 11.2 %copy-start.5 = (bf16[208,1024]{1,0:T(8,128)(2,1)}, bf16[208,1024]{1,0:T(8,128)(2,1)S(1)}, u32[]{:S(2)}) copy-start(bf16[208,1024]{1,0:T(8,128)(2,1)S(1)} %collective-permute-done.6.b_ref) | copy-start | bytes 1277956
  86.0 0.8 copy-start.6
  92.6 24.4 %all-to-all-start.1 = ((bf16[64,24,128]{2,1,0:T(8,128)(2,1)}), bf16[64,24,128]{2,1,0:T(8,128)(2,1)S(1)}, u32[]{:S(2)}, u32[]{:S(2)}) async-start(bf16[64,24,128]{2,1,0:T(8,128)(2,1)} %pad_maximum_fusion.1), calls=%async_computation.1 | async-start | bytes 786432 | tf_op jit(solution)/shard_map/all_to_all | solution.py:243

commit v2 on v0

v2 whole, which is shorter than its diff:
```python
import math

import jax
import jax.numpy as jnp
from jax import lax
from jax.experimental import pallas as pl
from jax.experimental.pallas import tpu as pltpu
from jax.sharding import PartitionSpec as P

D = 4096
HD = 128
CONCEPTS = 256
STEPS = 1000
EPS = 1e-06
F = 64
W = 1024
STEP = 40

BF = jnp.bfloat16
F32 = jnp.float32
NT = (((1,), (1,)), ((), ()))


def nt(a, b):
    return lax.dot_general(a, b, NT, preferred_element_type=F32)


def mod_kernel(t0, t1, t2, t3, ids_ref, steps_ref, mod_ref, late_ref, temp_ref):
    temp_ref[...] = jnp.zeros((F, 128), F32) + steps_ref[...]
    ids = ids_ref[:, 0:128].astype(F32)
    late_ref[...] = ids
    onehot = (ids[:, 0:1] == lax.broadcasted_iota(jnp.int32, (F, CONCEPTS), 1).astype(F32)).astype(BF)
    for k, table_ref in enumerate((t0, t1, t2, t3)):
        mod_ref[k] = 1.0 + jnp.dot(onehot, table_ref[...], preferred_element_type=F32)


def relay_kernel(*refs):
    v_ref, o_ref = refs[-2:]
    o_ref[...] = v_ref[...]


def pack_kernel(x_ref, d_ref, ids_ref, o_ref, in_s, out_s):
    y_hi = lax.axis_index("tp") >> 1
    for j in range(8):
        lanes = pl.ds(128 * j, 128)
        in_s[256 * j:256 * j + 128] = x_ref[:, lanes].astype(F32)
        in_s[256 * j + 128:256 * j + 256] = d_ref[:, lanes].astype(F32)
    for q in range(4):
        for j in range(8):
            rows = in_s[pl.ds(256 * j + (q // 2) * 128 + q % 2, F, stride=2), :]
            out_s[pl.ds(j * 4 + q, F, stride=STEP), :] = flip_rows(rows, y_hi)
        out_s[pl.ds(32 + q, F, stride=STEP), :] = jnp.zeros((F, 128), F32) + ids_ref[...].astype(F32)
    o_ref[...] = out_s[...].astype(BF)


def flip_rows(v, y_hi):
    v = v.reshape(8, 8, 128)
    swapped = jnp.concatenate([v[:, 4:8], v[:, 0:4]], axis=1)
    return jnp.where(y_hi == 1, swapped, v).reshape(F, 128)


def unpack_kernel(g_ref, x_ref, d_ref, ids_ref, in_s):
    in_s[...] = g_ref[...].astype(F32)
    for q in range(4):
        ref = (x_ref, d_ref)[q // 2]
        for j in range(8):
            ref[q % 2, :, 128 * j:128 * j + 128] = in_s[pl.ds(j * 4 + q, F, stride=STEP), :].astype(BF)
    ids_ref[:, 0:128] = in_s[pl.ds(32, F, stride=STEP), :].astype(BF)


def tail_kernel(g_ref, ids_ref, score_ref, table_ref, in_s, out_s):
    y_hi = lax.axis_index("tp") >> 1
    in_s[...] = g_ref[...].astype(F32)
    for p in range(2):
        for j in range(8):
            rows = in_s[pl.ds(p * 8 + j, F, stride=24), :]
            out_s[pl.ds(128 * j + p, F, stride=2), :] = flip_rows(rows, y_hi)
    for j in range(8):
        score_ref[:, 128 * j:128 * j + 128] = out_s[128 * j:128 * j + 128].astype(BF)
    total = jnp.sum(in_s[...].reshape(F, 24, 128)[:, 16:24], axis=0)
    cols = jnp.concatenate([total[:, 0:64], total[:, 64:128]], axis=0)
    ids = ids_ref[:, 0:1]
    onehot = (ids == lax.broadcasted_iota(jnp.int32, (F, CONCEPTS), 1).astype(F32)).astype(F32)
    table_ref[...] = jnp.dot(cols, onehot, precision=lax.Precision.HIGHEST, preferred_element_type=F32)


def forward(h_s, w_ref, out_ref):
    for part in range(4):
        cols = pl.ds(256 * part, 256)
        total = jnp.zeros((2 * F, 256), F32)
        for k in range(4):
            total = total + jnp.dot(h_s[k], w_ref[k, :, cols], preferred_element_type=F32)
        out_ref[:, cols] = total.astype(BF)


def eye128():
    return lax.broadcasted_iota(jnp.int32, (128, 128), 0) == lax.broadcasted_iota(jnp.int32, (128, 128), 1)


def spots():
    return [(pl.ds(64 * p, 64), pl.ds(128 * h, 128), pl.ds(512 + 128 * h, 128)) for p in range(2) for h in range(4)]


def latent_kernel(wq_ref, wk_ref, x0, x1, x2, x3, mod_ref, temp_ref,
                  u0, u1, u2, u3, qk_ref, soft_ref, stat_ref, w_ref, h_s, g_s, sems):
    xs, outs = (x0, x1, x2, x3), (u0, u1, u2, u3)
    me = lax.axis_index("tp")
    copies = []
    for k in range(4):
        rows = pl.ds(pl.multiple_of((me ^ k) * W, W), W)
        copies.append([
            pltpu.make_async_copy(ref.at[rows], w_ref.at[k, :, pl.ds(512 * i, 512)], sems.at[2 * k + i])
            for i, ref in enumerate((wq_ref, wk_ref))])
        for copy in copies[k]:
            copy.start()
    sq = jnp.zeros((2 * F, 128), F32)
    for k in range(4):
        for j in range(8):
            x = xs[k][:, :, 128 * j:128 * j + 128].astype(F32).reshape(2 * F, 128)
            sq = sq + x * x
    inv = lax.rsqrt(jnp.sum(sq, axis=-1, keepdims=True) / D + EPS)
    lane = lax.broadcasted_iota(jnp.int32, (2 * F, 128), 1)
    stat_ref[...] = jnp.where(lane == 0, inv, 0.0)
    for k in range(4):
        for j in range(4):
            lanes = pl.ds(256 * j, 256)
            m = mod_ref[k, :, lanes]
            n = xs[k][:, :, lanes].astype(F32).reshape(2 * F, 256) * inv
            h_s[k, :, lanes] = (n * jnp.concatenate([m, m], axis=0)).astype(BF)
    total = jnp.zeros((2 * F, W), F32)
    for k in range(4):
        for copy in copies[k]:
            copy.wait()
        total = total + jnp.dot(h_s[k], w_ref[k], preferred_element_type=F32)
    qk_ref[...] = total.astype(BF)

    temp = temp_ref[:, 0:64]
    where = spots()
    qs = [qk_ref[r, ql] for r, ql, _ in where]
    ks = [qk_ref[r, kl] for r, _, kl in where]
    scores = [nt(q, k) * temp for q, k in zip(qs, ks)]
    tops = [jnp.max(v, axis=-1, keepdims=True) for v in scores]
    exps = [jnp.exp(v - t) for v, t in zip(scores, tops)]
    sums = [jnp.sum(e, axis=-1, keepdims=True) for e in exps]
    ws = [e / v for e, v in zip(exps, sums)]
    for i, w in enumerate(ws):
        soft_ref[64 * i:64 * i + 64, :] = w
    gqs = [(-jnp.dot(w.astype(BF), k, preferred_element_type=F32)).astype(BF) for w, k in zip(ws, ks)]
    gks = [(-jnp.dot(w.T.astype(BF), q, preferred_element_type=F32)).astype(BF) for w, q in zip(ws, qs)]
    part = [jnp.zeros((F, HD), F32), jnp.zeros((F, HD), F32)]
    for i, (r, ql, kl) in enumerate(where):
        g_s[r, ql] = gqs[i]
        g_s[r, kl] = gks[i]
        part[i // 4] = part[i // 4] + gqs[i].astype(F32) * qs[i].astype(F32) + gks[i].astype(F32) * ks[i].astype(F32)
    scal = jnp.sum(jnp.concatenate(part, axis=0), axis=-1, keepdims=True)
    srow = jnp.sum(jnp.where(eye128(), scal, 0.0), axis=0, keepdims=True)
    hi = srow.astype(BF).astype(F32)
    sub = lax.broadcasted_iota(jnp.int32, (16, 128), 0)
    stats = jnp.where(sub == 0, hi, jnp.where(sub == 1, srow - hi, 0.0)).astype(BF)
    for k in (3, 2, 1, 0):
        for j in range(4):
            outs[k][0:128, 256 * j:256 * j + 256] = nt(g_s[...], w_ref[k, 256 * j:256 * j + 256, :]).astype(BF)
        outs[k][128:144, 0:128] = stats
        outs[k][128:144, 128:1024] = jnp.zeros((16, 896), BF)


def normed_of(x_ref, d_ref, lanes, inv, mean):
    n = x_ref[:, :, lanes].astype(F32).reshape(2 * F, -1) * inv
    d = d_ref[:, :, lanes].astype(F32).reshape(2 * F, -1)
    return n, inv * (d - n * mean)


def tangent_kernel(x0, x1, x2, x3, d0, d1, d2, d3, u0, u1, u2, u3, mod_ref, stat_ref, qk_ref, soft_ref, temp_ref, _, w_ref,
                   o0, o1, o2, o3, h_s, tan_s, g_s, drift_s, term_s):
    xs, ds, us, outs = (x0, x1, x2, x3), (d0, d1, d2, d3), (u0, u1, u2, u3), (o0, o1, o2, o3)
    me = lax.axis_index("tp")
    sd = jnp.zeros((2 * F, 128), F32)
    for k in range(4):
        for j in range(8):
            x = xs[k][:, :, 128 * j:128 * j + 128].astype(F32).reshape(2 * F, 128)
            d = ds[k][:, :, 128 * j:128 * j + 128].astype(F32).reshape(2 * F, 128)
            sd = sd + x * d
    inv = jnp.sum(stat_ref[...], axis=-1, keepdims=True)
    mean = inv * (jnp.sum(sd, axis=-1, keepdims=True) / D)

    for k in range(4):
        for j in range(4):
            lanes = pl.ds(256 * j, 256)
            nd = normed_of(xs[k], ds[k], lanes, inv, mean)[1]
            m = mod_ref[k, :, lanes]
            h_s[k, :, lanes] = (nd * jnp.concatenate([m, m], axis=0)).astype(BF)
    forward(h_s, w_ref, tan_s)

    temp = temp_ref[:, 0:64]
    where = spots()
    qs = [qk_ref[r, ql] for r, ql, _ in where]
    ks = [qk_ref[r, kl] for r, _, kl in where]
    qts = [tan_s[r, ql] for r, ql, _ in where]
    kts = [tan_s[r, kl] for r, _, kl in where]
    ws = [soft_ref[64 * i:64 * i + 64, :] for i in range(8)]
    tdots = [nt(jnp.concatenate([a, b], axis=1), jnp.concatenate([c, d], axis=1)) for a, b, c, d in zip(qts, qs, ks, kts)]
    means = [jnp.sum(w * t, axis=-1, keepdims=True) for w, t in zip(ws, tdots)]
    curs = [temp * w * (t - m) for w, t, m in zip(ws, tdots, means)]
    cw = [jnp.concatenate([c, w], axis=1).astype(BF) for w, c in zip(ws, curs)]
    cwt = [jnp.concatenate([c, w], axis=0).T.astype(BF) for w, c in zip(ws, curs)]
    aqs = [jnp.dot(m, jnp.concatenate([k, kt], axis=0), preferred_element_type=F32) for m, k, kt in zip(cw, ks, kts)]
    aks = [jnp.dot(m, jnp.concatenate([q, qt], axis=0), preferred_element_type=F32) for m, q, qt in zip(cwt, qs, qts)]
    for i, (r, ql, kl) in enumerate(where):
        g_s[r, ql] = (-aqs[i]).astype(BF)
        g_s[r, kl] = (-aks[i]).astype(BF)

    for k in range(4):
        for j in range(4):
            drift_s[k, :, 256 * j:256 * j + 256] = nt(g_s[...], w_ref[k, 256 * j:256 * j + 256, :])
    rr = lax.broadcasted_iota(jnp.int32, (128, 256), 0)
    cc = lax.broadcasted_iota(jnp.int32, (128, 256), 1)
    pick = (((rr >> 3) & 3) == (cc >> 6)) & ((rr >> 5) == ((cc >> 4) & 3)) & ((rr & 7) == (cc & 7))
    pick = pick.astype(BF)
    late = ((lax.broadcasted_iota(jnp.int32, (F, 256), 1) >> 3) & 1) == 1
    for k in range(4):
        for j in range(4):
            lanes = pl.ds(256 * j, 256)
            n, nd = normed_of(xs[k], ds[k], lanes, inv, mean)
            terms = n * drift_s[k, :, lanes] + nd * us[k][0:128, lanes].astype(F32)
            terms = terms[0:64] + terms[64:128]
            split = jnp.concatenate([jnp.where(late, 0.0, terms), jnp.where(late, terms, 0.0)], axis=0).astype(BF)
            moved = nt(pick, split).astype(BF)
            spot = pl.ds(pl.multiple_of((me ^ k) * 256 + 128 * (j // 2), 128), 128)
            low = 32 * (j % 2)
            for t in range(4):
                term_s[t, low:low + 32, spot] = moved[32 * t:32 * t + 32]
    for k in range(4):
        outs[k][...] = term_s[me ^ k]


def local_call(kernel, args, outs, scratch, limit, name, flops=1 << 20, hbm=0):
    vm = pl.BlockSpec(memory_space=pltpu.VMEM)
    args = [pltpu.with_memory_space_constraint(v, pltpu.HBM) if i < hbm else v for i, v in enumerate(args)]
    return pl.pallas_call(
        kernel,
        out_shape=tuple(jax.ShapeDtypeStruct(s, t) for s, t in outs),
        in_specs=[pl.BlockSpec(memory_space=pltpu.HBM)] * hbm + [vm] * (len(args) - hbm),
        out_specs=tuple(vm for _ in outs),
        scratch_shapes=scratch,
        compiler_params=pltpu.CompilerParams(vmem_limit_bytes=limit * 1024 * 1024),
        cost_estimate=pl.CostEstimate(flops=flops, bytes_accessed=1 << 20, transcendentals=0),
        name=name,
    )(*args)


def add_kernel(_, a_ref, b_ref, o_ref):
    o_ref[...] = (a_ref[...].astype(F32) + b_ref[...].astype(F32)).astype(BF)


def merge_kernel(a_ref, b_ref, o_ref):
    o_ref[0:128, :] = (a_ref[0:128, :].astype(F32) + b_ref[0:128, :].astype(F32)).astype(BF)
    o_ref[128:144, :] = jnp.concatenate(
        [a_ref[128:144, 0:128], b_ref[128:144, 0:128], a_ref[128:144, 256:1024]], axis=1)


def score_kernel(a_ref, b_ref, c_ref, x_ref, mod_ref, stat_ref, score_ref):
    srow = jnp.zeros((1, 128), F32)
    for ref, lane in ((a_ref, 0), (b_ref, 0), (c_ref, 0), (c_ref, 128)):
        part = ref[128:144, lane:lane + 128].astype(F32)
        srow = srow + (part[0:1] + part[1:2])
    mean = jnp.sum(jnp.where(eye128(), srow, 0.0), axis=1, keepdims=True) / D
    inv = jnp.sum(stat_ref[...], axis=1, keepdims=True)
    for j in range(4):
        lanes = pl.ds(256 * j, 256)
        units = (a_ref[0:128, lanes].astype(F32) + b_ref[0:128, lanes].astype(F32)) + c_ref[0:128, lanes].astype(F32)
        mod = mod_ref[0, :, lanes]
        mod = jnp.concatenate([mod, mod], axis=0)
        x = x_ref[:, :, lanes].astype(F32).reshape(2 * F, 256)
        score_ref[:, :, lanes] = (inv * (mod * units - (x * inv) * mean)).astype(BF).reshape(2, F, 256)


def body(latent, direction, concept, timestep, concept_table, w_query, w_key):
    cross = []
    for s in range(64):
        for t in range(4):
            cross.append((4 * s + t, 4 * (s ^ 4) + (t ^ 2)))
    core = [(t, t ^ 1) for t in range(4)]
    swap_core = lambda v: lax.ppermute(v, "tp", core)
    swap_chip = lambda v: lax.ppermute(v, ("seq", "tp"), cross)
    vmem = pltpu.VMEM

    sent, = local_call(
        pack_kernel, (latent.reshape(2 * F, W), direction.reshape(2 * F, W), concept.reshape(1, 1)),
        (((F * STEP, 128), BF),), (vmem((4 * F * 8, 128), F32), vmem((F * STEP, 128), F32)), 60, "pack")
    got = lax.all_to_all(sent, "seq", split_axis=0, concat_axis=0, tiled=True)

    t_core = swap_core(concept_table)
    t_chip = swap_chip(concept_table)
    t_both = swap_core(t_chip)

    half = ((2, F, W), BF)
    x0, d0, ids = local_call(
        unpack_kernel, (got,), (half, half, ((F, 2 * W), BF)), (vmem((F * STEP, 128), F32),), 8, "unpack")

    steps = ((0.25 + 1.75 * timestep.astype(F32) / STEPS) / math.sqrt(HD)).reshape(F, 1)
    mod, ids_late, temp = local_call(
        mod_kernel, (concept_table, t_core, t_chip, t_both, ids, steps),
        (((4, F, W), F32), ((F, 128), F32), ((F, 128), F32)), (), 8, "mod", 1 << 30)
    relay = lambda *v: local_call(relay_kernel, v, (half,), (), 4, "relay")[0]
    x2 = swap_chip(x0)
    x1 = swap_core(x0)
    x3 = swap_core(x2)
    d1 = swap_core(d0)
    d2 = swap_chip(relay(x3, mod, d0))

    units, terms = ((144, W), BF), ((F, W), BF)
    u0, u1, u2, u3, qk, soft, stat, weights = local_call(
        latent_kernel, (w_query, w_key, x0, x1, x2, x3, mod, temp),
        (units,) * 4
        + (((2 * F, W), BF), ((8 * F, F), F32), ((2 * F, 128), F32), ((4, W, W), BF)),
        (vmem((4, 2 * F, W), BF), vmem((2 * F, W), BF), pltpu.SemaphoreType.DMA((8,))), 20, "latents", 1 << 30, hbm=2)
    d3 = swap_core(relay(stat, d2))
    far = swap_core(u3)
    summed, = local_call(merge_kernel, (u2, far), (units,), (), 4, "merge")
    arrived = swap_chip(summed)
    beside = swap_core(u1)

    v0, v1, v2, v3 = local_call(
        tangent_kernel,
        (x0, x1, x2, x3, d0, d1, d2, d3, u0, u1, u2, u3, mod, stat, qk, soft, temp, summed, weights), (terms,) * 4,
        (vmem((4, 2 * F, W), BF), vmem((2 * F, W), BF), vmem((2 * F, W), BF), vmem((4, 2 * F, W), F32),
         vmem((4, F, W), BF)), 20, "tangent", 1 << 34)
    score, = local_call(score_kernel, (u0, beside, arrived, x0, mod, stat), (half,), (), 4, "score")
    v_far = swap_core(v3)
    v_sum, = local_call(add_kernel, (score, v2, v_far), (terms,), (), 4, "add")
    v_chip = swap_chip(v_sum)
    v_near = swap_core(v1)
    total = (v0.astype(F32) + v_near.astype(F32) + v_chip.astype(F32)).astype(BF)

    score_rows = jnp.transpose(score, (1, 0, 2)).reshape(F, 16, 128)
    term_rows = jnp.transpose(total.reshape(8, 8, 8, 128), (2, 0, 1, 3)).reshape(F, 8, 128)
    back = lax.all_to_all(
        jnp.concatenate([score_rows, term_rows], axis=1), "seq", split_axis=0, concat_axis=0, tiled=True)
    score_field, table = local_call(
        tail_kernel, (back.reshape(F * 24, 128), ids_late), (((2 * F, W), BF), ((16, CONCEPTS), F32)),
        (vmem((F * 24, 128), F32), vmem((2 * F * 8, 128), F32)), 8, "tail")
    return (score_field.reshape(1, 2 * F, W), table.T)


def solution(mesh):
    in_specs = (
        P("seq", None, "tp"),
        P("seq", None, "tp"),
        P("seq"),
        P(),
        P(None, "tp"),
        P(None, "tp"),
        P(None, "tp"),
    )
    out_specs = (P("seq", None, "tp"), P(None, ("seq", "tp")))
    return jax.shard_map(body, mesh=mesh, in_specs=in_specs, out_specs=out_specs, check_vma=False)
```

time: 374 us -> 99.8 us (0.27)
  waiting for transfers between devices: 213 us -> 30.5 us
  starting transfers between devices: 67.7 us -> 20.8 us
  matrix products: 33.3 us -> 0 us
  Pallas kernels: 0 us -> 17.2 us
  between operations: 14.9 us -> 1.43 us
  other arithmetic: 9.44 us -> 0.75 us
  local copies, waits for them, and re-layouts: 11.9 us -> 3.25 us
    psum x1 -> x0, waiting for transfers between devices: 57.8 us -> none  [body(): summed = lax.psum(units, 'tp')]
    all_gather x3 -> x0, waiting for transfers between devices: 54.7 us -> none  [the longest x1 28.9 us: body(): lax.all_gather(concept_table, 'tp', axis=1, tiled=True)]
    all_to_all x9 -> x1, starting transfers between devices: 67.5 us -> 12.9 us  [body(): got = lax.all_to_all(sent, 'seq', split_axis=0, concat_axis=0, tiled=True)]
    all_to_all x9 -> x1, waiting for transfers between devices: 61 us -> 6.6 us  [body(): got = lax.all_to_all(sent, 'seq', split_axis=0, concat_axis=0, tiled=True)]
    unnamed x6 -> x0, waiting for transfers between devices: 39.9 us -> none
    dot_general x19 -> x0, matrix products: 33.3 us -> none  [the longest x2 9.82 us: project_back(): jnp.dot(second.reshape(lead, -1), second_w.T, preferred_element_type=jnp....]
    all_to_all x0 -> x1, blocking collectives: none -> 25.6 us  [body(): lax.all_to_all(jnp.concatenate([score_rows, term_rows], axis=1), 'seq', s...]
    ppermute x0 -> x15, waiting for transfers between devices: none -> 23.9 us  [the longest x5 23.2 us: body(): swap_chip = lambda v: lax.ppermute(v, ('seq', 'tp'), cross)]
  transfers between devices with their start and end apart: 14 -> 16, of which waited for: 12 -> 7; matrix products, arithmetic and copies ran while one was open for 8% -> 1% of each run, Pallas kernels for 0% -> 14%
where the time goes in v2:
time: 99.8 us; the launch traced here: 99.5 us
  waiting for transfers between devices  30.5 us (31%)
  blocking collectives  25.6 us (26%)
  starting transfers between devices  20.8 us (21%)
  Pallas kernels  17.2 us (17%)
  local copies, waits for them, and re-layouts  3.25 us (3%)
  between operations  1.43 us (1%)
    all_to_all x1, blocking collectives, body(): lax.all_to_all(jnp.concatenate([score_rows, term_rows], axis=1), 'seq', s...  25.6 us
    ppermute x5, waiting for transfers between devices, body(): swap_chip = lambda v: lax.ppermute(v, ('seq', 'tp'), cross)  23.2 us
    pallas_call x11, Pallas kernels, local_call(): pl.pallas_call(kernel, out_shape=tuple((jax.ShapeDtypeStruct(s, t) for s,...  17.2 us
    all_to_all x1, starting transfers between devices, body(): got = lax.all_to_all(sent, 'seq', split_axis=0, concat_axis=0, tiled=True)  12.9 us
    all_to_all x1, waiting for transfers between devices, body(): got = lax.all_to_all(sent, 'seq', split_axis=0, concat_axis=0, tiled=True)  6.6 us
    ppermute x5, starting transfers between devices, body(): swap_chip = lambda v: lax.ppermute(v, ('seq', 'tp'), cross)  6.03 us
    unnamed x6, local copies, waits for them, and re-layouts  2.68 us
  transfers between devices with their start and end apart: 16, of which 7 were waited for; matrix products, arithmetic and copies ran while one was open for 1% of the time, Pallas kernels for 14%

profile of v2, /device:TPU:8, one launch (start us, length us, event | category | flops | bytes accessed | tf_op | source)
XLA Modules:
  0.0 99.5 jit_solution(9783605460466918227)
XLA Ops:
  1.3 2.3 %pack.1 = bf16[2560,128]{1,0:T(8,128)(2,1)} custom-call(bf16[128,1024]{1,0:T(8,128)(2,1)} %bitcast.22, bf16[128,1024]{1,0:T(8,128)(2,1)} %bitcast.23, s32[1,1]{1,0:T(1,128)} %bitcast.16.ids_ref), custom_call_target="tpu_custom_call" | custom-call | flops 1048576 | bytes 1048576 | tf_op jit(solution)/shard_map/pack/pallas_call | solution.py:239
  3.6 12.9 %all-to-all-start = ((bf16[64,40,128]{2,1,0:T(8,128)(2,1)}), bf16[64,40,128]{2,1,0:T(8,128)(2,1)S(1)}, u32[]{:S(2)}, u32[]{:S(2)}) async-start(bf16[64,40,128]{2,1,0:T(8,128)(2,1)} %bitcast.20), calls=%async_computation | async-start | bytes 1310720 | tf_op jit(solution)/shard_map/all_to_all | solution.py:290
  16.5 1.4 %collective-permute-start.4 = (bf16[256,1024]{1,0:T(8,128)(2,1)}, bf16[256,1024]{1,0:T(8,128)(2,1)S(1)}, u32[]{:S(2)}, u32[]{:S(2)}) collective-permute-start(bf16[256,1024]{1,0:T(8,128)(2,1)} %t0.1), channel_id=1, source_target_pairs={{0,18},{1,19},{2,16},{3,17},{4,22},{5,23},{6,20},{7,21},{8,26},{9,... | collective-permute-start | bytes 1572872 | tf_op jit(solution)/shard_map/ppermute | solution.py:284
  17.9 0.0 collective-permute-start.3
  17.9 12.0 %collective-permute-done.4.t2 = bf16[256,1024]{1,0:T(8,128)(2,1)S(1)} collective-permute-done((bf16[256,1024]{1,0:T(8,128)(2,1)}, bf16[256,1024]{1,0:T(8,128)(2,1)S(1)}, u32[]{:S(2)}, u32[]{:S(2)}) %collective-permute-start.4) | collective-permute-done | bytes 524320 | tf_op jit(solution)/shard_map/ppermute | solution.py:284
  29.9 0.0 collective-permute-start.5
  29.9 6.6 %all-to-all-done = bf16[64,40,128]{2,1,0:T(8,128)(2,1)S(1)} async-done(((bf16[64,40,128]{2,1,0:T(8,128)(2,1)}), bf16[64,40,128]{2,1,0:T(8,128)(2,1)S(1)}, u32[]{:S(2)}, u32[]{:S(2)}) %all-to-all-start) | async-done | bytes 655392 | tf_op jit(solution)/shard_map/all_to_all | solution.py:290
  36.5 0.3 unpack.1
  36.8 0.0 copy-start.1
  36.9 0.7 copy-done.1
  37.5 1.8 %collective-permute-start.1 = (bf16[2,64,1024]{2,1,0:T(8,128)(2,1)S(1)}, bf16[2,64,1024]{2,1,0:T(8,128)(2,1)S(1)}, u32[]{:S(2)}, u32[]{:S(2)}) collective-permute-start(bf16[2,64,1024]{2,1,0:T(8,128)(2,1)S(1)} %get-tuple-element.22.x0.x_ref), channel_id=1, source_target_pairs={{0,18},{1,19},{2,16},{3,17},{4,22},{5,23},{6,20},{7,21},{8,26},{9,... | collective-permute-start | bytes 786440 | tf_op jit(solution)/shard_map/ppermute | solution.py:284
  39.3 0.0 collective-permute-start
  39.3 4.6 %collective-permute-done.1.x2 = bf16[2,64,1024]{2,1,0:T(8,128)(2,1)S(1)} collective-permute-done((bf16[2,64,1024]{2,1,0:T(8,128)(2,1)S(1)}, bf16[2,64,1024]{2,1,0:T(8,128)(2,1)S(1)}, u32[]{:S(2)}, u32[]{:S(2)}) %collective-permute-start.1) | collective-permute-done | bytes 262176 | tf_op jit(solution)/shard_map/ppermute | solution.py:284
  43.9 0.0 collective-permute-start.2
  43.9 0.7 multiply_bitcast_fusion
  44.6 0.1 copy.11.steps_ref
  44.7 0.0 collective-permute-done.3.t1
  44.7 0.0 collective-permute-done.5.t3
  44.7 0.0 copy-start
  44.7 1.0 %copy-done = bf16[256,1024]{1,0:T(8,128)(2,1)S(1)} copy-done((bf16[256,1024]{1,0:T(8,128)(2,1)S(1)}, bf16[256,1024]{1,0:T(8,128)(2,1)}, u32[]{:S(2)}) %copy-start) | copy-done | bytes 524312
  45.7 0.0 copy-start.2
  45.7 0.9 copy-done.2
  46.7 0.5 mod.1
  47.2 0.0 collective-permute-done.2.x3.refs_0_
  47.3 1.9 %collective-permute-start.10 = (bf16[2,64,1024]{2,1,0:T(8,128)(2,1)S(1)}, bf16[2,64,1024]{2,1,0:T(8,128)(2,1)S(1)}, u32[]{:S(2)}, u32[]{:S(2)}) collective-permute-start(bf16[2,64,1024]{2,1,0:T(8,128)(2,1)S(1)} %relay.2), channel_id=1, source_target_pairs={{0,18},{1,19},{2,16},{3,17},{4,22},{5,23},{6,20},{7,21},{8,26},{9,... | collective-permute-start | bytes 786440 | tf_op jit(solution)/shard_map/ppermute | solution.py:284
  49.1 0.0 collective-permute-done.x1
  49.1 7.3 %latents.1 = (bf16[144,1024]{1,0:T(8,128)(2,1)S(1)}, bf16[144,1024]{1,0:T(8,128)(2,1)S(1)}, bf16[144,1024]{1,0:T(8,128)(2,1)S(1)}, bf16[144,1024]{1,0:T(8,128)(2...) custom-call(bf16[4096,512]{1,0:T(8,128)(2,1)} %wq_ref.1, ...), custom_call_target="tpu_custom_call" | custom-call | flops 1073741824 | bytes 1048576 | tf_op jit(solution)/shard_map/latents/pallas_call | solution.py:239
  56.4 0.3 collective-permute-start.7
  56.7 0.3 collective-permute-start.9
  57.0 0.0 collective-permute-done.10.refs_1_.d2
  57.0 0.3 collective-permute-start.11
  57.3 0.3 collective-permute-start.6
  57.6 0.4 collective-permute-done.7.b_ref
  58.0 0.1 merge.1._
  58.1 0.5 collective-permute-start.8
  58.6 0.0 collective-permute-done.9.d1
  58.6 0.2 collective-permute-done.11.d3
  58.8 5.4 %tangent.1 = (bf16[64,1024]{1,0:T(8,128)(2,1)S(1)}, bf16[64,1024]{1,0:T(8,128)(2,1)S(1)}, bf16[64,1024]{1,0:T(8,128)(2,1)S(1)}, bf16[64,1024]{1,0:T(8,128)(2,1)S(1)}) custom-call(bf16[2,64,1024]{2,1,0:T(8,128)(2,1)S(1)} %get-tuple-element.22.x0.x_ref, bf16[2,64,1024]{2,1,0:T(8,128)(2,1)S(1)} %collective-permute-done.x1, ...), custom_call_target="tpu_custom_call" | custom-call | flops 17179869184 | bytes 1048576 | tf_op jit(solution)/shard_map/tangent/pallas_call | solution.py:239
  64.2 0.3 collective-permute-start.13
  64.5 0.3 collective-permute-start.12
  64.8 0.0 collective-permute-done.6.b_ref
  64.8 2.5 %collective-permute-done.8.c_ref = bf16[144,1024]{1,0:T(8,128)(2,1)S(1)} collective-permute-done((bf16[144,1024]{1,0:T(8,128)(2,1)S(1)}, bf16[144,1024]{1,0:T(8,128)(2,1)S(1)}, u32[]{:S(2)}, u32[]{:S(2)}) %collective-permute-start.8) | collective-permute-done | bytes 294944 | tf_op jit(solution)/shard_map/ppermute | solution.py:284
  67.3 0.3 score.1._
  67.6 0.0 collective-permute-done.13.b_ref
  67.7 0.5 collective-permute-start.14
  68.2 0.3 copy.12
  68.5 0.2 reshape.37
  68.7 0.0 collective-permute-done.12
  68.7 4.0 %collective-permute-done.14 = bf16[64,1024]{1,0:T(8,128)(2,1)S(1)} collective-permute-done((bf16[64,1024]{1,0:T(8,128)(2,1)S(1)}, bf16[64,1024]{1,0:T(8,128)(2,1)S(1)}, u32[]{:S(2)}, u32[]{:S(2)}) %collective-permute-start.14) | collective-permute-done | bytes 131104 | tf_op jit(solution)/shard_map/ppermute | solution.py:284
  72.7 0.1 fusion
  72.8 25.6 %all_to_all.16 = bf16[64,24,128]{2,1,0:T(8,128)(2,1)S(1)} all-to-all(bf16[64,24,128]{2,1,0:T(8,128)(2,1)S(1)} %pad_maximum_fusion), channel_id=1, replica_groups=mesh['seq'=64,'tp'=4] {'seq'}, dimensions={0} | all-to-all | bytes 786432 | tf_op jit(solution)/shard_map/all_to_all | solution.py:337
  98.4 1.0 %tail.1 = (bf16[128,1024]{1,0:T(8,128)(2,1)}, f32[16,256]{1,0:T(8,128)}) custom-call(bf16[1536,128]{1,0:T(8,128)(2,1)S(1)} %bitcast.19, f32[64,128]{1,0:T(8,128)S(1)} %get-tuple-element.39.ids_ref), custom_call_target="tpu_custom_call" | custom-call | flops 1048576 | bytes 1048576 | tf_op jit(solution)/shard_map/tail/pallas_call | solution.py:239
  (5 shorter events, 0.1 us)
Async XLA Ops:
  3.6 33.0 %all-to-all-start = ((bf16[64,40,128]{2,1,0:T(8,128)(2,1)}), bf16[64,40,128]{2,1,0:T(8,128)(2,1)S(1)}, u32[]{:S(2)}, u32[]{:S(2)}) async-start(bf16[64,40,128]{2,1,0:T(8,128)(2,1)} %bitcast.20), calls=%async_computation | async-start | bytes 1310720 | tf_op jit(solution)/shard_map/all_to_all | solution.py:290
  16.5 13.4 %collective-permute-start.4 = (bf16[256,1024]{1,0:T(8,128)(2,1)}, bf16[256,1024]{1,0:T(8,128)(2,1)S(1)}, u32[]{:S(2)}, u32[]{:S(2)}) collective-permute-start(bf16[256,1024]{1,0:T(8,128)(2,1)} %t0.1), channel_id=1, source_target_pairs={{0,18},{1,19},{2,16},{3,17},{4,22},{5,23},{6,20},{7,21},{8,26},{9,... | collective-permute-start | bytes 1572872 | tf_op jit(solution)/shard_map/ppermute | solution.py:284
  17.9 26.8 %collective-permute-start.3 = (bf16[256,1024]{1,0:T(8,128)(2,1)}, bf16[256,1024]{1,0:T(8,128)(2,1)S(1)}, u32[]{:S(2)}, u32[]{:S(2)}) collective-permute-start(bf16[256,1024]{1,0:T(8,128)(2,1)} %t0.1), channel_id=1, source_target_pairs={{0,1},{1,0},{2,3},{3,2},{4,5},{5,4},{6,7},{7,6},{8,9},{9,8},{10,11... | collective-permute-start | bytes 1572872 | tf_op jit(solution)/shard_map/ppermute | solution.py:283
  29.9 14.7 %collective-permute-start.5 = (bf16[256,1024]{1,0:T(8,128)(2,1)S(1)}, bf16[256,1024]{1,0:T(8,128)(2,1)S(1)}, u32[]{:S(2)}, u32[]{:S(2)}) collective-permute-start(bf16[256,1024]{1,0:T(8,128)(2,1)S(1)} %collective-permute-done.4.t2), channel_id=1, source_target_pairs={{0,1},{1,0},{2,3},{3,2},{4,5},{5,4},{6,7},{7,6},{8,9},{9,8},{10,11... | collective-permute-start | bytes 1572872 | tf_op jit(solution)/shard_map/ppermute | solution.py:283
  36.8 0.7 copy-start.1
  37.5 6.4 %collective-permute-start.1 = (bf16[2,64,1024]{2,1,0:T(8,128)(2,1)S(1)}, bf16[2,64,1024]{2,1,0:T(8,128)(2,1)S(1)}, u32[]{:S(2)}, u32[]{:S(2)}) collective-permute-start(bf16[2,64,1024]{2,1,0:T(8,128)(2,1)S(1)} %get-tuple-element.22.x0.x_ref), channel_id=1, source_target_pairs={{0,18},{1,19},{2,16},{3,17},{4,22},{5,23},{6,20},{7,21},{8,26},{9,... | collective-permute-start | bytes 786440 | tf_op jit(solution)/shard_map/ppermute | solution.py:284
  39.3 9.8 %collective-permute-start = (bf16[2,64,1024]{2,1,0:T(8,128)(2,1)S(1)}, bf16[2,64,1024]{2,1,0:T(8,128)(2,1)S(1)}, u32[]{:S(2)}, u32[]{:S(2)}) collective-permute-start(bf16[2,64,1024]{2,1,0:T(8,128)(2,1)S(1)} %get-tuple-element.22.x0.x_ref), channel_id=1, source_target_pairs={{0,1},{1,0},{2,3},{3,2},{4,5},{5,4},{6,7},{7,6},{8,9},{9,8},{10,11... | collective-permute-start | bytes 786440 | tf_op jit(solution)/shard_map/ppermute | solution.py:283
  43.9 3.3 %collective-permute-start.2 = (bf16[2,64,1024]{2,1,0:T(8,128)(2,1)S(1)}, bf16[2,64,1024]{2,1,0:T(8,128)(2,1)S(1)}, u32[]{:S(2)}, u32[]{:S(2)}) collective-permute-start(bf16[2,64,1024]{2,1,0:T(8,128)(2,1)S(1)} %collective-permute-done.1.x2), channel_id=1, source_target_pairs={{0,1},{1,0},{2,3},{3,2},{4,5},{5,4},{6,7},{7,6},{8,9},{9,8},{10,11... | collective-permute-start | bytes 786440 | tf_op jit(solution)/shard_map/ppermute | solution.py:283
  44.7 1.0 %copy-start = (bf16[256,1024]{1,0:T(8,128)(2,1)S(1)}, bf16[256,1024]{1,0:T(8,128)(2,1)}, u32[]{:S(2)}) copy-start(bf16[256,1024]{1,0:T(8,128)(2,1)} %t0.1) | copy-start | bytes 1572868
  45.7 0.9 copy-start.2
  47.3 9.7 %collective-permute-start.10 = (bf16[2,64,1024]{2,1,0:T(8,128)(2,1)S(1)}, bf16[2,64,1024]{2,1,0:T(8,128)(2,1)S(1)}, u32[]{:S(2)}, u32[]{:S(2)}) collective-permute-start(bf16[2,64,1024]{2,1,0:T(8,128)(2,1)S(1)} %relay.2), channel_id=1, source_target_pairs={{0,18},{1,19},{2,16},{3,17},{4,22},{5,23},{6,20},{7,21},{8,26},{9,... | collective-permute-start | bytes 786440 | tf_op jit(solution)/shard_map/ppermute | solution.py:284
  56.4 1.7 %collective-permute-start.7 = (bf16[144,1024]{1,0:T(8,128)(2,1)S(1)}, bf16[144,1024]{1,0:T(8,128)(2,1)S(1)}, u32[]{:S(2)}, u32[]{:S(2)}) collective-permute-start(bf16[144,1024]{1,0:T(8,128)(2,1)S(1)} %get-tuple-element.29.u3), channel_id=1, source_target_pairs={{0,1},{1,0},{2,3},{3,2},{4,5},{5,4},{6,7},{7,6},{8,9},{9,8},{10,11... | collective-permute-start | bytes 884744 | tf_op jit(solution)/shard_map/ppermute | solution.py:283
  56.7 1.9 %collective-permute-start.9 = (bf16[2,64,1024]{2,1,0:T(8,128)(2,1)S(1)}, bf16[2,64,1024]{2,1,0:T(8,128)(2,1)S(1)}, u32[]{:S(2)}, u32[]{:S(2)}) collective-permute-start(bf16[2,64,1024]{2,1,0:T(8,128)(2,1)S(1)} %get-tuple-element.31.refs_2_.d0), channel_id=1, source_target_pairs={{0,1},{1,0},{2,3},{3,2},{4,5},{5,4},{6,7},{7,6},{8,9},{9,8},{10,11... | collective-permute-start | bytes 786440 | tf_op jit(solution)/shard_map/ppermute | solution.py:283
  57.0 1.8 %collective-permute-start.11 = (bf16[2,64,1024]{2,1,0:T(8,128)(2,1)S(1)}, bf16[2,64,1024]{2,1,0:T(8,128)(2,1)S(1)}, u32[]{:S(2)}, u32[]{:S(2)}) collective-permute-start(bf16[2,64,1024]{2,1,0:T(8,128)(2,1)S(1)} %relay.3), channel_id=1, source_target_pairs={{0,1},{1,0},{2,3},{3,2},{4,5},{5,4},{6,7},{7,6},{8,9},{9,8},{10,11... | collective-permute-start | bytes 786440 | tf_op jit(solution)/shard_map/ppermute | solution.py:283
  57.3 7.5 %collective-permute-start.6 = (bf16[144,1024]{1,0:T(8,128)(2,1)S(1)}, bf16[144,1024]{1,0:T(8,128)(2,1)S(1)}, u32[]{:S(2)}, u32[]{:S(2)}) collective-permute-start(bf16[144,1024]{1,0:T(8,128)(2,1)S(1)} %get-tuple-element.27.u1), channel_id=1, source_target_pairs={{0,1},{1,0},{2,3},{3,2},{4,5},{5,4},{6,7},{7,6},{8,9},{9,8},{10,11... | collective-permute-start | bytes 884744 | tf_op jit(solution)/shard_map/ppermute | solution.py:283
  58.1 9.2 %collective-permute-start.8 = (bf16[144,1024]{1,0:T(8,128)(2,1)S(1)}, bf16[144,1024]{1,0:T(8,128)(2,1)S(1)}, u32[]{:S(2)}, u32[]{:S(2)}) collective-permute-start(bf16[144,1024]{1,0:T(8,128)(2,1)S(1)} %merge.1._), channel_id=1, source_target_pairs={{0,18},{1,19},{2,16},{3,17},{4,22},{5,23},{6,20},{7,21},{8,26},{9,... | collective-permute-start | bytes 884744 | tf_op jit(solution)/shard_map/ppermute | solution.py:284
  64.2 3.4 %collective-permute-start.13 = (bf16[64,1024]{1,0:T(8,128)(2,1)S(1)}, bf16[64,1024]{1,0:T(8,128)(2,1)S(1)}, u32[]{:S(2)}, u32[]{:S(2)}) collective-permute-start(bf16[64,1024]{1,0:T(8,128)(2,1)S(1)} %get-tuple-element.38), channel_id=1, source_target_pairs={{0,1},{1,0},{2,3},{3,2},{4,5},{5,4},{6,7},{7,6},{8,9},{9,8},{10,11... | collective-permute-start | bytes 393224 | tf_op jit(solution)/shard_map/ppermute | solution.py:283
  64.5 4.2 %collective-permute-start.12 = (bf16[64,1024]{1,0:T(8,128)(2,1)S(1)}, bf16[64,1024]{1,0:T(8,128)(2,1)S(1)}, u32[]{:S(2)}, u32[]{:S(2)}) collective-permute-start(bf16[64,1024]{1,0:T(8,128)(2,1)S(1)} %get-tuple-element.36), channel_id=1, source_target_pairs={{0,1},{1,0},{2,3},{3,2},{4,5},{5,4},{6,7},{7,6},{8,9},{9,8},{10,11... | collective-permute-start | bytes 393224 | tf_op jit(solution)/shard_map/ppermute | solution.py:283
  67.7 5.1 %collective-permute-start.14 = (bf16[64,1024]{1,0:T(8,128)(2,1)S(1)}, bf16[64,1024]{1,0:T(8,128)(2,1)S(1)}, u32[]{:S(2)}, u32[]{:S(2)}) collective-permute-start(bf16[64,1024]{1,0:T(8,128)(2,1)S(1)} %add.25), channel_id=1, source_target_pairs={{0,18},{1,19},{2,16},{3,17},{4,22},{5,23},{6,20},{7,21},{8,26},{9,... | collective-permute-start | bytes 393224 | tf_op jit(solution)/shard_map/ppermute | solution.py:284

commit v3 on v2

--- a/solution.py
+++ b/solution.py
@@ -14,7 +14,7 @@
 EPS = 1e-06
 F = 64
 W = 1024
-STEP = 40
+STEP = 36
 
 BF = jnp.bfloat16
 F32 = jnp.float32
@@ -25,18 +25,62 @@
     return lax.dot_general(a, b, NT, preferred_element_type=F32)
 
 
-def mod_kernel(t0, t1, t2, t3, ids_ref, steps_ref, mod_ref, late_ref, temp_ref):
-    temp_ref[...] = jnp.zeros((F, 128), F32) + steps_ref[...]
+def turn_kernel(wq_ref, wk_ref, o_ref, token_ref, w_s, t_s, sems, out_sems):
+    me = lax.axis_index("tp")
+    copies, outs = [], []
+    for k in range(4):
+        rows = pl.ds(pl.multiple_of((me ^ k) * W, W), W)
+        for i, ref in enumerate((wq_ref, wk_ref)):
+            copy = pltpu.make_async_copy(ref.at[rows], w_s.at[k, :, pl.ds(512 * i, 512)], sems.at[2 * k + i])
+            copy.start()
+            copies.append(copy)
+    for k in range(4):
+        copies[2 * k].wait()
+        copies[2 * k + 1].wait()
+        for j in range(4):
+            t_s[k, :, 256 * j:256 * j + 256] = w_s[k, 256 * j:256 * j + 256, :].T
+        out = pltpu.make_async_copy(t_s.at[k], o_ref.at[k], out_sems.at[k])
+        out.start()
+        outs.append(out)
+    for out in outs:
+        out.wait()
+    token_ref[...] = jnp.zeros_like(token_ref)
+
+
+def prepare_kernel(wq_ref, wk_ref, table_ref, t1, t2, t3, ids_ref, steps_ref, w_ref, mod_ref, t0, sems):
+    me = lax.axis_index("tp")
+    own = pltpu.make_async_copy(table_ref, t0, sems.at[8])
+    own.start()
+    copies = []
+    for k in range(4):
+        rows = pl.ds(pl.multiple_of((me ^ k) * W, W), W)
+        for i, ref in enumerate((wq_ref, wk_ref)):
+            copy = pltpu.make_async_copy(ref.at[rows], w_ref.at[k, :, pl.ds(512 * i, 512)], sems.at[2 * k + i])
+            copy.start()
+            copies.append(copy)
     ids = ids_ref[:, 0:128].astype(F32)
-    late_ref[...] = ids
     onehot = (ids[:, 0:1] == lax.broadcasted_iota(jnp.int32, (F, CONCEPTS), 1).astype(F32)).astype(BF)
-    for k, table_ref in enumerate((t0, t1, t2, t3)):
-        mod_ref[k] = 1.0 + jnp.dot(onehot, table_ref[...], preferred_element_type=F32)
-
-
-def relay_kernel(*refs):
-    v_ref, o_ref = refs[-2:]
+    for k, ref in ((1, t1), (2, t2), (3, t3), (0, t0)):
+        if k == 0:
+            own.wait()
+        mod_ref[k] = 1.0 + jnp.dot(onehot, ref[...], preferred_element_type=F32)
+    mod_ref[4, :, 0:128] = ids
+    mod_ref[4, :, 128:256] = jnp.zeros((F, 128), F32) + steps_ref[...]
+    for copy in copies:
+        copy.wait()
+
+
+def relay_kernel(_, v_ref, o_ref):
     o_ref[...] = v_ref[...]
+
+
+def join_kernel(_, a_ref, b_ref, o_ref):
+    o_ref[0:2] = a_ref[...]
+    o_ref[2:4] = b_ref[...]
+
+
+def slices(own, chip, near):
+    return [own.at[0:2], near.at[0:2], chip.at[0:2], near.at[2:4]]
 
 
 def pack_kernel(x_ref, d_ref, ids_ref, o_ref, in_s, out_s):
@@ -49,8 +93,8 @@
         for j in range(8):
             rows = in_s[pl.ds(256 * j + (q // 2) * 128 + q % 2, F, stride=2), :]
             out_s[pl.ds(j * 4 + q, F, stride=STEP), :] = flip_rows(rows, y_hi)
-        out_s[pl.ds(32 + q, F, stride=STEP), :] = jnp.zeros((F, 128), F32) + ids_ref[...].astype(F32)
-    o_ref[...] = out_s[...].astype(BF)
+        out_s[pl.ds(32 + q, F, stride=STEP), :] = jnp.zeros((F, 128), F32) + ids_ref[0].astype(F32)
+    o_ref[...] = out_s[...].astype(BF).reshape(F, 9, 4, 128)
 
 
 def flip_rows(v, y_hi):
@@ -59,8 +103,8 @@
     return jnp.where(y_hi == 1, swapped, v).reshape(F, 128)
 
 
-def unpack_kernel(g_ref, x_ref, d_ref, ids_ref, in_s):
-    in_s[...] = g_ref[...].astype(F32)
+def unpack_kernel(_, g_ref, x_ref, d_ref, ids_ref, in_s):
+    in_s[...] = g_ref[...].reshape(F * STEP, 128).astype(F32)
     for q in range(4):
         ref = (x_ref, d_ref)[q // 2]
         for j in range(8):
@@ -101,18 +145,12 @@
     return [(pl.ds(64 * p, 64), pl.ds(128 * h, 128), pl.ds(512 + 128 * h, 128)) for p in range(2) for h in range(4)]
 
 
-def latent_kernel(wq_ref, wk_ref, x0, x1, x2, x3, mod_ref, temp_ref,
-                  u0, u1, u2, u3, qk_ref, soft_ref, stat_ref, w_ref, h_s, g_s, sems):
-    xs, outs = (x0, x1, x2, x3), (u0, u1, u2, u3)
-    me = lax.axis_index("tp")
-    copies = []
-    for k in range(4):
-        rows = pl.ds(pl.multiple_of((me ^ k) * W, W), W)
-        copies.append([
-            pltpu.make_async_copy(ref.at[rows], w_ref.at[k, :, pl.ds(512 * i, 512)], sems.at[2 * k + i])
-            for i, ref in enumerate((wq_ref, wk_ref))])
-        for copy in copies[k]:
-            copy.start()
+def latent_kernel(turned_ref, x0, x2, xn, mod_ref, _, w_ref,
+                  u0, u1, u2, u3_low, u3_high, qk_ref, soft_ref, stat_ref, back_ref, h_s, g_s, u3, sems):
+    xs, outs = slices(x0, x2, xn), (u0, u1, u2, u3)
+    copies = [pltpu.make_async_copy(turned_ref.at[k], back_ref.at[k], sems.at[k]) for k in range(4)]
+    for k in (3, 2, 1, 0):
+        copies[k].start()
     sq = jnp.zeros((2 * F, 128), F32)
     for k in range(4):
         for j in range(8):
@@ -127,14 +165,9 @@
             m = mod_ref[k, :, lanes]
             n = xs[k][:, :, lanes].astype(F32).reshape(2 * F, 256) * inv
             h_s[k, :, lanes] = (n * jnp.concatenate([m, m], axis=0)).astype(BF)
-    total = jnp.zeros((2 * F, W), F32)
-    for k in range(4):
-        for copy in copies[k]:
-            copy.wait()
-        total = total + jnp.dot(h_s[k], w_ref[k], preferred_element_type=F32)
-    qk_ref[...] = total.astype(BF)
-
-    temp = temp_ref[:, 0:64]
+    forward(h_s, w_ref, qk_ref)
+
+    temp = mod_ref[4, :, 128:192]
     where = spots()
     qs = [qk_ref[r, ql] for r, ql, _ in where]
     ks = [qk_ref[r, kl] for r, _, kl in where]
@@ -158,10 +191,14 @@
     sub = lax.broadcasted_iota(jnp.int32, (16, 128), 0)
     stats = jnp.where(sub == 0, hi, jnp.where(sub == 1, srow - hi, 0.0)).astype(BF)
     for k in (3, 2, 1, 0):
-        for j in range(4):
-            outs[k][0:128, 256 * j:256 * j + 256] = nt(g_s[...], w_ref[k, 256 * j:256 * j + 256, :]).astype(BF)
+        copies[k].wait()
+        for j in range(4):
+            lanes = pl.ds(256 * j, 256)
+            outs[k][0:128, lanes] = jnp.dot(g_s[...], back_ref[k, :, lanes], preferred_element_type=F32).astype(BF)
         outs[k][128:144, 0:128] = stats
         outs[k][128:144, 128:1024] = jnp.zeros((16, 896), BF)
+    u3_low[...] = u3[0:64, :]
+    u3_high[...] = u3[64:144, :]
 
 
 def normed_of(x_ref, d_ref, lanes, inv, mean):
@@ -170,10 +207,11 @@
     return n, inv * (d - n * mean)
 
 
-def tangent_kernel(x0, x1, x2, x3, d0, d1, d2, d3, u0, u1, u2, u3, mod_ref, stat_ref, qk_ref, soft_ref, temp_ref, _, w_ref,
-                   o0, o1, o2, o3, h_s, tan_s, g_s, drift_s, term_s):
-    xs, ds, us, outs = (x0, x1, x2, x3), (d0, d1, d2, d3), (u0, u1, u2, u3), (o0, o1, o2, o3)
+def tangent_kernel(x0, x2, xn, d0, d2, dn, u0, u1, u2, u3_low, u3_high, mod_ref, stat_ref, qk_ref, soft_ref, _, w_ref, back_ref,
+                   o0, o2, near_ref, ids_ref, h_s, tan_s, g_s, drift_s, term_s):
+    xs, ds = slices(x0, x2, xn), slices(d0, d2, dn)
     me = lax.axis_index("tp")
+    ids_ref[...] = mod_ref[4, :, 0:128]
     sd = jnp.zeros((2 * F, 128), F32)
     for k in range(4):
         for j in range(8):
@@ -191,7 +229,7 @@
             h_s[k, :, lanes] = (nd * jnp.concatenate([m, m], axis=0)).astype(BF)
     forward(h_s, w_ref, tan_s)
 
-    temp = temp_ref[:, 0:64]
+    temp = mod_ref[4, :, 128:192]
     where = spots()
     qs = [qk_ref[r, ql] for r, ql, _ in where]
     ks = [qk_ref[r, kl] for r, _, kl in where]
@@ -211,7 +249,8 @@
 
     for k in range(4):
         for j in range(4):
-            drift_s[k, :, 256 * j:256 * j + 256] = nt(g_s[...], w_ref[k, 256 * j:256 * j + 256, :])
+            lanes = pl.ds(256 * j, 256)
+            drift_s[k, :, lanes] = jnp.dot(g_s[...], back_ref[k, :, lanes], preferred_element_type=F32)
     rr = lax.broadcasted_iota(jnp.int32, (128, 256), 0)
     cc = lax.broadcasted_iota(jnp.int32, (128, 256), 1)
     pick = (((rr >> 3) & 3) == (cc >> 6)) & ((rr >> 5) == ((cc >> 4) & 3)) & ((rr & 7) == (cc & 7))
@@ -221,7 +260,11 @@
         for j in range(4):
             lanes = pl.ds(256 * j, 256)
             n, nd = normed_of(xs[k], ds[k], lanes, inv, mean)
-            terms = n * drift_s[k, :, lanes] + nd * us[k][0:128, lanes].astype(F32)
+            if k == 3:
+                units = jnp.concatenate([u3_low[:, lanes], u3_high[0:64, lanes]], axis=0)
+            else:
+                units = (u0, u1, u2)[k][0:128, lanes]
+            terms = n * drift_s[k, :, lanes] + nd * units.astype(F32)
             terms = terms[0:64] + terms[64:128]
             split = jnp.concatenate([jnp.where(late, 0.0, terms), jnp.where(late, terms, 0.0)], axis=0).astype(BF)
             moved = nt(pick, split).astype(BF)
@@ -229,17 +272,20 @@
             low = 32 * (j % 2)
             for t in range(4):
                 term_s[t, low:low + 32, spot] = moved[32 * t:32 * t + 32]
-    for k in range(4):
-        outs[k][...] = term_s[me ^ k]
-
-
-def local_call(kernel, args, outs, scratch, limit, name, flops=1 << 20, hbm=0):
+    o0[...] = term_s[me]
+    o2[...] = term_s[me ^ 2]
+    near_ref[0:64, :] = term_s[me ^ 3]
+    near_ref[64:128, :] = term_s[me ^ 1]
+
+
+def local_call(kernel, args, outs, scratch, limit, name, flops=1 << 20, hbm=0, smem=0):
     vm = pl.BlockSpec(memory_space=pltpu.VMEM)
     args = [pltpu.with_memory_space_constraint(v, pltpu.HBM) if i < hbm else v for i, v in enumerate(args)]
     return pl.pallas_call(
         kernel,
         out_shape=tuple(jax.ShapeDtypeStruct(s, t) for s, t in outs),
-        in_specs=[pl.BlockSpec(memory_space=pltpu.HBM)] * hbm + [vm] * (len(args) - hbm),
+        in_specs=[pl.BlockSpec(memory_space=pltpu.HBM)] * hbm + [vm] * (len(args) - hbm - smem)
+        + [pl.BlockSpec(memory_space=pltpu.SMEM)] * smem,
         out_specs=tuple(vm for _ in outs),
         scratch_shapes=scratch,
         compiler_params=pltpu.CompilerParams(vmem_limit_bytes=limit * 1024 * 1024),
@@ -249,16 +295,17 @@
 
 
 def add_kernel(_, a_ref, b_ref, o_ref):
-    o_ref[...] = (a_ref[...].astype(F32) + b_ref[...].astype(F32)).astype(BF)
-
-
-def merge_kernel(a_ref, b_ref, o_ref):
-    o_ref[0:128, :] = (a_ref[0:128, :].astype(F32) + b_ref[0:128, :].astype(F32)).astype(BF)
+    o_ref[...] = (a_ref[...].astype(F32) + b_ref[0:64, :].astype(F32)).astype(BF)
+
+
+def merge_kernel(a_ref, low_ref, high_ref, o_ref):
+    o_ref[0:64, :] = (a_ref[0:64, :].astype(F32) + low_ref[...].astype(F32)).astype(BF)
+    o_ref[64:128, :] = (a_ref[64:128, :].astype(F32) + high_ref[0:64, :].astype(F32)).astype(BF)
     o_ref[128:144, :] = jnp.concatenate(
-        [a_ref[128:144, 0:128], b_ref[128:144, 0:128], a_ref[128:144, 256:1024]], axis=1)
-
-
-def score_kernel(a_ref, b_ref, c_ref, x_ref, mod_ref, stat_ref, score_ref):
+        [a_ref[128:144, 0:128], high_ref[64:80, 0:128], a_ref[128:144, 256:1024]], axis=1)
+
+
+def score_kernel(a_ref, b_ref, c_ref, x_ref, mod_ref, stat_ref, score_ref, out_s):
     srow = jnp.zeros((1, 128), F32)
     for ref, lane in ((a_ref, 0), (b_ref, 0), (c_ref, 0), (c_ref, 128)):
         part = ref[128:144, lane:lane + 128].astype(F32)
@@ -271,7 +318,19 @@
         mod = mod_ref[0, :, lanes]
         mod = jnp.concatenate([mod, mod], axis=0)
         x = x_ref[:, :, lanes].astype(F32).reshape(2 * F, 256)
-        score_ref[:, :, lanes] = (inv * (mod * units - (x * inv) * mean)).astype(BF).reshape(2, F, 256)
+        score = inv * (mod * units - (x * inv) * mean)
+        for p in range(2):
+            for i in range(2):
+                out_s[pl.ds(8 * p + 2 * j + i, F, stride=16), :] = score[64 * p:64 * p + 64, 128 * i:128 * i + 128]
+    score_ref[...] = out_s[...].astype(BF)
+
+
+def finish_kernel(score_ref, a_ref, b_ref, c_ref, o_ref, out_s):
+    out_s[:, 0:16] = score_ref[...].astype(F32).reshape(F, 16, 128)
+    total = (a_ref[...].astype(F32) + b_ref[64:128, :].astype(F32)) + c_ref[...].astype(F32)
+    for j in range(8):
+        out_s[8 * j:8 * j + 8, 16:24] = total[:, 128 * j:128 * j + 128].reshape(8, 8, 128)
+    o_ref[...] = out_s[...].reshape(F * 24, 128).astype(BF)
 
 
 def body(latent, direction, concept, timestep, concept_table, w_query, w_key):
@@ -285,59 +344,71 @@
     vmem = pltpu.VMEM
 
     sent, = local_call(
-        pack_kernel, (latent.reshape(2 * F, W), direction.reshape(2 * F, W), concept.reshape(1, 1)),
-        (((F * STEP, 128), BF),), (vmem((4 * F * 8, 128), F32), vmem((F * STEP, 128), F32)), 60, "pack")
+        pack_kernel, (latent.reshape(2 * F, W), direction.reshape(2 * F, W), concept),
+        (((F, 9, 4, 128), BF),), (vmem((4 * F * 8, 128), F32), vmem((F * STEP, 128), F32)), 60, "pack", smem=1)
     got = lax.all_to_all(sent, "seq", split_axis=0, concat_axis=0, tiled=True)
 
+    hbm = pl.BlockSpec(memory_space=pltpu.HBM)
+    turned, token = pl.pallas_call(
+        turn_kernel,
+        out_shape=(jax.ShapeDtypeStruct((4, W, W), BF), jax.ShapeDtypeStruct((8, 128), F32)),
+        in_specs=[hbm, hbm],
+        out_specs=(hbm, pl.BlockSpec(memory_space=pltpu.VMEM)),
+        scratch_shapes=[vmem((4, W, W), BF), vmem((4, W, W), BF),
+                        pltpu.SemaphoreType.DMA((8,)), pltpu.SemaphoreType.DMA((4,))],
+        compiler_params=pltpu.CompilerParams(vmem_limit_bytes=24 * 1024 * 1024),
+        cost_estimate=pl.CostEstimate(flops=1 << 33, bytes_accessed=1 << 24, transcendentals=0),
+        name="turn",
+    )(pltpu.with_memory_space_constraint(w_query, pltpu.HBM), pltpu.with_memory_space_constraint(w_key, pltpu.HBM))
     t_core = swap_core(concept_table)
     t_chip = swap_chip(concept_table)
     t_both = swap_core(t_chip)
 
     half = ((2, F, W), BF)
     x0, d0, ids = local_call(
-        unpack_kernel, (got,), (half, half, ((F, 2 * W), BF)), (vmem((F * STEP, 128), F32),), 8, "unpack")
+        unpack_kernel, (token, got), (half, half, ((F, 2 * W), BF)), (vmem((F * STEP, 128), F32),), 8, "unpack")
 
     steps = ((0.25 + 1.75 * timestep.astype(F32) / STEPS) / math.sqrt(HD)).reshape(F, 1)
-    mod, ids_late, temp = local_call(
-        mod_kernel, (concept_table, t_core, t_chip, t_both, ids, steps),
-        (((4, F, W), F32), ((F, 128), F32), ((F, 128), F32)), (), 8, "mod", 1 << 30)
-    relay = lambda *v: local_call(relay_kernel, v, (half,), (), 4, "relay")[0]
+    weights, mod = local_call(
+        prepare_kernel, (w_query, w_key, concept_table, t_core, t_chip, t_both, ids, steps),
+        (((4, W, W), BF), ((5, F, W), F32)), (vmem((CONCEPTS, W), BF), pltpu.SemaphoreType.DMA((9,))), 12, "prepare", 1 << 32, hbm=3)
+    full = ((4, F, W), BF)
+    join = lambda *v: local_call(join_kernel, v, (full,), (), 4, "join")[0]
     x2 = swap_chip(x0)
-    x1 = swap_core(x0)
-    x3 = swap_core(x2)
-    d1 = swap_core(d0)
-    d2 = swap_chip(relay(x3, mod, d0))
+    xn = swap_core(join(mod, x0, x2))
+    d_out, = local_call(relay_kernel, (x2, d0), (half,), (), 4, "relay")
+    d2 = swap_chip(d_out)
 
     units, terms = ((144, W), BF), ((F, W), BF)
-    u0, u1, u2, u3, qk, soft, stat, weights = local_call(
-        latent_kernel, (w_query, w_key, x0, x1, x2, x3, mod, temp),
-        (units,) * 4
-        + (((2 * F, W), BF), ((8 * F, F), F32), ((2 * F, 128), F32), ((4, W, W), BF)),
-        (vmem((4, 2 * F, W), BF), vmem((2 * F, W), BF), pltpu.SemaphoreType.DMA((8,))), 20, "latents", 1 << 30, hbm=2)
-    d3 = swap_core(relay(stat, d2))
-    far = swap_core(u3)
-    summed, = local_call(merge_kernel, (u2, far), (units,), (), 4, "merge")
+    u0, u1, u2, u3_low, u3_high, qk, soft, stat, back_w = local_call(
+        latent_kernel, (turned, x0, x2, xn, mod, d_out, weights),
+        (units,) * 3
+        + (terms, ((80, W), BF), ((2 * F, W), BF), ((8 * F, F), F32), ((2 * F, 128), F32), ((4, W, W), BF)),
+        (vmem((4, 2 * F, W), BF), vmem((2 * F, W), BF), vmem((144, W), BF), pltpu.SemaphoreType.DMA((4,))),
+        16, "latents", 1 << 30, hbm=1)
+    low, high = swap_core(u3_low), swap_core(u3_high)
+    summed, = local_call(merge_kernel, (u2, low, high), (units,), (), 4, "merge")
     arrived = swap_chip(summed)
+    dn = swap_core(join(summed, d0, d2))
     beside = swap_core(u1)
 
-    v0, v1, v2, v3 = local_call(
+    v0, v2, v_send, ids_late = local_call(
         tangent_kernel,
-        (x0, x1, x2, x3, d0, d1, d2, d3, u0, u1, u2, u3, mod, stat, qk, soft, temp, summed, weights), (terms,) * 4,
+        (x0, x2, xn, d0, d2, dn, u0, u1, u2, u3_low, u3_high, mod, stat, qk, soft, summed, weights, back_w),
+        (terms, terms, ((2 * F, W), BF), ((F, 128), F32)),
         (vmem((4, 2 * F, W), BF), vmem((2 * F, W), BF), vmem((2 * F, W), BF), vmem((4, 2 * F, W), F32),
          vmem((4, F, W), BF)), 20, "tangent", 1 << 34)
-    score, = local_call(score_kernel, (u0, beside, arrived, x0, mod, stat), (half,), (), 4, "score")
-    v_far = swap_core(v3)
-    v_sum, = local_call(add_kernel, (score, v2, v_far), (terms,), (), 4, "add")
+    score, = local_call(
+        score_kernel, (u0, beside, arrived, x0, mod, stat), (((F * 16, 128), BF),), (vmem((F * 16, 128), F32),), 6, "score")
+    v_got = swap_core(v_send)
+    v_sum, = local_call(add_kernel, (score, v2, v_got), (terms,), (), 4, "add")
     v_chip = swap_chip(v_sum)
-    v_near = swap_core(v1)
-    total = (v0.astype(F32) + v_near.astype(F32) + v_chip.astype(F32)).astype(BF)
-
-    score_rows = jnp.transpose(score, (1, 0, 2)).reshape(F, 16, 128)
-    term_rows = jnp.transpose(total.reshape(8, 8, 8, 128), (2, 0, 1, 3)).reshape(F, 8, 128)
-    back = lax.all_to_all(
-        jnp.concatenate([score_rows, term_rows], axis=1), "seq", split_axis=0, concat_axis=0, tiled=True)
+
+    ready, = local_call(
+        finish_kernel, (score, v0, v_got, v_chip), (((F * 24, 128), BF),), (vmem((F, 24, 128), F32),), 6, "finish")
+    back = lax.all_to_all(ready, "seq", split_axis=0, concat_axis=0, tiled=True)
     score_field, table = local_call(
-        tail_kernel, (back.reshape(F * 24, 128), ids_late), (((2 * F, W), BF), ((16, CONCEPTS), F32)),
+        tail_kernel, (back, ids_late), (((2 * F, W), BF), ((16, CONCEPTS), F32)),
         (vmem((F * 24, 128), F32), vmem((2 * F * 8, 128), F32)), 8, "tail")
     return (score_field.reshape(1, 2 * F, W), table.T)
 

time: 99.8 us -> 94.4 us (0.946)
  waiting for transfers between devices: 30.5 us -> 24.8 us
  Pallas kernels: 17.2 us -> 21 us
  starting transfers between devices: 20.8 us -> 18 us
    ppermute x5, waiting for transfers between devices: 23.2 us -> 11.7 us  [body(): swap_chip = lambda v: lax.ppermute(v, ('seq', 'tp'), cross)]
    pallas_call x0 -> x1, Pallas kernels: none -> 4.87 us  [body(): pl.pallas_call(turn_kernel, out_shape=(jax.ShapeDtypeStruct((4, W, W), BF...]
    ppermute x5, starting transfers between devices: 6.03 us -> 2.51 us  [body(): swap_chip = lambda v: lax.ppermute(v, ('seq', 'tp'), cross)]
    ppermute x10 -> x8, waiting for transfers between devices: 0.66 us -> 4.01 us  [body(): swap_core = lambda v: lax.ppermute(v, 'tp', core)]
    all_to_all x1, waiting for transfers between devices: 6.6 us -> 9.1 us  [body(): got = lax.all_to_all(sent, 'seq', split_axis=0, concat_axis=0, tiled=True)]
    pallas_call x11 -> x13, Pallas kernels: 17.2 us -> 16.2 us  [local_call(): pl.pallas_call(kernel, out_shape=tuple((jax.ShapeDtypeStruct(s, t) for s,...]
    unnamed x6 -> x2, local copies, waits for them, and re-layouts: 2.68 us -> 3.24 us
    ppermute x10 -> x8, starting transfers between devices: 1.8 us -> 2.17 us  [body(): swap_core = lambda v: lax.ppermute(v, 'tp', core)]
  transfers between devices with their start and end apart: 16 -> 14, of which waited for: 7 -> 8; matrix products, arithmetic and copies ran while one was open for 1% -> 1% of each run, Pallas kernels for 14% -> 21%
where the time goes in v3:
time: 94.4 us; the launch traced here: 94.2 us
  waiting for transfers between devices  24.8 us (26%)
  blocking collectives  24.8 us (26%)
  Pallas kernels  21 us (22%)
  starting transfers between devices  18 us (19%)
  local copies, waits for them, and re-layouts  3.34 us (4%)
  between operations  1.45 us (2%)
    all_to_all x1, blocking collectives, body(): back = lax.all_to_all(ready, 'seq', split_axis=0, concat_axis=0, tiled=True)  24.8 us
    pallas_call x13, Pallas kernels, local_call(): pl.pallas_call(kernel, out_shape=tuple((jax.ShapeDtypeStruct(s, t) for s,...  16.2 us
    all_to_all x1, starting transfers between devices, body(): got = lax.all_to_all(sent, 'seq', split_axis=0, concat_axis=0, tiled=True)  13.4 us
    ppermute x5, waiting for transfers between devices, body(): swap_chip = lambda v: lax.ppermute(v, ('seq', 'tp'), cross)  11.7 us
    all_to_all x1, waiting for transfers between devices, body(): got = lax.all_to_all(sent, 'seq', split_axis=0, concat_axis=0, tiled=True)  9.1 us
    pallas_call x1, Pallas kernels, body(): pl.pallas_call(turn_kernel, out_shape=(jax.ShapeDtypeStruct((4, W, W), BF...  4.87 us
    ppermute x8, waiting for transfers between devices, body(): swap_core = lambda v: lax.ppermute(v, 'tp', core)  4.01 us
    unnamed x2, local copies, waits for them, and re-layouts  3.24 us
  transfers between devices with their start and end apart: 14, of which 8 were waited for; matrix products, arithmetic and copies ran while one was open for 1% of the time, Pallas kernels for 21%

profile of v3, /device:TPU:8, one launch (start us, length us, event | category | flops | bytes accessed | tf_op | source)
XLA Modules:
  0.0 94.2 jit_solution(2590200628460363115)
XLA Ops:
  0.6 1.7 %collective-permute-start.2 = (bf16[256,1024]{1,0:T(8,128)(2,1)}, bf16[256,1024]{1,0:T(8,128)(2,1)S(1)}, u32[]{:S(2)}, u32[]{:S(2)}) collective-permute-start(bf16[256,1024]{1,0:T(8,128)(2,1)} %table_ref.1), channel_id=1, source_target_pairs={{0,18},{1,19},{2,16},{3,17},{4,22},{5,23},{6,20},{7,21},{8,26},{9,... | collective-permute-start | bytes 1572872 | tf_op jit(solution)/shard_map/ppermute | solution.py:343
  2.9 2.4 %pack.1 = bf16[64,9,4,128]{3,2,1,0:T(4,128)(2,1)} custom-call(bf16[128,1024]{1,0:T(8,128)(2,1)} %bitcast.10, bf16[128,1024]{1,0:T(8,128)(2,1)} %bitcast.11, s32[1]{0:T(128)S(6)} %copy.10.ids_ref), custom_call_target="tpu_custom_call" | custom-call | flops 1048576 | bytes 1048576 | tf_op jit(solution)/shard_map/pack/pallas_call | solution.py:284
  5.3 13.4 %all-to-all-start = ((bf16[64,9,4,128]{3,2,1,0:T(4,128)(2,1)}), bf16[64,9,4,128]{3,2,1,0:T(4,128)(2,1)S(1)}, u32[]{:S(2)}, u32[]{:S(2)}) async-start(bf16[64,9,4,128]{3,2,1,0:T(4,128)(2,1)} %pack.1), calls=%async_computation | async-start | bytes 1179648 | tf_op jit(solution)/shard_map/all_to_all | solution.py:349
  18.7 0.1 collective-permute-start.1
  18.8 0.7 multiply_bitcast_fusion
  19.4 0.1 copy.9.steps_ref
  19.5 0.0 collective-permute-done.2.t2
  19.6 0.6 collective-permute-start.3
  20.1 4.9 %turn.1 = (bf16[4,1024,1024]{2,1,0:T(8,128)(2,1)S(1)}, f32[8,128]{1,0:T(8,128)S(1)}) custom-call(bf16[4096,512]{1,0:T(8,128)(2,1)} %wq_ref.3, bf16[4096,512]{1,0:T(8,128)(2,1)} %wk_ref.3), custom_call_target="tpu_custom_call" | custom-call | flops 8589934592 | bytes 16777216 | tf_op jit(solution)/shard_map/turn/pallas_call | solution.py:352
  25.0 0.0 copy-start
  25.0 3.2 %copy-done = bf16[4,1024,1024]{2,1,0:T(8,128)(2,1)} copy-done((bf16[4,1024,1024]{2,1,0:T(8,128)(2,1)}, bf16[4,1024,1024]{2,1,0:T(8,128)(2,1)S(1)}, u32[]{:S(2)}) %copy-start) | copy-done | bytes 8388632
  28.2 9.1 %all-to-all-done.g_ref = bf16[64,9,4,128]{3,2,1,0:T(4,128)(2,1)S(1)} async-done(((bf16[64,9,4,128]{3,2,1,0:T(4,128)(2,1)}), bf16[64,9,4,128]{3,2,1,0:T(4,128)(2,1)S(1)}, u32[]{:S(2)}, u32[]{:S(2)}) %all-to-all-start) | async-done | bytes 589856 | tf_op jit(solution)/shard_map/all_to_all | solution.py:349
  37.4 0.4 unpack.1
  37.7 0.1 collective-permute-start
  37.8 0.0 collective-permute-done.1.t1
  37.8 0.0 collective-permute-done.3.t3
  37.8 3.8 %prepare.1 = (bf16[4,1024,1024]{2,1,0:T(8,128)(2,1)S(1)}, f32[5,64,1024]{2,1,0:T(8,128)S(1)}) custom-call(bf16[4096,512]{1,0:T(8,128)(2,1)} %wq_ref.3, bf16[4096,512]{1,0:T(8,128)(2,1)} %wk_ref.3, bf16[256,1024]{1,0:T(8,128)(2,1)} %table_ref.1, bf16[256,1024]{1,0:T(8,128)(2,1)S(1)} %collective-permute-done.1.t1, ...), custom_call_target="tpu_custom_call" | custom-call | flops 4294967296 | bytes 1048576 | tf_op jit(solution)/shard_map/prepare/pallas_call | solution.py:284
  41.7 2.5 %collective-permute-done.b_ref._.x2 = bf16[2,64,1024]{2,1,0:T(8,128)(2,1)S(1)} collective-permute-done((bf16[2,64,1024]{2,1,0:T(8,128)(2,1)S(1)}, bf16[2,64,1024]{2,1,0:T(8,128)(2,1)S(1)}, u32[]{:S(2)}, u32[]{:S(2)}) %collective-permute-start) | collective-permute-done | bytes 262176 | tf_op jit(solution)/shard_map/ppermute | solution.py:343
  44.2 0.1 collective-permute-start.4
  44.3 0.1 collective-permute-start.9
  44.4 1.8 %collective-permute-done.4.xn = bf16[4,64,1024]{2,1,0:T(8,128)(2,1)S(1)} collective-permute-done((bf16[4,64,1024]{2,1,0:T(8,128)(2,1)S(1)}, bf16[4,64,1024]{2,1,0:T(8,128)(2,1)S(1)}, u32[]{:S(2)}, u32[]{:S(2)}) %collective-permute-start.4) | collective-permute-done | bytes 524320 | tf_op jit(solution)/shard_map/ppermute | solution.py:342
  46.2 4.2 %latents.1 = (bf16[144,1024]{1,0:T(8,128)(2,1)S(1)}, bf16[144,1024]{1,0:T(8,128)(2,1)S(1)}, bf16[144,1024]{1,0:T(8,128)(2,1)S(1)}, bf16[64,1024]{1,0:T(8,128)(2,...) custom-call(bf16[4,1024,1024]{2,1,0:T(8,128)(2,1)} %copy-done, ...), custom_call_target="tpu_custom_call" | custom-call | flops 1073741824 | bytes 1048576 | tf_op jit(solution)/shard_map/latents/pallas_call | solution.py:284
  50.4 0.2 collective-permute-start.7
  50.6 0.4 collective-permute-start.6
  51.0 1.1 %collective-permute-done.6.low_ref = bf16[64,1024]{1,0:T(8,128)(2,1)S(1)} collective-permute-done((bf16[64,1024]{1,0:T(8,128)(2,1)S(1)}, bf16[64,1024]{1,0:T(8,128)(2,1)S(1)}, u32[]{:S(2)}, u32[]{:S(2)}) %collective-permute-start.6) | collective-permute-done | bytes 131104 | tf_op jit(solution)/shard_map/ppermute | solution.py:342
  52.1 0.0 collective-permute-done.7.high_ref
  52.1 0.1 merge.1._
  52.2 0.9 collective-permute-done.9.b_ref.d2
  53.2 0.1 collective-permute-start.10
  53.3 0.5 collective-permute-start.5
  53.8 0.3 collective-permute-start.8
  54.1 1.1 %collective-permute-done.10.dn = bf16[4,64,1024]{2,1,0:T(8,128)(2,1)S(1)} collective-permute-done((bf16[4,64,1024]{2,1,0:T(8,128)(2,1)S(1)}, bf16[4,64,1024]{2,1,0:T(8,128)(2,1)S(1)}, u32[]{:S(2)}, u32[]{:S(2)}) %collective-permute-start.10) | collective-permute-done | bytes 524320 | tf_op jit(solution)/shard_map/ppermute | solution.py:342
  55.2 3.8 %tangent.1 = (bf16[64,1024]{1,0:T(8,128)(2,1)S(1)}, bf16[64,1024]{1,0:T(8,128)(2,1)S(1)}, bf16[128,1024]{1,0:T(8,128)(2,1)S(1)}, f32[64,128]{1,0:T(8,128)S(1)}) custom-call(bf16[2,64,1024]{2,1,0:T(8,128)(2,1)S(1)} %get-tuple-element.26.a_ref.x0.x_ref, bf16[2,64,1024]{2,1,0:T(8,128)(2,1)S(1)} %collective-permute-done.b_ref._.x2, ...), custom_call_target="tpu_custom_call" | custom-call | flops 17179869184 | bytes 1048576 | tf_op jit(solution)/shard_map/tangent/pallas_call | solution.py:284
  59.0 0.2 collective-permute-start.11
  59.2 0.0 collective-permute-done.5.b_ref
  59.2 3.6 %collective-permute-done.8.c_ref = bf16[144,1024]{1,0:T(8,128)(2,1)S(1)} collective-permute-done((bf16[144,1024]{1,0:T(8,128)(2,1)S(1)}, bf16[144,1024]{1,0:T(8,128)(2,1)S(1)}, u32[]{:S(2)}, u32[]{:S(2)}) %collective-permute-start.8) | collective-permute-done | bytes 294944 | tf_op jit(solution)/shard_map/ppermute | solution.py:343
  62.8 0.4 score.1._.score_ref
  63.1 0.0 collective-permute-done.11.b_ref
  63.2 0.4 collective-permute-start.12
  63.6 4.7 %collective-permute-done.12.c_ref = bf16[64,1024]{1,0:T(8,128)(2,1)S(1)} collective-permute-done((bf16[64,1024]{1,0:T(8,128)(2,1)S(1)}, bf16[64,1024]{1,0:T(8,128)(2,1)S(1)}, u32[]{:S(2)}, u32[]{:S(2)}) %collective-permute-start.12) | collective-permute-done | bytes 131104 | tf_op jit(solution)/shard_map/ppermute | solution.py:343
  68.2 0.1 finish.1
  68.3 24.8 %all_to_all.16 = bf16[64,24,128]{2,1,0:T(8,128)(2,1)S(1)} all-to-all(bf16[64,24,128]{2,1,0:T(8,128)(2,1)S(1)} %bitcast.9), channel_id=1, replica_groups=mesh['seq'=64,'tp'=4] {'seq'}, dimensions={0} | all-to-all | bytes 786432 | tf_op jit(solution)/shard_map/all_to_all | solution.py:409
  93.2 1.0 %tail.1 = (bf16[128,1024]{1,0:T(8,128)(2,1)}, f32[16,256]{1,0:T(8,128)}) custom-call(bf16[1536,128]{1,0:T(8,128)(2,1)S(1)} %bitcast.8, f32[64,128]{1,0:T(8,128)S(1)} %get-tuple-element.43.ids_ref), custom_call_target="tpu_custom_call" | custom-call | flops 1048576 | bytes 1048576 | tf_op jit(solution)/shard_map/tail/pallas_call | solution.py:284
  (4 shorter events, 0.1 us)
Async XLA Ops:
  0.6 18.9 %collective-permute-start.2 = (bf16[256,1024]{1,0:T(8,128)(2,1)}, bf16[256,1024]{1,0:T(8,128)(2,1)S(1)}, u32[]{:S(2)}, u32[]{:S(2)}) collective-permute-start(bf16[256,1024]{1,0:T(8,128)(2,1)} %table_ref.1), channel_id=1, source_target_pairs={{0,18},{1,19},{2,16},{3,17},{4,22},{5,23},{6,20},{7,21},{8,26},{9,... | collective-permute-start | bytes 1572872 | tf_op jit(solution)/shard_map/ppermute | solution.py:343
  5.3 32.0 %all-to-all-start = ((bf16[64,9,4,128]{3,2,1,0:T(4,128)(2,1)}), bf16[64,9,4,128]{3,2,1,0:T(4,128)(2,1)S(1)}, u32[]{:S(2)}, u32[]{:S(2)}) async-start(bf16[64,9,4,128]{3,2,1,0:T(4,128)(2,1)} %pack.1), calls=%async_computation | async-start | bytes 1179648 | tf_op jit(solution)/shard_map/all_to_all | solution.py:349
  18.7 19.1 %collective-permute-start.1 = (bf16[256,1024]{1,0:T(8,128)(2,1)}, bf16[256,1024]{1,0:T(8,128)(2,1)S(1)}, u32[]{:S(2)}, u32[]{:S(2)}) collective-permute-start(bf16[256,1024]{1,0:T(8,128)(2,1)} %table_ref.1), channel_id=1, source_target_pairs={{0,1},{1,0},{2,3},{3,2},{4,5},{5,4},{6,7},{7,6},{8,9},{9,8},{10,11... | collective-permute-start | bytes 1572872 | tf_op jit(solution)/shard_map/ppermute | solution.py:342
  19.6 18.3 %collective-permute-start.3 = (bf16[256,1024]{1,0:T(8,128)(2,1)S(1)}, bf16[256,1024]{1,0:T(8,128)(2,1)S(1)}, u32[]{:S(2)}, u32[]{:S(2)}) collective-permute-start(bf16[256,1024]{1,0:T(8,128)(2,1)S(1)} %collective-permute-done.2.t2), channel_id=1, source_target_pairs={{0,1},{1,0},{2,3},{3,2},{4,5},{5,4},{6,7},{7,6},{8,9},{9,8},{10,11... | collective-permute-start | bytes 1572872 | tf_op jit(solution)/shard_map/ppermute | solution.py:342
  25.0 3.2 %copy-start = (bf16[4,1024,1024]{2,1,0:T(8,128)(2,1)}, bf16[4,1024,1024]{2,1,0:T(8,128)(2,1)S(1)}, u32[]{:S(2)}) copy-start(bf16[4,1024,1024]{2,1,0:T(8,128)(2,1)S(1)} %get-tuple-element.24.turned_ref) | copy-start | bytes 25165828
  37.7 6.5 %collective-permute-start = (bf16[2,64,1024]{2,1,0:T(8,128)(2,1)S(1)}, bf16[2,64,1024]{2,1,0:T(8,128)(2,1)S(1)}, u32[]{:S(2)}, u32[]{:S(2)}) collective-permute-start(bf16[2,64,1024]{2,1,0:T(8,128)(2,1)S(1)} %get-tuple-element.26.a_ref.x0.x_ref), channel_id=1, source_target_pairs={{0,18},{1,19},{2,16},{3,17},{4,22},{5,23},{6,20},{7,21},{8,26},{9,... | collective-permute-start | bytes 786440 | tf_op jit(solution)/shard_map/ppermute | solution.py:343
  44.2 2.0 %collective-permute-start.4 = (bf16[4,64,1024]{2,1,0:T(8,128)(2,1)S(1)}, bf16[4,64,1024]{2,1,0:T(8,128)(2,1)S(1)}, u32[]{:S(2)}, u32[]{:S(2)}) collective-permute-start(bf16[4,64,1024]{2,1,0:T(8,128)(2,1)S(1)} %join.2), channel_id=1, source_target_pairs={{0,1},{1,0},{2,3},{3,2},{4,5},{5,4},{6,7},{7,6},{8,9},{9,8},{10,11... | collective-permute-start | bytes 1572872 | tf_op jit(solution)/shard_map/ppermute | solution.py:342
  44.3 8.8 %collective-permute-start.9 = (bf16[2,64,1024]{2,1,0:T(8,128)(2,1)S(1)}, bf16[2,64,1024]{2,1,0:T(8,128)(2,1)S(1)}, u32[]{:S(2)}, u32[]{:S(2)}) collective-permute-start(bf16[2,64,1024]{2,1,0:T(8,128)(2,1)S(1)} %relay.1._), channel_id=1, source_target_pairs={{0,18},{1,19},{2,16},{3,17},{4,22},{5,23},{6,20},{7,21},{8,26},{9,... | collective-permute-start | bytes 786440 | tf_op jit(solution)/shard_map/ppermute | solution.py:343
  50.4 1.7 %collective-permute-start.7 = (bf16[80,1024]{1,0:T(8,128)(2,1)S(1)}, bf16[80,1024]{1,0:T(8,128)(2,1)S(1)}, u32[]{:S(2)}, u32[]{:S(2)}) collective-permute-start(bf16[80,1024]{1,0:T(8,128)(2,1)S(1)} %get-tuple-element.35.u3_high), channel_id=1, source_target_pairs={{0,1},{1,0},{2,3},{3,2},{4,5},{5,4},{6,7},{7,6},{8,9},{9,8},{10,11... | collective-permute-start | bytes 491528 | tf_op jit(solution)/shard_map/ppermute | solution.py:342
  50.6 1.5 %collective-permute-start.6 = (bf16[64,1024]{1,0:T(8,128)(2,1)S(1)}, bf16[64,1024]{1,0:T(8,128)(2,1)S(1)}, u32[]{:S(2)}, u32[]{:S(2)}) collective-permute-start(bf16[64,1024]{1,0:T(8,128)(2,1)S(1)} %get-tuple-element.34.u3_low), channel_id=1, source_target_pairs={{0,1},{1,0},{2,3},{3,2},{4,5},{5,4},{6,7},{7,6},{8,9},{9,8},{10,11... | collective-permute-start | bytes 393224 | tf_op jit(solution)/shard_map/ppermute | solution.py:342
  53.2 2.0 %collective-permute-start.10 = (bf16[4,64,1024]{2,1,0:T(8,128)(2,1)S(1)}, bf16[4,64,1024]{2,1,0:T(8,128)(2,1)S(1)}, u32[]{:S(2)}, u32[]{:S(2)}) collective-permute-start(bf16[4,64,1024]{2,1,0:T(8,128)(2,1)S(1)} %join.3), channel_id=1, source_target_pairs={{0,1},{1,0},{2,3},{3,2},{4,5},{5,4},{6,7},{7,6},{8,9},{9,8},{10,11... | collective-permute-start | bytes 1572872 | tf_op jit(solution)/shard_map/ppermute | solution.py:342
  53.3 5.9 %collective-permute-start.5 = (bf16[144,1024]{1,0:T(8,128)(2,1)S(1)}, bf16[144,1024]{1,0:T(8,128)(2,1)S(1)}, u32[]{:S(2)}, u32[]{:S(2)}) collective-permute-start(bf16[144,1024]{1,0:T(8,128)(2,1)S(1)} %get-tuple-element.32.u1), channel_id=1, source_target_pairs={{0,1},{1,0},{2,3},{3,2},{4,5},{5,4},{6,7},{7,6},{8,9},{9,8},{10,11... | collective-permute-start | bytes 884744 | tf_op jit(solution)/shard_map/ppermute | solution.py:342
  53.8 9.0 %collective-permute-start.8 = (bf16[144,1024]{1,0:T(8,128)(2,1)S(1)}, bf16[144,1024]{1,0:T(8,128)(2,1)S(1)}, u32[]{:S(2)}, u32[]{:S(2)}) collective-permute-start(bf16[144,1024]{1,0:T(8,128)(2,1)S(1)} %merge.1._), channel_id=1, source_target_pairs={{0,18},{1,19},{2,16},{3,17},{4,22},{5,23},{6,20},{7,21},{8,26},{9,... | collective-permute-start | bytes 884744 | tf_op jit(solution)/shard_map/ppermute | solution.py:343
  59.0 4.2 %collective-permute-start.11 = (bf16[128,1024]{1,0:T(8,128)(2,1)S(1)}, bf16[128,1024]{1,0:T(8,128)(2,1)S(1)}, u32[]{:S(2)}, u32[]{:S(2)}) collective-permute-start(bf16[128,1024]{1,0:T(8,128)(2,1)S(1)} %get-tuple-element.41), channel_id=1, source_target_pairs={{0,1},{1,0},{2,3},{3,2},{4,5},{5,4},{6,7},{7,6},{8,9},{9,8},{10,11... | collective-permute-start | bytes 786440 | tf_op jit(solution)/shard_map/ppermute | solution.py:342
  63.2 5.1 %collective-permute-start.12 = (bf16[64,1024]{1,0:T(8,128)(2,1)S(1)}, bf16[64,1024]{1,0:T(8,128)(2,1)S(1)}, u32[]{:S(2)}, u32[]{:S(2)}) collective-permute-start(bf16[64,1024]{1,0:T(8,128)(2,1)S(1)} %add.11), channel_id=1, source_target_pairs={{0,18},{1,19},{2,16},{3,17},{4,22},{5,23},{6,20},{7,21},{8,26},{9,... | collective-permute-start | bytes 393224 | tf_op jit(solution)/shard_map/ppermute | solution.py:343

commit v4 on v3

--- a/solution.py
+++ b/solution.py
@@ -47,7 +47,7 @@
     token_ref[...] = jnp.zeros_like(token_ref)
 
 
-def prepare_kernel(wq_ref, wk_ref, table_ref, t1, t2, t3, ids_ref, steps_ref, w_ref, mod_ref, t0, sems):
+def prepare_kernel(wq_ref, wk_ref, turned_ref, table_ref, t1, t2, t3, ids_ref, steps_ref, w_ref, late_ref, mod_ref, t0, sems):
     me = lax.axis_index("tp")
     own = pltpu.make_async_copy(table_ref, t0, sems.at[8])
     own.start()
@@ -58,6 +58,10 @@
             copy = pltpu.make_async_copy(ref.at[rows], w_ref.at[k, :, pl.ds(512 * i, 512)], sems.at[2 * k + i])
             copy.start()
             copies.append(copy)
+    for k in range(2):
+        copy = pltpu.make_async_copy(turned_ref.at[2 + k], late_ref.at[k], sems.at[9 + k])
+        copy.start()
+        copies.append(copy)
     ids = ids_ref[:, 0:128].astype(F32)
     onehot = (ids[:, 0:1] == lax.broadcasted_iota(jnp.int32, (F, CONCEPTS), 1).astype(F32)).astype(BF)
     for k, ref in ((1, t1), (2, t2), (3, t3), (0, t0)):
@@ -83,18 +87,33 @@
     return [own.at[0:2], near.at[0:2], chip.at[0:2], near.at[2:4]]
 
 
-def pack_kernel(x_ref, d_ref, ids_ref, o_ref, in_s, out_s):
+def pack_kernel(x_ref, d_ref, concept_ref, o_ref, x_s, d_s, id_s, in_s, out_s, send_s, sems):
     y_hi = lax.axis_index("tp") >> 1
-    for j in range(8):
-        lanes = pl.ds(128 * j, 128)
-        in_s[256 * j:256 * j + 128] = x_ref[:, lanes].astype(F32)
-        in_s[256 * j + 128:256 * j + 256] = d_ref[:, lanes].astype(F32)
+    copies = [
+        pltpu.make_async_copy(src, dst, sems.at[i])
+        for i, (src, dst) in enumerate(((x_ref, x_s), (d_ref, d_s), (concept_ref, id_s)))]
+    for copy in copies:
+        copy.start()
+    for half, ref in enumerate((x_s, d_s)):
+        copies[half].wait()
+        for j in range(8):
+            in_s[256 * j + 128 * half:256 * j + 128 * half + 128] = ref[:, 128 * j:128 * j + 128].astype(F32)
+        for p in range(2):
+            for j in range(8):
+                rows = in_s[pl.ds(256 * j + 128 * half + p, F, stride=2), :]
+                out_s[pl.ds(j * 4 + 2 * half + p, F, stride=STEP), :] = flip_rows(rows, y_hi)
+    copies[2].wait()
     for q in range(4):
-        for j in range(8):
-            rows = in_s[pl.ds(256 * j + (q // 2) * 128 + q % 2, F, stride=2), :]
-            out_s[pl.ds(j * 4 + q, F, stride=STEP), :] = flip_rows(rows, y_hi)
-        out_s[pl.ds(32 + q, F, stride=STEP), :] = jnp.zeros((F, 128), F32) + ids_ref[0].astype(F32)
-    o_ref[...] = out_s[...].astype(BF).reshape(F, 9, 4, 128)
+        out_s[pl.ds(32 + q, F, stride=STEP), :] = jnp.zeros((F, 128), F32) + id_s[0].astype(F32)
+    outs = []
+    for i in range(4):
+        rows = pl.ds(16 * i, 16)
+        send_s[rows] = out_s[16 * STEP * i:16 * STEP * i + 16 * STEP].astype(BF).reshape(16, 9, 4, 128)
+        out = pltpu.make_async_copy(send_s.at[rows], o_ref.at[rows], sems.at[3 + i])
+        out.start()
+        outs.append(out)
+    for out in outs:
+        out.wait()
 
 
 def flip_rows(v, y_hi):
@@ -145,12 +164,9 @@
     return [(pl.ds(64 * p, 64), pl.ds(128 * h, 128), pl.ds(512 + 128 * h, 128)) for p in range(2) for h in range(4)]
 
 
-def latent_kernel(turned_ref, x0, x2, xn, mod_ref, _, w_ref,
-                  u0, u1, u2, u3_low, u3_high, qk_ref, soft_ref, stat_ref, back_ref, h_s, g_s, u3, sems):
-    xs, outs = slices(x0, x2, xn), (u0, u1, u2, u3)
-    copies = [pltpu.make_async_copy(turned_ref.at[k], back_ref.at[k], sems.at[k]) for k in range(4)]
-    for k in (3, 2, 1, 0):
-        copies[k].start()
+def latent_kernel(x0, x2, xn, mod_ref, _, w_ref, late_ref,
+                  u2, u3_low, u3_high, qk_ref, soft_ref, stat_ref, g_s, h_s, u3):
+    xs = slices(x0, x2, xn)
     sq = jnp.zeros((2 * F, 128), F32)
     for k in range(4):
         for j in range(8):
@@ -190,13 +206,12 @@
     hi = srow.astype(BF).astype(F32)
     sub = lax.broadcasted_iota(jnp.int32, (16, 128), 0)
     stats = jnp.where(sub == 0, hi, jnp.where(sub == 1, srow - hi, 0.0)).astype(BF)
-    for k in (3, 2, 1, 0):
-        copies[k].wait()
-        for j in range(4):
-            lanes = pl.ds(256 * j, 256)
-            outs[k][0:128, lanes] = jnp.dot(g_s[...], back_ref[k, :, lanes], preferred_element_type=F32).astype(BF)
-        outs[k][128:144, 0:128] = stats
-        outs[k][128:144, 128:1024] = jnp.zeros((16, 896), BF)
+    for ref, k in ((u3, 1), (u2, 0)):
+        for j in range(4):
+            lanes = pl.ds(256 * j, 256)
+            ref[0:128, lanes] = jnp.dot(g_s[...], late_ref[k, :, lanes], preferred_element_type=F32).astype(BF)
+        ref[128:144, 0:128] = stats
+        ref[128:144, 128:1024] = jnp.zeros((16, 896), BF)
     u3_low[...] = u3[0:64, :]
     u3_high[...] = u3[64:144, :]
 
@@ -207,8 +222,8 @@
     return n, inv * (d - n * mean)
 
 
-def tangent_kernel(x0, x2, xn, d0, d2, dn, u0, u1, u2, u3_low, u3_high, mod_ref, stat_ref, qk_ref, soft_ref, _, w_ref, back_ref,
-                   o0, o2, near_ref, ids_ref, h_s, tan_s, g_s, drift_s, term_s):
+def tangent_kernel(x0, x2, xn, d0, d2, dn, u0, u1, u2, u3_low, u3_high, mod_ref, stat_ref, qk_ref, soft_ref,
+                   w_ref, back_ref, late_ref, o0, o1, o2, o3, ids_ref, h_s, tan_s, g_s, drift_s, term_s):
     xs, ds = slices(x0, x2, xn), slices(d0, d2, dn)
     me = lax.axis_index("tp")
     ids_ref[...] = mod_ref[4, :, 0:128]
@@ -248,9 +263,11 @@
         g_s[r, kl] = (-aks[i]).astype(BF)
 
     for k in range(4):
-        for j in range(4):
-            lanes = pl.ds(256 * j, 256)
-            drift_s[k, :, lanes] = jnp.dot(g_s[...], back_ref[k, :, lanes], preferred_element_type=F32)
+        source = back_ref if k < 2 else late_ref
+        for j in range(4):
+            lanes = pl.ds(256 * j, 256)
+            drift_s[k, :, lanes] = jnp.dot(g_s[...], source[k % 2, :, lanes], preferred_element_type=F32)
+
     rr = lax.broadcasted_iota(jnp.int32, (128, 256), 0)
     cc = lax.broadcasted_iota(jnp.int32, (128, 256), 1)
     pick = (((rr >> 3) & 3) == (cc >> 6)) & ((rr >> 5) == ((cc >> 4) & 3)) & ((rr & 7) == (cc & 7))
@@ -274,47 +291,60 @@
                 term_s[t, low:low + 32, spot] = moved[32 * t:32 * t + 32]
     o0[...] = term_s[me]
     o2[...] = term_s[me ^ 2]
-    near_ref[0:64, :] = term_s[me ^ 3]
-    near_ref[64:128, :] = term_s[me ^ 1]
-
-
-def local_call(kernel, args, outs, scratch, limit, name, flops=1 << 20, hbm=0, smem=0):
+    o3[...] = term_s[me ^ 3]
+    o1[...] = term_s[me ^ 1]
+
+
+def local_call(kernel, args, outs, scratch, limit, name, flops=1 << 12, hbm=0):
     vm = pl.BlockSpec(memory_space=pltpu.VMEM)
     args = [pltpu.with_memory_space_constraint(v, pltpu.HBM) if i < hbm else v for i, v in enumerate(args)]
     return pl.pallas_call(
         kernel,
         out_shape=tuple(jax.ShapeDtypeStruct(s, t) for s, t in outs),
-        in_specs=[pl.BlockSpec(memory_space=pltpu.HBM)] * hbm + [vm] * (len(args) - hbm - smem)
-        + [pl.BlockSpec(memory_space=pltpu.SMEM)] * smem,
+        in_specs=[pl.BlockSpec(memory_space=pltpu.HBM)] * hbm + [vm] * (len(args) - hbm),
         out_specs=tuple(vm for _ in outs),
         scratch_shapes=scratch,
         compiler_params=pltpu.CompilerParams(vmem_limit_bytes=limit * 1024 * 1024),
-        cost_estimate=pl.CostEstimate(flops=flops, bytes_accessed=1 << 20, transcendentals=0),
+        cost_estimate=pl.CostEstimate(flops=flops, bytes_accessed=1 << 12, transcendentals=0),
         name=name,
     )(*args)
 
 
 def add_kernel(_, a_ref, b_ref, o_ref):
-    o_ref[...] = (a_ref[...].astype(F32) + b_ref[0:64, :].astype(F32)).astype(BF)
-
-
-def merge_kernel(a_ref, low_ref, high_ref, o_ref):
-    o_ref[0:64, :] = (a_ref[0:64, :].astype(F32) + low_ref[...].astype(F32)).astype(BF)
-    o_ref[64:128, :] = (a_ref[64:128, :].astype(F32) + high_ref[0:64, :].astype(F32)).astype(BF)
-    o_ref[128:144, :] = jnp.concatenate(
+    o_ref[...] = (a_ref[...].astype(F32) + b_ref[...].astype(F32)).astype(BF)
+
+
+def merge_kernel(a_ref, low_ref, high_ref, first_ref, rest_ref):
+    first_ref[...] = (a_ref[0:32, :].astype(F32) + low_ref[0:32, :].astype(F32)).astype(BF)
+    rest_ref[0:32, :] = (a_ref[32:64, :].astype(F32) + low_ref[32:64, :].astype(F32)).astype(BF)
+    rest_ref[32:96, :] = (a_ref[64:128, :].astype(F32) + high_ref[0:64, :].astype(F32)).astype(BF)
+    rest_ref[96:112, :] = jnp.concatenate(
         [a_ref[128:144, 0:128], high_ref[64:80, 0:128], a_ref[128:144, 256:1024]], axis=1)
 
 
-def score_kernel(a_ref, b_ref, c_ref, x_ref, mod_ref, stat_ref, score_ref, out_s):
+def others_kernel(turned_ref, _, grad_ref, u2, back_ref, u0, u1, sems):
+    copies = [pltpu.make_async_copy(turned_ref.at[k], back_ref.at[k], sems.at[k]) for k in range(2)]
+    for copy in copies:
+        copy.start()
+    for k, ref in enumerate((u0, u1)):
+        copies[k].wait()
+        for j in range(4):
+            lanes = pl.ds(256 * j, 256)
+            ref[0:128, lanes] = jnp.dot(grad_ref[...], back_ref[k, :, lanes], preferred_element_type=F32).astype(BF)
+        ref[128:144, :] = u2[128:144, :]
+
+
+def score_kernel(a_ref, b_ref, first_ref, rest_ref, x_ref, mod_ref, stat_ref, score_ref, out_s):
     srow = jnp.zeros((1, 128), F32)
-    for ref, lane in ((a_ref, 0), (b_ref, 0), (c_ref, 0), (c_ref, 128)):
-        part = ref[128:144, lane:lane + 128].astype(F32)
+    for ref, row, lane in ((a_ref, 128, 0), (b_ref, 128, 0), (rest_ref, 96, 0), (rest_ref, 96, 128)):
+        part = ref[row:row + 16, lane:lane + 128].astype(F32)
         srow = srow + (part[0:1] + part[1:2])
     mean = jnp.sum(jnp.where(eye128(), srow, 0.0), axis=1, keepdims=True) / D
     inv = jnp.sum(stat_ref[...], axis=1, keepdims=True)
     for j in range(4):
         lanes = pl.ds(256 * j, 256)
-        units = (a_ref[0:128, lanes].astype(F32) + b_ref[0:128, lanes].astype(F32)) + c_ref[0:128, lanes].astype(F32)
+        far = jnp.concatenate([first_ref[:, lanes], rest_ref[0:96, lanes]], axis=0).astype(F32)
+        units = (a_ref[0:128, lanes].astype(F32) + b_ref[0:128, lanes].astype(F32)) + far
         mod = mod_ref[0, :, lanes]
         mod = jnp.concatenate([mod, mod], axis=0)
         x = x_ref[:, :, lanes].astype(F32).reshape(2 * F, 256)
@@ -327,7 +357,7 @@
 
 def finish_kernel(score_ref, a_ref, b_ref, c_ref, o_ref, out_s):
     out_s[:, 0:16] = score_ref[...].astype(F32).reshape(F, 16, 128)
-    total = (a_ref[...].astype(F32) + b_ref[64:128, :].astype(F32)) + c_ref[...].astype(F32)
+    total = (a_ref[...].astype(F32) + b_ref[...].astype(F32)) + c_ref[...].astype(F32)
     for j in range(8):
         out_s[8 * j:8 * j + 8, 16:24] = total[:, 128 * j:128 * j + 128].reshape(8, 8, 128)
     o_ref[...] = out_s[...].reshape(F * 24, 128).astype(BF)
@@ -343,12 +373,20 @@
     swap_chip = lambda v: lax.ppermute(v, ("seq", "tp"), cross)
     vmem = pltpu.VMEM
 
-    sent, = local_call(
-        pack_kernel, (latent.reshape(2 * F, W), direction.reshape(2 * F, W), concept),
-        (((F, 9, 4, 128), BF),), (vmem((4 * F * 8, 128), F32), vmem((F * STEP, 128), F32)), 60, "pack", smem=1)
+    hbm = pl.BlockSpec(memory_space=pltpu.HBM)
+    sent = pl.pallas_call(
+        pack_kernel,
+        out_shape=jax.ShapeDtypeStruct((F, 9, 4, 128), BF),
+        in_specs=[hbm, hbm, pl.BlockSpec(memory_space=pl.ANY)],
+        out_specs=hbm,
+        scratch_shapes=[
+            vmem((2 * F, W), BF), vmem((2 * F, W), BF), pltpu.SMEM((1,), jnp.int32), vmem((4 * F * 8, 128), F32),
+            vmem((F * STEP, 128), F32), vmem((F, 9, 4, 128), BF), pltpu.SemaphoreType.DMA((7,))],
+        compiler_params=pltpu.CompilerParams(vmem_limit_bytes=8 * 1024 * 1024),
+        name="pack",
+    )(*[pltpu.with_memory_space_constraint(v.reshape(2 * F, W), pltpu.HBM) for v in (latent, direction)], concept)
     got = lax.all_to_all(sent, "seq", split_axis=0, concat_axis=0, tiled=True)
 
-    hbm = pl.BlockSpec(memory_space=pltpu.HBM)
     turned, token = pl.pallas_call(
         turn_kernel,
         out_shape=(jax.ShapeDtypeStruct((4, W, W), BF), jax.ShapeDtypeStruct((8, 128), F32)),
@@ -369,9 +407,10 @@
         unpack_kernel, (token, got), (half, half, ((F, 2 * W), BF)), (vmem((F * STEP, 128), F32),), 8, "unpack")
 
     steps = ((0.25 + 1.75 * timestep.astype(F32) / STEPS) / math.sqrt(HD)).reshape(F, 1)
-    weights, mod = local_call(
-        prepare_kernel, (w_query, w_key, concept_table, t_core, t_chip, t_both, ids, steps),
-        (((4, W, W), BF), ((5, F, W), F32)), (vmem((CONCEPTS, W), BF), pltpu.SemaphoreType.DMA((9,))), 12, "prepare", 1 << 32, hbm=3)
+    weights, back_late, mod = local_call(
+        prepare_kernel, (w_query, w_key, turned, concept_table, t_core, t_chip, t_both, ids, steps),
+        (((4, W, W), BF), ((2, W, W), BF), ((5, F, W), F32)),
+        (vmem((CONCEPTS, W), BF), pltpu.SemaphoreType.DMA((11,))), 16, "prepare", 1 << 32, hbm=4)
     full = ((4, F, W), BF)
     join = lambda *v: local_call(join_kernel, v, (full,), (), 4, "join")[0]
     x2 = swap_chip(x0)
@@ -380,32 +419,35 @@
     d2 = swap_chip(d_out)
 
     units, terms = ((144, W), BF), ((F, W), BF)
-    u0, u1, u2, u3_low, u3_high, qk, soft, stat, back_w = local_call(
-        latent_kernel, (turned, x0, x2, xn, mod, d_out, weights),
-        (units,) * 3
-        + (terms, ((80, W), BF), ((2 * F, W), BF), ((8 * F, F), F32), ((2 * F, 128), F32), ((4, W, W), BF)),
-        (vmem((4, 2 * F, W), BF), vmem((2 * F, W), BF), vmem((144, W), BF), pltpu.SemaphoreType.DMA((4,))),
-        16, "latents", 1 << 30, hbm=1)
+    u2, u3_low, u3_high, qk, soft, stat, grads = local_call(
+        latent_kernel, (x0, x2, xn, mod, d_out, weights, back_late),
+        (units, terms, ((80, W), BF), ((2 * F, W), BF), ((8 * F, F), F32), ((2 * F, 128), F32), ((2 * F, W), BF)),
+        (vmem((4, 2 * F, W), BF), vmem((144, W), BF)), 16, "latents", 1 << 30)
     low, high = swap_core(u3_low), swap_core(u3_high)
-    summed, = local_call(merge_kernel, (u2, low, high), (units,), (), 4, "merge")
-    arrived = swap_chip(summed)
-    dn = swap_core(join(summed, d0, d2))
-    beside = swap_core(u1)
-
-    v0, v2, v_send, ids_late = local_call(
+    first, rest = local_call(
+        merge_kernel, (u2, low, high), (((32, W), BF), ((112, W), BF)), (), 4, "merge")
+    back_w, u0, u1 = local_call(
+        others_kernel, (turned, first, grads, u2), (((2, W, W), BF), units, units), (pltpu.SemaphoreType.DMA((2,)),),
+        8, "others", 1 << 12, hbm=1)
+    dn = swap_core(join(u0, d0, d2))
+    got_first = swap_chip(first)
+    rest, = local_call(relay_kernel, (got_first, rest), (((112, W), BF),), (), 4, "relay", 1 << 34)
+    got_rest = swap_chip(rest)
+    v0, v1, v2, v3, ids_late = local_call(
         tangent_kernel,
-        (x0, x2, xn, d0, d2, dn, u0, u1, u2, u3_low, u3_high, mod, stat, qk, soft, summed, weights, back_w),
-        (terms, terms, ((2 * F, W), BF), ((F, 128), F32)),
+        (x0, x2, xn, d0, d2, dn, u0, u1, u2, u3_low, u3_high, mod, stat, qk, soft, weights, back_w, back_late),
+        (terms,) * 4 + (((F, 128), F32),),
         (vmem((4, 2 * F, W), BF), vmem((2 * F, W), BF), vmem((2 * F, W), BF), vmem((4, 2 * F, W), F32),
          vmem((4, F, W), BF)), 20, "tangent", 1 << 34)
+    beside = swap_core(u1)
     score, = local_call(
-        score_kernel, (u0, beside, arrived, x0, mod, stat), (((F * 16, 128), BF),), (vmem((F * 16, 128), F32),), 6, "score")
-    v_got = swap_core(v_send)
-    v_sum, = local_call(add_kernel, (score, v2, v_got), (terms,), (), 4, "add")
+        score_kernel, (u0, beside, got_first, got_rest, x0, mod, stat), (((F * 16, 128), BF),), (vmem((F * 16, 128), F32),), 6, "score")
+    v_far, v_near = swap_core(v3), swap_core(v1)
+    v_sum, = local_call(add_kernel, (got_rest, v2, v_far), (terms,), (), 4, "add")
     v_chip = swap_chip(v_sum)
 
     ready, = local_call(
-        finish_kernel, (score, v0, v_got, v_chip), (((F * 24, 128), BF),), (vmem((F, 24, 128), F32),), 6, "finish")
+        finish_kernel, (score, v0, v_near, v_chip), (((F * 24, 128), BF),), (vmem((F, 24, 128), F32),), 6, "finish")
     back = lax.all_to_all(ready, "seq", split_axis=0, concat_axis=0, tiled=True)
     score_field, table = local_call(
         tail_kernel, (back, ids_late), (((2 * F, W), BF), ((16, CONCEPTS), F32)),

time: 94.4 us -> 92.9 us (0.984)
  waiting for transfers between devices: 24.8 us -> 17.6 us
  starting transfers between devices: 18 us -> 22.3 us
  Pallas kernels: 21 us -> 23.5 us
  blocking collectives: 24.8 us -> 23.7 us
    ppermute x5 -> x6, waiting for transfers between devices: 11.7 us -> 6.11 us  [body(): swap_chip = lambda v: lax.ppermute(v, ('seq', 'tp'), cross)]
    ppermute x5 -> x6, starting transfers between devices: 2.51 us -> 6.33 us  [body(): swap_chip = lambda v: lax.ppermute(v, ('seq', 'tp'), cross)]
    pallas_call x0 -> x1, Pallas kernels: none -> 2.21 us  [body(): pl.pallas_call(pack_kernel, out_shape=jax.ShapeDtypeStruct((F, 9, 4, 128)...]
    ppermute x8 -> x9, waiting for transfers between devices: 4.01 us -> 2.43 us  [body(): swap_core = lambda v: lax.ppermute(v, 'tp', core)]
    all_to_all x1, blocking collectives: 24.8 us -> 23.7 us  [body(): back = lax.all_to_all(ready, 'seq', split_axis=0, concat_axis=0, tiled=True)]
    ppermute x8 -> x9, starting transfers between devices: 2.17 us -> 2.62 us  [body(): swap_core = lambda v: lax.ppermute(v, 'tp', core)]
    pallas_call x13 -> x14, Pallas kernels: 16.2 us -> 16.4 us  [local_call(): pl.pallas_call(kernel, out_shape=tuple((jax.ShapeDtypeStruct(s, t) for s,...]
  transfers between devices with their start and end apart: 14 -> 16, of which waited for: 8 -> 7; matrix products, arithmetic and copies ran while one was open for 1% -> 1% of each run, Pallas kernels for 21% -> 24%
where the time goes in v4:
time: 92.9 us; the launch traced here: 92.7 us
  blocking collectives  23.7 us (26%)
  Pallas kernels  23.5 us (25%)
  starting transfers between devices  22.3 us (24%)
  waiting for transfers between devices  17.6 us (19%)
  local copies, waits for them, and re-layouts  3.35 us (4%)
  between operations  1.47 us (2%)
    all_to_all x1, blocking collectives, body(): back = lax.all_to_all(ready, 'seq', split_axis=0, concat_axis=0, tiled=True)  23.7 us
    pallas_call x14, Pallas kernels, local_call(): pl.pallas_call(kernel, out_shape=tuple((jax.ShapeDtypeStruct(s, t) for s,...  16.4 us
    all_to_all x1, starting transfers between devices, body(): got = lax.all_to_all(sent, 'seq', split_axis=0, concat_axis=0, tiled=True)  13.4 us
    all_to_all x1, waiting for transfers between devices, body(): got = lax.all_to_all(sent, 'seq', split_axis=0, concat_axis=0, tiled=True)  9.09 us
    ppermute x6, starting transfers between devices, body(): swap_chip = lambda v: lax.ppermute(v, ('seq', 'tp'), cross)  6.33 us
    ppermute x6, waiting for transfers between devices, body(): swap_chip = lambda v: lax.ppermute(v, ('seq', 'tp'), cross)  6.11 us
    pallas_call x1, Pallas kernels, body(): pl.pallas_call(turn_kernel, out_shape=(jax.ShapeDtypeStruct((4, W, W), BF...  4.87 us
    unnamed x2, local copies, waits for them, and re-layouts  3.25 us
  transfers between devices with their start and end apart: 16, of which 7 were waited for; matrix products, arithmetic and copies ran while one was open for 1% of the time, Pallas kernels for 24%

profile of v4, /device:TPU:8, one launch (start us, length us, event | category | flops | bytes accessed | tf_op | source)
XLA Modules:
  0.0 92.7 jit_solution(3869655958325078341)
XLA Ops:
  0.6 1.7 %collective-permute-start.2 = (bf16[256,1024]{1,0:T(8,128)(2,1)}, bf16[256,1024]{1,0:T(8,128)(2,1)S(1)}, u32[]{:S(2)}, u32[]{:S(2)}) collective-permute-start(bf16[256,1024]{1,0:T(8,128)(2,1)} %table_ref.1), channel_id=1, source_target_pairs={{0,18},{1,19},{2,16},{3,17},{4,22},{5,23},{6,20},{7,21},{8,26},{9,... | collective-permute-start | bytes 1572872 | tf_op jit(solution)/shard_map/ppermute | solution.py:373
  2.9 2.2 %pack.1 = bf16[64,9,4,128]{3,2,1,0:T(4,128)(2,1)} custom-call(bf16[128,1024]{1,0:T(8,128)(2,1)} %bitcast.10, bf16[128,1024]{1,0:T(8,128)(2,1)} %bitcast.11, s32[1]{0:T(128)S(6)} %copy.10.concept_ref), custom_call_target="tpu_custom_call" | custom-call | tf_op jit(solution)/shard_map/pack/pallas_call | solution.py:377
  5.2 13.4 %all-to-all-start = ((bf16[64,9,4,128]{3,2,1,0:T(4,128)(2,1)}), bf16[64,9,4,128]{3,2,1,0:T(4,128)(2,1)S(1)}, u32[]{:S(2)}, u32[]{:S(2)}) async-start(bf16[64,9,4,128]{3,2,1,0:T(4,128)(2,1)} %pack.1), calls=%async_computation | async-start | bytes 1179648 | tf_op jit(solution)/shard_map/all_to_all | solution.py:388
  18.5 0.1 collective-permute-start.1
  18.7 0.7 multiply_bitcast_fusion
  19.3 0.1 copy.9.steps_ref
  19.4 0.0 collective-permute-done.2.t2
  19.4 0.6 collective-permute-start.3
  20.0 4.9 %turn.1 = (bf16[4,1024,1024]{2,1,0:T(8,128)(2,1)S(1)}, f32[8,128]{1,0:T(8,128)S(1)}) custom-call(bf16[4096,512]{1,0:T(8,128)(2,1)} %wq_ref.3, bf16[4096,512]{1,0:T(8,128)(2,1)} %wk_ref.3), custom_call_target="tpu_custom_call" | custom-call | flops 8589934592 | bytes 16777216 | tf_op jit(solution)/shard_map/turn/pallas_call | solution.py:390
  24.9 0.0 copy-start
  24.9 3.3 %copy-done = bf16[4,1024,1024]{2,1,0:T(8,128)(2,1)} copy-done((bf16[4,1024,1024]{2,1,0:T(8,128)(2,1)}, bf16[4,1024,1024]{2,1,0:T(8,128)(2,1)S(1)}, u32[]{:S(2)}) %copy-start) | copy-done | bytes 8388632
  28.1 9.1 %all-to-all-done.g_ref = bf16[64,9,4,128]{3,2,1,0:T(4,128)(2,1)S(1)} async-done(((bf16[64,9,4,128]{3,2,1,0:T(4,128)(2,1)}), bf16[64,9,4,128]{3,2,1,0:T(4,128)(2,1)S(1)}, u32[]{:S(2)}, u32[]{:S(2)}) %all-to-all-start) | async-done | bytes 589856 | tf_op jit(solution)/shard_map/all_to_all | solution.py:388
  37.2 0.4 unpack.1
  37.6 0.1 collective-permute-start
  37.7 0.0 collective-permute-done.1.t1
  37.7 0.0 collective-permute-done.3.t3
  37.7 5.2 %prepare.1 = (bf16[4,1024,1024]{2,1,0:T(8,128)(2,1)S(1)}, bf16[2,1024,1024]{2,1,0:T(8,128)(2,1)S(1)}, f32[5,64,1024]{2,1,0:T(8,128)S(1)}) custom-call(bf16[4096,512]{1,0:T(8,128)(2,1)} %wq_ref.3, bf16[4096,512]{1,0:T(8,128)(2,1)} %wk_ref.3, bf16[4,1024,1024]{2,1,0:T(8,128)(2,1)} %copy-done, bf16[256,1024]{1,0:T(8,128)(2,1)} %table_ref.1, ...), custom_call_target="tpu_custom_call" | custom-call | flops 4294967296 | bytes 4096 | tf_op jit(solution)/shard_map/prepare/pallas_call | solution.py:301
  42.9 1.1 %collective-permute-done.b_ref._.x2 = bf16[2,64,1024]{2,1,0:T(8,128)(2,1)S(1)} collective-permute-done((bf16[2,64,1024]{2,1,0:T(8,128)(2,1)S(1)}, bf16[2,64,1024]{2,1,0:T(8,128)(2,1)S(1)}, u32[]{:S(2)}, u32[]{:S(2)}) %collective-permute-start) | collective-permute-done | bytes 262176 | tf_op jit(solution)/shard_map/ppermute | solution.py:373
  44.1 0.1 collective-permute-start.4
  44.2 1.0 %collective-permute-start.10 = (bf16[2,64,1024]{2,1,0:T(8,128)(2,1)S(1)}, bf16[2,64,1024]{2,1,0:T(8,128)(2,1)S(1)}, u32[]{:S(2)}, u32[]{:S(2)}) collective-permute-start(bf16[2,64,1024]{2,1,0:T(8,128)(2,1)S(1)} %relay.2._), channel_id=1, source_target_pairs={{0,18},{1,19},{2,16},{3,17},{4,22},{5,23},{6,20},{7,21},{8,26},{9,... | collective-permute-start | bytes 786440 | tf_op jit(solution)/shard_map/ppermute | solution.py:373
  45.2 0.9 collective-permute-done.4.xn
  46.1 2.7 %latents.1 = (bf16[144,1024]{1,0:T(8,128)(2,1)S(1)}, bf16[64,1024]{1,0:T(8,128)(2,1)S(1)}, bf16[80,1024]{1,0:T(8,128)(2,1)S(1)}, bf16[128,1024]{1,0:T(8,128)(2,1...) custom-call(bf16[2,64,1024]{2,1,0:T(8,128)(2,1)S(1)} %get-tuple-element.31.a_ref.x0.x_ref, ...), custom_call_target="tpu_custom_call" | custom-call | flops 1073741824 | bytes 4096 | tf_op jit(solution)/shard_map/latents/pallas_call | solution.py:301
  48.8 0.2 collective-permute-start.6
  49.0 0.4 collective-permute-start.5
  49.4 1.1 %collective-permute-done.5.low_ref = bf16[64,1024]{1,0:T(8,128)(2,1)S(1)} collective-permute-done((bf16[64,1024]{1,0:T(8,128)(2,1)S(1)}, bf16[64,1024]{1,0:T(8,128)(2,1)S(1)}, u32[]{:S(2)}, u32[]{:S(2)}) %collective-permute-start.5) | collective-permute-done | bytes 131104 | tf_op jit(solution)/shard_map/ppermute | solution.py:372
  50.5 0.0 collective-permute-done.6.high_ref
  50.5 0.1 merge.1
  50.5 1.2 %collective-permute-start.8 = (bf16[32,1024]{1,0:T(8,128)(2,1)S(1)}, bf16[32,1024]{1,0:T(8,128)(2,1)S(1)}, u32[]{:S(2)}, u32[]{:S(2)}) collective-permute-start(bf16[32,1024]{1,0:T(8,128)(2,1)S(1)} %get-tuple-element.40._), channel_id=1, source_target_pairs={{0,18},{1,19},{2,16},{3,17},{4,22},{5,23},{6,20},{7,21},{8,26},{9,... | collective-permute-start | bytes 196616 | tf_op jit(solution)/shard_map/ppermute | solution.py:373
  51.7 2.7 %others.1 = (bf16[2,1024,1024]{2,1,0:T(8,128)(2,1)S(1)}, bf16[144,1024]{1,0:T(8,128)(2,1)S(1)}, bf16[144,1024]{1,0:T(8,128)(2,1)S(1)}) custom-call(bf16[4,1024,1024]{2,1,0:T(8,128)(2,1)} %copy-done, bf16[32,1024]{1,0:T(8,128)(2,1)S(1)} %get-tuple-element.40._, bf16[128,1024]{1,0:T(8,128)(2,1)S(1)} %get-tuple-element.41.grad_ref, ...), custom_call_target="tpu_custom_call" | custom-call | flops 4096 | bytes 4096 | tf_op jit(solution)/shard_map/others/pallas_call | solution.py:301
  54.4 0.1 collective-permute-start.7
  54.5 0.0 collective-permute-done.10.b_ref.d2
  54.6 0.6 collective-permute-start.11
  55.2 0.0 collective-permute-done.8._.first_ref
  55.2 1.2 %collective-permute-start.9 = (bf16[112,1024]{1,0:T(8,128)(2,1)S(1)}, bf16[112,1024]{1,0:T(8,128)(2,1)S(1)}, u32[]{:S(2)}, u32[]{:S(2)}) collective-permute-start(bf16[112,1024]{1,0:T(8,128)(2,1)S(1)} %relay.3), channel_id=1, source_target_pairs={{0,18},{1,19},{2,16},{3,17},{4,22},{5,23},{6,20},{7,21},{8,26},{9,... | collective-permute-start | bytes 688136 | tf_op jit(solution)/shard_map/ppermute | solution.py:373
  56.4 0.5 collective-permute-done.11.dn
  56.8 3.8 %tangent.1 = (bf16[64,1024]{1,0:T(8,128)(2,1)S(1)}, bf16[64,1024]{1,0:T(8,128)(2,1)S(1)}, bf16[64,1024]{1,0:T(8,128)(2,1)S(1)}, bf16[64,1024]{1,0:T(8,128)(2,1)S(1)}, f32[64,128]{1,0:T(8,128)S(1)}) custom-call(bf16[2,64,1024]{2,1,0:T(8,128)(2,1)S(1)} %get-tuple-element.31.a_ref.x0.x_ref, bf16[2,64,1024]{2,1,0:T(8,128)(2,1)S(1)} %collective-permute-done.b_ref._.x2, ...), custom_call_target="tpu_custom_call" | custom-call | flops 17179869184 | bytes 4096 | tf_op jit(solution)/shard_map/tangent/pallas_call | solution.py:301
  60.7 0.3 collective-permute-start.13
  61.0 0.3 collective-permute-start.12
  61.3 1.5 %collective-permute-done.9.rest_ref._ = bf16[112,1024]{1,0:T(8,128)(2,1)S(1)} collective-permute-done((bf16[112,1024]{1,0:T(8,128)(2,1)S(1)}, bf16[112,1024]{1,0:T(8,128)(2,1)S(1)}, u32[]{:S(2)}, u32[]{:S(2)}) %collective-permute-start.9) | collective-permute-done | bytes 229408 | tf_op jit(solution)/shard_map/ppermute | solution.py:373
  62.8 0.0 collective-permute-done.13.b_ref
  62.8 1.2 %collective-permute-start.14 = (bf16[64,1024]{1,0:T(8,128)(2,1)S(1)}, bf16[64,1024]{1,0:T(8,128)(2,1)S(1)}, u32[]{:S(2)}, u32[]{:S(2)}) collective-permute-start(bf16[64,1024]{1,0:T(8,128)(2,1)S(1)} %add.11), channel_id=1, source_target_pairs={{0,18},{1,19},{2,16},{3,17},{4,22},{5,23},{6,20},{7,21},{8,26},{9,... | collective-permute-start | bytes 393224 | tf_op jit(solution)/shard_map/ppermute | solution.py:373
  64.0 0.0 collective-permute-done.7.b_ref
  64.0 0.4 score.1.score_ref
  64.4 0.0 collective-permute-done.12.b_ref
  64.4 3.5 %collective-permute-done.14.c_ref = bf16[64,1024]{1,0:T(8,128)(2,1)S(1)} collective-permute-done((bf16[64,1024]{1,0:T(8,128)(2,1)S(1)}, bf16[64,1024]{1,0:T(8,128)(2,1)S(1)}, u32[]{:S(2)}, u32[]{:S(2)}) %collective-permute-start.14) | collective-permute-done | bytes 131104 | tf_op jit(solution)/shard_map/ppermute | solution.py:373
  67.9 0.1 finish.1
  68.0 23.7 %all_to_all.16 = bf16[64,24,128]{2,1,0:T(8,128)(2,1)S(1)} all-to-all(bf16[64,24,128]{2,1,0:T(8,128)(2,1)S(1)} %bitcast.9), channel_id=1, replica_groups=mesh['seq'=64,'tp'=4] {'seq'}, dimensions={0} | all-to-all | bytes 786432 | tf_op jit(solution)/shard_map/all_to_all | solution.py:451
  91.6 1.0 %tail.1 = (bf16[128,1024]{1,0:T(8,128)(2,1)}, f32[16,256]{1,0:T(8,128)}) custom-call(bf16[1536,128]{1,0:T(8,128)(2,1)S(1)} %bitcast.8, f32[64,128]{1,0:T(8,128)S(1)} %get-tuple-element.53.ids_ref), custom_call_target="tpu_custom_call" | custom-call | flops 4096 | bytes 4096 | tf_op jit(solution)/shard_map/tail/pallas_call | solution.py:301
  (5 shorter events, 0.1 us)
Async XLA Ops:
  0.6 18.8 %collective-permute-start.2 = (bf16[256,1024]{1,0:T(8,128)(2,1)}, bf16[256,1024]{1,0:T(8,128)(2,1)S(1)}, u32[]{:S(2)}, u32[]{:S(2)}) collective-permute-start(bf16[256,1024]{1,0:T(8,128)(2,1)} %table_ref.1), channel_id=1, source_target_pairs={{0,18},{1,19},{2,16},{3,17},{4,22},{5,23},{6,20},{7,21},{8,26},{9,... | collective-permute-start | bytes 1572872 | tf_op jit(solution)/shard_map/ppermute | solution.py:373
  5.2 32.1 %all-to-all-start = ((bf16[64,9,4,128]{3,2,1,0:T(4,128)(2,1)}), bf16[64,9,4,128]{3,2,1,0:T(4,128)(2,1)S(1)}, u32[]{:S(2)}, u32[]{:S(2)}) async-start(bf16[64,9,4,128]{3,2,1,0:T(4,128)(2,1)} %pack.1), calls=%async_computation | async-start | bytes 1179648 | tf_op jit(solution)/shard_map/all_to_all | solution.py:388
  18.5 19.1 %collective-permute-start.1 = (bf16[256,1024]{1,0:T(8,128)(2,1)}, bf16[256,1024]{1,0:T(8,128)(2,1)S(1)}, u32[]{:S(2)}, u32[]{:S(2)}) collective-permute-start(bf16[256,1024]{1,0:T(8,128)(2,1)} %table_ref.1), channel_id=1, source_target_pairs={{0,1},{1,0},{2,3},{3,2},{4,5},{5,4},{6,7},{7,6},{8,9},{9,8},{10,11... | collective-permute-start | bytes 1572872 | tf_op jit(solution)/shard_map/ppermute | solution.py:372
  19.4 18.3 %collective-permute-start.3 = (bf16[256,1024]{1,0:T(8,128)(2,1)S(1)}, bf16[256,1024]{1,0:T(8,128)(2,1)S(1)}, u32[]{:S(2)}, u32[]{:S(2)}) collective-permute-start(bf16[256,1024]{1,0:T(8,128)(2,1)S(1)} %collective-permute-done.2.t2), channel_id=1, source_target_pairs={{0,1},{1,0},{2,3},{3,2},{4,5},{5,4},{6,7},{7,6},{8,9},{9,8},{10,11... | collective-permute-start | bytes 1572872 | tf_op jit(solution)/shard_map/ppermute | solution.py:372
  24.9 3.3 %copy-start = (bf16[4,1024,1024]{2,1,0:T(8,128)(2,1)}, bf16[4,1024,1024]{2,1,0:T(8,128)(2,1)S(1)}, u32[]{:S(2)}) copy-start(bf16[4,1024,1024]{2,1,0:T(8,128)(2,1)S(1)} %get-tuple-element.29.turned_ref) | copy-start | bytes 25165828
  37.6 6.5 %collective-permute-start = (bf16[2,64,1024]{2,1,0:T(8,128)(2,1)S(1)}, bf16[2,64,1024]{2,1,0:T(8,128)(2,1)S(1)}, u32[]{:S(2)}, u32[]{:S(2)}) collective-permute-start(bf16[2,64,1024]{2,1,0:T(8,128)(2,1)S(1)} %get-tuple-element.31.a_ref.x0.x_ref), channel_id=1, source_target_pairs={{0,18},{1,19},{2,16},{3,17},{4,22},{5,23},{6,20},{7,21},{8,26},{9,... | collective-permute-start | bytes 786440 | tf_op jit(solution)/shard_map/ppermute | solution.py:373
  44.1 2.0 %collective-permute-start.4 = (bf16[4,64,1024]{2,1,0:T(8,128)(2,1)S(1)}, bf16[4,64,1024]{2,1,0:T(8,128)(2,1)S(1)}, u32[]{:S(2)}, u32[]{:S(2)}) collective-permute-start(bf16[4,64,1024]{2,1,0:T(8,128)(2,1)S(1)} %join.2), channel_id=1, source_target_pairs={{0,1},{1,0},{2,3},{3,2},{4,5},{5,4},{6,7},{7,6},{8,9},{9,8},{10,11... | collective-permute-start | bytes 1572872 | tf_op jit(solution)/shard_map/ppermute | solution.py:372
  44.2 10.3 %collective-permute-start.10 = (bf16[2,64,1024]{2,1,0:T(8,128)(2,1)S(1)}, bf16[2,64,1024]{2,1,0:T(8,128)(2,1)S(1)}, u32[]{:S(2)}, u32[]{:S(2)}) collective-permute-start(bf16[2,64,1024]{2,1,0:T(8,128)(2,1)S(1)} %relay.2._), channel_id=1, source_target_pairs={{0,18},{1,19},{2,16},{3,17},{4,22},{5,23},{6,20},{7,21},{8,26},{9,... | collective-permute-start | bytes 786440 | tf_op jit(solution)/shard_map/ppermute | solution.py:373
  48.8 1.7 %collective-permute-start.6 = (bf16[80,1024]{1,0:T(8,128)(2,1)S(1)}, bf16[80,1024]{1,0:T(8,128)(2,1)S(1)}, u32[]{:S(2)}, u32[]{:S(2)}) collective-permute-start(bf16[80,1024]{1,0:T(8,128)(2,1)S(1)} %get-tuple-element.39.u3_high), channel_id=1, source_target_pairs={{0,1},{1,0},{2,3},{3,2},{4,5},{5,4},{6,7},{7,6},{8,9},{9,8},{10,11... | collective-permute-start | bytes 491528 | tf_op jit(solution)/shard_map/ppermute | solution.py:372
  49.0 1.4 %collective-permute-start.5 = (bf16[64,1024]{1,0:T(8,128)(2,1)S(1)}, bf16[64,1024]{1,0:T(8,128)(2,1)S(1)}, u32[]{:S(2)}, u32[]{:S(2)}) collective-permute-start(bf16[64,1024]{1,0:T(8,128)(2,1)S(1)} %get-tuple-element.38.u3_low), channel_id=1, source_target_pairs={{0,1},{1,0},{2,3},{3,2},{4,5},{5,4},{6,7},{7,6},{8,9},{9,8},{10,11... | collective-permute-start | bytes 393224 | tf_op jit(solution)/shard_map/ppermute | solution.py:372
  50.5 4.6 %collective-permute-start.8 = (bf16[32,1024]{1,0:T(8,128)(2,1)S(1)}, bf16[32,1024]{1,0:T(8,128)(2,1)S(1)}, u32[]{:S(2)}, u32[]{:S(2)}) collective-permute-start(bf16[32,1024]{1,0:T(8,128)(2,1)S(1)} %get-tuple-element.40._), channel_id=1, source_target_pairs={{0,18},{1,19},{2,16},{3,17},{4,22},{5,23},{6,20},{7,21},{8,26},{9,... | collective-permute-start | bytes 196616 | tf_op jit(solution)/shard_map/ppermute | solution.py:373
  54.4 9.6 %collective-permute-start.7 = (bf16[144,1024]{1,0:T(8,128)(2,1)S(1)}, bf16[144,1024]{1,0:T(8,128)(2,1)S(1)}, u32[]{:S(2)}, u32[]{:S(2)}) collective-permute-start(bf16[144,1024]{1,0:T(8,128)(2,1)S(1)} %get-tuple-element.43.u1), channel_id=1, source_target_pairs={{0,1},{1,0},{2,3},{3,2},{4,5},{5,4},{6,7},{7,6},{8,9},{9,8},{10,11... | collective-permute-start | bytes 884744 | tf_op jit(solution)/shard_map/ppermute | solution.py:372
  54.6 2.3 %collective-permute-start.11 = (bf16[4,64,1024]{2,1,0:T(8,128)(2,1)S(1)}, bf16[4,64,1024]{2,1,0:T(8,128)(2,1)S(1)}, u32[]{:S(2)}, u32[]{:S(2)}) collective-permute-start(bf16[4,64,1024]{2,1,0:T(8,128)(2,1)S(1)} %join.3), channel_id=1, source_target_pairs={{0,1},{1,0},{2,3},{3,2},{4,5},{5,4},{6,7},{7,6},{8,9},{9,8},{10,11... | collective-permute-start | bytes 1572872 | tf_op jit(solution)/shard_map/ppermute | solution.py:372
  55.2 7.6 %collective-permute-start.9 = (bf16[112,1024]{1,0:T(8,128)(2,1)S(1)}, bf16[112,1024]{1,0:T(8,128)(2,1)S(1)}, u32[]{:S(2)}, u32[]{:S(2)}) collective-permute-start(bf16[112,1024]{1,0:T(8,128)(2,1)S(1)} %relay.3), channel_id=1, source_target_pairs={{0,18},{1,19},{2,16},{3,17},{4,22},{5,23},{6,20},{7,21},{8,26},{9,... | collective-permute-start | bytes 688136 | tf_op jit(solution)/shard_map/ppermute | solution.py:373
  60.7 2.1 %collective-permute-start.13 = (bf16[64,1024]{1,0:T(8,128)(2,1)S(1)}, bf16[64,1024]{1,0:T(8,128)(2,1)S(1)}, u32[]{:S(2)}, u32[]{:S(2)}) collective-permute-start(bf16[64,1024]{1,0:T(8,128)(2,1)S(1)} %get-tuple-element.52), channel_id=1, source_target_pairs={{0,1},{1,0},{2,3},{3,2},{4,5},{5,4},{6,7},{7,6},{8,9},{9,8},{10,11... | collective-permute-start | bytes 393224 | tf_op jit(solution)/shard_map/ppermute | solution.py:372
  61.0 3.4 %collective-permute-start.12 = (bf16[64,1024]{1,0:T(8,128)(2,1)S(1)}, bf16[64,1024]{1,0:T(8,128)(2,1)S(1)}, u32[]{:S(2)}, u32[]{:S(2)}) collective-permute-start(bf16[64,1024]{1,0:T(8,128)(2,1)S(1)} %get-tuple-element.50), channel_id=1, source_target_pairs={{0,1},{1,0},{2,3},{3,2},{4,5},{5,4},{6,7},{7,6},{8,9},{9,8},{10,11... | collective-permute-start | bytes 393224 | tf_op jit(solution)/shard_map/ppermute | solution.py:372
  62.8 5.1 %collective-permute-start.14 = (bf16[64,1024]{1,0:T(8,128)(2,1)S(1)}, bf16[64,1024]{1,0:T(8,128)(2,1)S(1)}, u32[]{:S(2)}, u32[]{:S(2)}) collective-permute-start(bf16[64,1024]{1,0:T(8,128)(2,1)S(1)} %add.11), channel_id=1, source_target_pairs={{0,18},{1,19},{2,16},{3,17},{4,22},{5,23},{6,20},{7,21},{8,26},{9,... | collective-permute-start | bytes 393224 | tf_op jit(solution)/shard_map/ppermute | solution.py:373

commit v5 on v4

--- a/solution.py
+++ b/solution.py
@@ -58,8 +58,8 @@
             copy = pltpu.make_async_copy(ref.at[rows], w_ref.at[k, :, pl.ds(512 * i, 512)], sems.at[2 * k + i])
             copy.start()
             copies.append(copy)
-    for k in range(2):
-        copy = pltpu.make_async_copy(turned_ref.at[2 + k], late_ref.at[k], sems.at[9 + k])
+    for k in range(3):
+        copy = pltpu.make_async_copy(turned_ref.at[1 + k], late_ref.at[k], sems.at[9 + k])
         copy.start()
         copies.append(copy)
     ids = ids_ref[:, 0:128].astype(F32)
@@ -206,7 +206,7 @@
     hi = srow.astype(BF).astype(F32)
     sub = lax.broadcasted_iota(jnp.int32, (16, 128), 0)
     stats = jnp.where(sub == 0, hi, jnp.where(sub == 1, srow - hi, 0.0)).astype(BF)
-    for ref, k in ((u3, 1), (u2, 0)):
+    for ref, k in ((u3, 2), (u2, 1)):
         for j in range(4):
             lanes = pl.ds(256 * j, 256)
             ref[0:128, lanes] = jnp.dot(g_s[...], late_ref[k, :, lanes], preferred_element_type=F32).astype(BF)
@@ -263,10 +263,10 @@
         g_s[r, kl] = (-aks[i]).astype(BF)
 
     for k in range(4):
-        source = back_ref if k < 2 else late_ref
-        for j in range(4):
-            lanes = pl.ds(256 * j, 256)
-            drift_s[k, :, lanes] = jnp.dot(g_s[...], source[k % 2, :, lanes], preferred_element_type=F32)
+        for j in range(4):
+            lanes = pl.ds(256 * j, 256)
+            block = back_ref[:, lanes] if k == 0 else late_ref[k - 1, :, lanes]
+            drift_s[k, :, lanes] = jnp.dot(g_s[...], block, preferred_element_type=F32)
 
     rr = lax.broadcasted_iota(jnp.int32, (128, 256), 0)
     cc = lax.broadcasted_iota(jnp.int32, (128, 256), 1)
@@ -322,15 +322,16 @@
         [a_ref[128:144, 0:128], high_ref[64:80, 0:128], a_ref[128:144, 256:1024]], axis=1)
 
 
-def others_kernel(turned_ref, _, grad_ref, u2, back_ref, u0, u1, sems):
-    copies = [pltpu.make_async_copy(turned_ref.at[k], back_ref.at[k], sems.at[k]) for k in range(2)]
-    for copy in copies:
-        copy.start()
-    for k, ref in enumerate((u0, u1)):
-        copies[k].wait()
-        for j in range(4):
-            lanes = pl.ds(256 * j, 256)
-            ref[0:128, lanes] = jnp.dot(grad_ref[...], back_ref[k, :, lanes], preferred_element_type=F32).astype(BF)
+def others_kernel(turned_ref, _, grad_ref, u2, late_ref, back_ref, u0, u1, sem):
+    copy = pltpu.make_async_copy(turned_ref.at[0], back_ref, sem)
+    copy.start()
+    for k, ref in ((1, u1), (0, u0)):
+        if k == 0:
+            copy.wait()
+        for j in range(4):
+            lanes = pl.ds(256 * j, 256)
+            block = back_ref[:, lanes] if k == 0 else late_ref[0, :, lanes]
+            ref[0:128, lanes] = jnp.dot(grad_ref[...], block, preferred_element_type=F32).astype(BF)
         ref[128:144, :] = u2[128:144, :]
 
 
@@ -409,8 +410,8 @@
     steps = ((0.25 + 1.75 * timestep.astype(F32) / STEPS) / math.sqrt(HD)).reshape(F, 1)
     weights, back_late, mod = local_call(
         prepare_kernel, (w_query, w_key, turned, concept_table, t_core, t_chip, t_both, ids, steps),
-        (((4, W, W), BF), ((2, W, W), BF), ((5, F, W), F32)),
-        (vmem((CONCEPTS, W), BF), pltpu.SemaphoreType.DMA((11,))), 16, "prepare", 1 << 32, hbm=4)
+        (((4, W, W), BF), ((3, W, W), BF), ((5, F, W), F32)),
+        (vmem((CONCEPTS, W), BF), pltpu.SemaphoreType.DMA((12,))), 18, "prepare", 1 << 32, hbm=4)
     full = ((4, F, W), BF)
     join = lambda *v: local_call(join_kernel, v, (full,), (), 4, "join")[0]
     x2 = swap_chip(x0)
@@ -427,7 +428,7 @@
     first, rest = local_call(
         merge_kernel, (u2, low, high), (((32, W), BF), ((112, W), BF)), (), 4, "merge")
     back_w, u0, u1 = local_call(
-        others_kernel, (turned, first, grads, u2), (((2, W, W), BF), units, units), (pltpu.SemaphoreType.DMA((2,)),),
+        others_kernel, (turned, first, grads, u2, back_late), (((W, W), BF), units, units), (pltpu.SemaphoreType.DMA,),
         8, "others", 1 << 12, hbm=1)
     dn = swap_core(join(u0, d0, d2))
     got_first = swap_chip(first)

time: 92.9 us -> 92.9 us (level)
  waiting for transfers between devices: 17.6 us -> 16.4 us
  starting transfers between devices: 22.3 us -> 23.5 us
    ppermute x6, starting transfers between devices: 6.33 us -> 7.52 us  [body(): swap_chip = lambda v: lax.ppermute(v, ('seq', 'tp'), cross)]
  transfers between devices with their start and end apart: 16 -> 16, of which waited for: 7 -> 8; matrix products, arithmetic and copies ran while one was open for 1% -> 1% of each run, Pallas kernels for 24% -> 24%
where the time goes in v5:
time: 92.9 us; the launch traced here: 92.6 us
  blocking collectives  23.8 us (26%)
  starting transfers between devices  23.5 us (25%)
  Pallas kernels  23.4 us (25%)
  waiting for transfers between devices  16.4 us (18%)
  local copies, waits for them, and re-layouts  3.35 us (4%)
  between operations  1.47 us (2%)
    all_to_all x1, blocking collectives, body(): back = lax.all_to_all(ready, 'seq', split_axis=0, concat_axis=0, tiled=True)  23.8 us
    pallas_call x14, Pallas kernels, local_call(): pl.pallas_call(kernel, out_shape=tuple((jax.ShapeDtypeStruct(s, t) for s,...  16.3 us
    all_to_all x1, starting transfers between devices, body(): got = lax.all_to_all(sent, 'seq', split_axis=0, concat_axis=0, tiled=True)  13.4 us
    all_to_all x1, waiting for transfers between devices, body(): got = lax.all_to_all(sent, 'seq', split_axis=0, concat_axis=0, tiled=True)  9.09 us
    ppermute x6, starting transfers between devices, body(): swap_chip = lambda v: lax.ppermute(v, ('seq', 'tp'), cross)  7.52 us
    ppermute x6, waiting for transfers between devices, body(): swap_chip = lambda v: lax.ppermute(v, ('seq', 'tp'), cross)  5.83 us
    pallas_call x1, Pallas kernels, body(): pl.pallas_call(turn_kernel, out_shape=(jax.ShapeDtypeStruct((4, W, W), BF...  4.87 us
    unnamed x2, local copies, waits for them, and re-layouts  3.25 us
  transfers between devices with their start and end apart: 16, of which 8 were waited for; matrix products, arithmetic and copies ran while one was open for 1% of the time, Pallas kernels for 24%

profile of v5, /device:TPU:8, one launch (start us, length us, event | category | flops | bytes accessed | tf_op | source)
XLA Modules:
  0.0 92.6 jit_solution(12626747414471488320)
XLA Ops:
  0.6 1.7 %collective-permute-start.2 = (bf16[256,1024]{1,0:T(8,128)(2,1)}, bf16[256,1024]{1,0:T(8,128)(2,1)S(1)}, u32[]{:S(2)}, u32[]{:S(2)}) collective-permute-start(bf16[256,1024]{1,0:T(8,128)(2,1)} %table_ref.1), channel_id=1, source_target_pairs={{0,18},{1,19},{2,16},{3,17},{4,22},{5,23},{6,20},{7,21},{8,26},{9,... | collective-permute-start | bytes 1572872 | tf_op jit(solution)/shard_map/ppermute | solution.py:374
  2.9 2.2 %pack.1 = bf16[64,9,4,128]{3,2,1,0:T(4,128)(2,1)} custom-call(bf16[128,1024]{1,0:T(8,128)(2,1)} %bitcast.10, bf16[128,1024]{1,0:T(8,128)(2,1)} %bitcast.11, s32[1]{0:T(128)S(6)} %copy.10.concept_ref), custom_call_target="tpu_custom_call" | custom-call | tf_op jit(solution)/shard_map/pack/pallas_call | solution.py:378
  5.2 13.4 %all-to-all-start = ((bf16[64,9,4,128]{3,2,1,0:T(4,128)(2,1)}), bf16[64,9,4,128]{3,2,1,0:T(4,128)(2,1)S(1)}, u32[]{:S(2)}, u32[]{:S(2)}) async-start(bf16[64,9,4,128]{3,2,1,0:T(4,128)(2,1)} %pack.1), calls=%async_computation | async-start | bytes 1179648 | tf_op jit(solution)/shard_map/all_to_all | solution.py:389
  18.5 0.1 collective-permute-start.1
  18.7 0.7 multiply_bitcast_fusion
  19.3 0.1 copy.9.steps_ref
  19.4 0.0 collective-permute-done.2.t2
  19.4 0.6 collective-permute-start.3
  20.0 4.9 %turn.1 = (bf16[4,1024,1024]{2,1,0:T(8,128)(2,1)S(1)}, f32[8,128]{1,0:T(8,128)S(1)}) custom-call(bf16[4096,512]{1,0:T(8,128)(2,1)} %wq_ref.3, bf16[4096,512]{1,0:T(8,128)(2,1)} %wk_ref.3), custom_call_target="tpu_custom_call" | custom-call | flops 8589934592 | bytes 16777216 | tf_op jit(solution)/shard_map/turn/pallas_call | solution.py:391
  24.9 0.0 copy-start
  24.9 3.3 %copy-done = bf16[4,1024,1024]{2,1,0:T(8,128)(2,1)} copy-done((bf16[4,1024,1024]{2,1,0:T(8,128)(2,1)}, bf16[4,1024,1024]{2,1,0:T(8,128)(2,1)S(1)}, u32[]{:S(2)}) %copy-start) | copy-done | bytes 8388632
  28.1 9.1 %all-to-all-done.g_ref = bf16[64,9,4,128]{3,2,1,0:T(4,128)(2,1)S(1)} async-done(((bf16[64,9,4,128]{3,2,1,0:T(4,128)(2,1)}), bf16[64,9,4,128]{3,2,1,0:T(4,128)(2,1)S(1)}, u32[]{:S(2)}, u32[]{:S(2)}) %all-to-all-start) | async-done | bytes 589856 | tf_op jit(solution)/shard_map/all_to_all | solution.py:389
  37.2 0.4 unpack.1
  37.6 0.1 collective-permute-start
  37.7 0.0 collective-permute-done.1.t1
  37.7 0.0 collective-permute-done.3.t3
  37.7 5.8 %prepare.1 = (bf16[4,1024,1024]{2,1,0:T(8,128)(2,1)S(1)}, bf16[3,1024,1024]{2,1,0:T(8,128)(2,1)S(1)}, f32[5,64,1024]{2,1,0:T(8,128)S(1)}) custom-call(bf16[4096,512]{1,0:T(8,128)(2,1)} %wq_ref.3, bf16[4096,512]{1,0:T(8,128)(2,1)} %wk_ref.3, bf16[4,1024,1024]{2,1,0:T(8,128)(2,1)} %copy-done, bf16[256,1024]{1,0:T(8,128)(2,1)} %table_ref.1, ...), custom_call_target="tpu_custom_call" | custom-call | flops 4294967296 | bytes 4096 | tf_op jit(solution)/shard_map/prepare/pallas_call | solution.py:301
  43.5 0.6 collective-permute-done.b_ref._.x2
  44.1 0.1 collective-permute-start.4
  44.2 1.5 %collective-permute-start.10 = (bf16[2,64,1024]{2,1,0:T(8,128)(2,1)S(1)}, bf16[2,64,1024]{2,1,0:T(8,128)(2,1)S(1)}, u32[]{:S(2)}, u32[]{:S(2)}) collective-permute-start(bf16[2,64,1024]{2,1,0:T(8,128)(2,1)S(1)} %relay.2._), channel_id=1, source_target_pairs={{0,18},{1,19},{2,16},{3,17},{4,22},{5,23},{6,20},{7,21},{8,26},{9,... | collective-permute-start | bytes 786440 | tf_op jit(solution)/shard_map/ppermute | solution.py:374
  45.7 0.3 collective-permute-done.4.xn
  46.1 2.7 %latents.1 = (bf16[144,1024]{1,0:T(8,128)(2,1)S(1)}, bf16[64,1024]{1,0:T(8,128)(2,1)S(1)}, bf16[80,1024]{1,0:T(8,128)(2,1)S(1)}, bf16[128,1024]{1,0:T(8,128)(2,1...) custom-call(bf16[2,64,1024]{2,1,0:T(8,128)(2,1)S(1)} %get-tuple-element.31.a_ref.x0.x_ref, ...), custom_call_target="tpu_custom_call" | custom-call | flops 1073741824 | bytes 4096 | tf_op jit(solution)/shard_map/latents/pallas_call | solution.py:301
  48.8 0.2 collective-permute-start.6
  49.0 0.4 collective-permute-start.5
  49.4 1.1 %collective-permute-done.5.low_ref = bf16[64,1024]{1,0:T(8,128)(2,1)S(1)} collective-permute-done((bf16[64,1024]{1,0:T(8,128)(2,1)S(1)}, bf16[64,1024]{1,0:T(8,128)(2,1)S(1)}, u32[]{:S(2)}, u32[]{:S(2)}) %collective-permute-start.5) | collective-permute-done | bytes 131104 | tf_op jit(solution)/shard_map/ppermute | solution.py:373
  50.5 0.0 collective-permute-done.6.high_ref
  50.5 0.1 merge.1
  50.5 1.7 %collective-permute-start.8 = (bf16[32,1024]{1,0:T(8,128)(2,1)S(1)}, bf16[32,1024]{1,0:T(8,128)(2,1)S(1)}, u32[]{:S(2)}, u32[]{:S(2)}) collective-permute-start(bf16[32,1024]{1,0:T(8,128)(2,1)S(1)} %get-tuple-element.40._), channel_id=1, source_target_pairs={{0,18},{1,19},{2,16},{3,17},{4,22},{5,23},{6,20},{7,21},{8,26},{9,... | collective-permute-start | bytes 196616 | tf_op jit(solution)/shard_map/ppermute | solution.py:374
  52.3 2.1 %others.1 = (bf16[1024,1024]{1,0:T(8,128)(2,1)S(1)}, bf16[144,1024]{1,0:T(8,128)(2,1)S(1)}, bf16[144,1024]{1,0:T(8,128)(2,1)S(1)}) custom-call(bf16[4,1024,1024]{2,1,0:T(8,128)(2,1)} %copy-done, bf16[32,1024]{1,0:T(8,128)(2,1)S(1)} %get-tuple-element.40._, bf16[128,1024]{1,0:T(8,128)(2,1)S(1)} %get-tuple-element.41.grad_ref, ...), custom_call_target="tpu_custom_call" | custom-call | flops 4096 | bytes 4096 | tf_op jit(solution)/shard_map/others/pallas_call | solution.py:301
  54.3 0.1 collective-permute-start.7
  54.4 0.0 collective-permute-done.10.b_ref.d2
  54.5 0.6 collective-permute-start.11
  55.0 0.1 collective-permute-done.8._.first_ref
  55.1 1.5 %collective-permute-start.9 = (bf16[112,1024]{1,0:T(8,128)(2,1)S(1)}, bf16[112,1024]{1,0:T(8,128)(2,1)S(1)}, u32[]{:S(2)}, u32[]{:S(2)}) collective-permute-start(bf16[112,1024]{1,0:T(8,128)(2,1)S(1)} %relay.3), channel_id=1, source_target_pairs={{0,18},{1,19},{2,16},{3,17},{4,22},{5,23},{6,20},{7,21},{8,26},{9,... | collective-permute-start | bytes 688136 | tf_op jit(solution)/shard_map/ppermute | solution.py:374
  56.6 0.1 collective-permute-done.11.dn
  56.7 3.8 %tangent.1 = (bf16[64,1024]{1,0:T(8,128)(2,1)S(1)}, bf16[64,1024]{1,0:T(8,128)(2,1)S(1)}, bf16[64,1024]{1,0:T(8,128)(2,1)S(1)}, bf16[64,1024]{1,0:T(8,128)(2,1)S(1)}, f32[64,128]{1,0:T(8,128)S(1)}) custom-call(bf16[2,64,1024]{2,1,0:T(8,128)(2,1)S(1)} %get-tuple-element.31.a_ref.x0.x_ref, bf16[2,64,1024]{2,1,0:T(8,128)(2,1)S(1)} %collective-permute-done.b_ref._.x2, ...), custom_call_target="tpu_custom_call" | custom-call | flops 17179869184 | bytes 4096 | tf_op jit(solution)/shard_map/tangent/pallas_call | solution.py:301
  60.6 0.3 collective-permute-start.13
  60.9 0.3 collective-permute-start.12
  61.2 1.5 %collective-permute-done.9.rest_ref._ = bf16[112,1024]{1,0:T(8,128)(2,1)S(1)} collective-permute-done((bf16[112,1024]{1,0:T(8,128)(2,1)S(1)}, bf16[112,1024]{1,0:T(8,128)(2,1)S(1)}, u32[]{:S(2)}, u32[]{:S(2)}) %collective-permute-start.9) | collective-permute-done | bytes 229408 | tf_op jit(solution)/shard_map/ppermute | solution.py:374
  62.7 0.0 collective-permute-done.13.b_ref
  62.7 1.0 %collective-permute-start.14 = (bf16[64,1024]{1,0:T(8,128)(2,1)S(1)}, bf16[64,1024]{1,0:T(8,128)(2,1)S(1)}, u32[]{:S(2)}, u32[]{:S(2)}) collective-permute-start(bf16[64,1024]{1,0:T(8,128)(2,1)S(1)} %add.11), channel_id=1, source_target_pairs={{0,18},{1,19},{2,16},{3,17},{4,22},{5,23},{6,20},{7,21},{8,26},{9,... | collective-permute-start | bytes 393224 | tf_op jit(solution)/shard_map/ppermute | solution.py:374
  63.7 0.0 collective-permute-done.7.b_ref
  63.7 0.4 score.1.score_ref
  64.1 0.0 collective-permute-done.12.b_ref
  64.1 3.7 %collective-permute-done.14.c_ref = bf16[64,1024]{1,0:T(8,128)(2,1)S(1)} collective-permute-done((bf16[64,1024]{1,0:T(8,128)(2,1)S(1)}, bf16[64,1024]{1,0:T(8,128)(2,1)S(1)}, u32[]{:S(2)}, u32[]{:S(2)}) %collective-permute-start.14) | collective-permute-done | bytes 131104 | tf_op jit(solution)/shard_map/ppermute | solution.py:374
  67.8 0.1 finish.1
  67.8 23.8 %all_to_all.16 = bf16[64,24,128]{2,1,0:T(8,128)(2,1)S(1)} all-to-all(bf16[64,24,128]{2,1,0:T(8,128)(2,1)S(1)} %bitcast.9), channel_id=1, replica_groups=mesh['seq'=64,'tp'=4] {'seq'}, dimensions={0} | all-to-all | bytes 786432 | tf_op jit(solution)/shard_map/all_to_all | solution.py:452
  91.6 1.0 %tail.1 = (bf16[128,1024]{1,0:T(8,128)(2,1)}, f32[16,256]{1,0:T(8,128)}) custom-call(bf16[1536,128]{1,0:T(8,128)(2,1)S(1)} %bitcast.8, f32[64,128]{1,0:T(8,128)S(1)} %get-tuple-element.53.ids_ref), custom_call_target="tpu_custom_call" | custom-call | flops 4096 | bytes 4096 | tf_op jit(solution)/shard_map/tail/pallas_call | solution.py:301
  (5 shorter events, 0.1 us)
Async XLA Ops:
  0.6 18.8 %collective-permute-start.2 = (bf16[256,1024]{1,0:T(8,128)(2,1)}, bf16[256,1024]{1,0:T(8,128)(2,1)S(1)}, u32[]{:S(2)}, u32[]{:S(2)}) collective-permute-start(bf16[256,1024]{1,0:T(8,128)(2,1)} %table_ref.1), channel_id=1, source_target_pairs={{0,18},{1,19},{2,16},{3,17},{4,22},{5,23},{6,20},{7,21},{8,26},{9,... | collective-permute-start | bytes 1572872 | tf_op jit(solution)/shard_map/ppermute | solution.py:374
  5.2 32.1 %all-to-all-start = ((bf16[64,9,4,128]{3,2,1,0:T(4,128)(2,1)}), bf16[64,9,4,128]{3,2,1,0:T(4,128)(2,1)S(1)}, u32[]{:S(2)}, u32[]{:S(2)}) async-start(bf16[64,9,4,128]{3,2,1,0:T(4,128)(2,1)} %pack.1), calls=%async_computation | async-start | bytes 1179648 | tf_op jit(solution)/shard_map/all_to_all | solution.py:389
  18.5 19.1 %collective-permute-start.1 = (bf16[256,1024]{1,0:T(8,128)(2,1)}, bf16[256,1024]{1,0:T(8,128)(2,1)S(1)}, u32[]{:S(2)}, u32[]{:S(2)}) collective-permute-start(bf16[256,1024]{1,0:T(8,128)(2,1)} %table_ref.1), channel_id=1, source_target_pairs={{0,1},{1,0},{2,3},{3,2},{4,5},{5,4},{6,7},{7,6},{8,9},{9,8},{10,11... | collective-permute-start | bytes 1572872 | tf_op jit(solution)/shard_map/ppermute | solution.py:373
  19.4 18.3 %collective-permute-start.3 = (bf16[256,1024]{1,0:T(8,128)(2,1)S(1)}, bf16[256,1024]{1,0:T(8,128)(2,1)S(1)}, u32[]{:S(2)}, u32[]{:S(2)}) collective-permute-start(bf16[256,1024]{1,0:T(8,128)(2,1)S(1)} %collective-permute-done.2.t2), channel_id=1, source_target_pairs={{0,1},{1,0},{2,3},{3,2},{4,5},{5,4},{6,7},{7,6},{8,9},{9,8},{10,11... | collective-permute-start | bytes 1572872 | tf_op jit(solution)/shard_map/ppermute | solution.py:373
  24.9 3.3 %copy-start = (bf16[4,1024,1024]{2,1,0:T(8,128)(2,1)}, bf16[4,1024,1024]{2,1,0:T(8,128)(2,1)S(1)}, u32[]{:S(2)}) copy-start(bf16[4,1024,1024]{2,1,0:T(8,128)(2,1)S(1)} %get-tuple-element.29.turned_ref) | copy-start | bytes 25165828
  37.6 6.5 %collective-permute-start = (bf16[2,64,1024]{2,1,0:T(8,128)(2,1)S(1)}, bf16[2,64,1024]{2,1,0:T(8,128)(2,1)S(1)}, u32[]{:S(2)}, u32[]{:S(2)}) collective-permute-start(bf16[2,64,1024]{2,1,0:T(8,128)(2,1)S(1)} %get-tuple-element.31.a_ref.x0.x_ref), channel_id=1, source_target_pairs={{0,18},{1,19},{2,16},{3,17},{4,22},{5,23},{6,20},{7,21},{8,26},{9,... | collective-permute-start | bytes 786440 | tf_op jit(solution)/shard_map/ppermute | solution.py:374
  44.1 2.0 %collective-permute-start.4 = (bf16[4,64,1024]{2,1,0:T(8,128)(2,1)S(1)}, bf16[4,64,1024]{2,1,0:T(8,128)(2,1)S(1)}, u32[]{:S(2)}, u32[]{:S(2)}) collective-permute-start(bf16[4,64,1024]{2,1,0:T(8,128)(2,1)S(1)} %join.2), channel_id=1, source_target_pairs={{0,1},{1,0},{2,3},{3,2},{4,5},{5,4},{6,7},{7,6},{8,9},{9,8},{10,11... | collective-permute-start | bytes 1572872 | tf_op jit(solution)/shard_map/ppermute | solution.py:373
  44.2 10.2 %collective-permute-start.10 = (bf16[2,64,1024]{2,1,0:T(8,128)(2,1)S(1)}, bf16[2,64,1024]{2,1,0:T(8,128)(2,1)S(1)}, u32[]{:S(2)}, u32[]{:S(2)}) collective-permute-start(bf16[2,64,1024]{2,1,0:T(8,128)(2,1)S(1)} %relay.2._), channel_id=1, source_target_pairs={{0,18},{1,19},{2,16},{3,17},{4,22},{5,23},{6,20},{7,21},{8,26},{9,... | collective-permute-start | bytes 786440 | tf_op jit(solution)/shard_map/ppermute | solution.py:374
  48.8 1.7 %collective-permute-start.6 = (bf16[80,1024]{1,0:T(8,128)(2,1)S(1)}, bf16[80,1024]{1,0:T(8,128)(2,1)S(1)}, u32[]{:S(2)}, u32[]{:S(2)}) collective-permute-start(bf16[80,1024]{1,0:T(8,128)(2,1)S(1)} %get-tuple-element.39.u3_high), channel_id=1, source_target_pairs={{0,1},{1,0},{2,3},{3,2},{4,5},{5,4},{6,7},{7,6},{8,9},{9,8},{10,11... | collective-permute-start | bytes 491528 | tf_op jit(solution)/shard_map/ppermute | solution.py:373
  49.0 1.4 %collective-permute-start.5 = (bf16[64,1024]{1,0:T(8,128)(2,1)S(1)}, bf16[64,1024]{1,0:T(8,128)(2,1)S(1)}, u32[]{:S(2)}, u32[]{:S(2)}) collective-permute-start(bf16[64,1024]{1,0:T(8,128)(2,1)S(1)} %get-tuple-element.38.u3_low), channel_id=1, source_target_pairs={{0,1},{1,0},{2,3},{3,2},{4,5},{5,4},{6,7},{7,6},{8,9},{9,8},{10,11... | collective-permute-start | bytes 393224 | tf_op jit(solution)/shard_map/ppermute | solution.py:373
  50.5 4.5 %collective-permute-start.8 = (bf16[32,1024]{1,0:T(8,128)(2,1)S(1)}, bf16[32,1024]{1,0:T(8,128)(2,1)S(1)}, u32[]{:S(2)}, u32[]{:S(2)}) collective-permute-start(bf16[32,1024]{1,0:T(8,128)(2,1)S(1)} %get-tuple-element.40._), channel_id=1, source_target_pairs={{0,18},{1,19},{2,16},{3,17},{4,22},{5,23},{6,20},{7,21},{8,26},{9,... | collective-permute-start | bytes 196616 | tf_op jit(solution)/shard_map/ppermute | solution.py:374
  54.3 9.4 %collective-permute-start.7 = (bf16[144,1024]{1,0:T(8,128)(2,1)S(1)}, bf16[144,1024]{1,0:T(8,128)(2,1)S(1)}, u32[]{:S(2)}, u32[]{:S(2)}) collective-permute-start(bf16[144,1024]{1,0:T(8,128)(2,1)S(1)} %get-tuple-element.43.u1), channel_id=1, source_target_pairs={{0,1},{1,0},{2,3},{3,2},{4,5},{5,4},{6,7},{7,6},{8,9},{9,8},{10,11... | collective-permute-start | bytes 884744 | tf_op jit(solution)/shard_map/ppermute | solution.py:373
  54.5 2.3 %collective-permute-start.11 = (bf16[4,64,1024]{2,1,0:T(8,128)(2,1)S(1)}, bf16[4,64,1024]{2,1,0:T(8,128)(2,1)S(1)}, u32[]{:S(2)}, u32[]{:S(2)}) collective-permute-start(bf16[4,64,1024]{2,1,0:T(8,128)(2,1)S(1)} %join.3), channel_id=1, source_target_pairs={{0,1},{1,0},{2,3},{3,2},{4,5},{5,4},{6,7},{7,6},{8,9},{9,8},{10,11... | collective-permute-start | bytes 1572872 | tf_op jit(solution)/shard_map/ppermute | solution.py:373
  55.1 7.6 %collective-permute-start.9 = (bf16[112,1024]{1,0:T(8,128)(2,1)S(1)}, bf16[112,1024]{1,0:T(8,128)(2,1)S(1)}, u32[]{:S(2)}, u32[]{:S(2)}) collective-permute-start(bf16[112,1024]{1,0:T(8,128)(2,1)S(1)} %relay.3), channel_id=1, source_target_pairs={{0,18},{1,19},{2,16},{3,17},{4,22},{5,23},{6,20},{7,21},{8,26},{9,... | collective-permute-start | bytes 688136 | tf_op jit(solution)/shard_map/ppermute | solution.py:374
  60.6 2.1 %collective-permute-start.13 = (bf16[64,1024]{1,0:T(8,128)(2,1)S(1)}, bf16[64,1024]{1,0:T(8,128)(2,1)S(1)}, u32[]{:S(2)}, u32[]{:S(2)}) collective-permute-start(bf16[64,1024]{1,0:T(8,128)(2,1)S(1)} %get-tuple-element.52), channel_id=1, source_target_pairs={{0,1},{1,0},{2,3},{3,2},{4,5},{5,4},{6,7},{7,6},{8,9},{9,8},{10,11... | collective-permute-start | bytes 393224 | tf_op jit(solution)/shard_map/ppermute | solution.py:373
  60.9 3.2 %collective-permute-start.12 = (bf16[64,1024]{1,0:T(8,128)(2,1)S(1)}, bf16[64,1024]{1,0:T(8,128)(2,1)S(1)}, u32[]{:S(2)}, u32[]{:S(2)}) collective-permute-start(bf16[64,1024]{1,0:T(8,128)(2,1)S(1)} %get-tuple-element.50), channel_id=1, source_target_pairs={{0,1},{1,0},{2,3},{3,2},{4,5},{5,4},{6,7},{7,6},{8,9},{9,8},{10,11... | collective-permute-start | bytes 393224 | tf_op jit(solution)/shard_map/ppermute | solution.py:373
  62.7 5.1 %collective-permute-start.14 = (bf16[64,1024]{1,0:T(8,128)(2,1)S(1)}, bf16[64,1024]{1,0:T(8,128)(2,1)S(1)}, u32[]{:S(2)}, u32[]{:S(2)}) collective-permute-start(bf16[64,1024]{1,0:T(8,128)(2,1)S(1)} %add.11), channel_id=1, source_target_pairs={{0,18},{1,19},{2,16},{3,17},{4,22},{5,23},{6,20},{7,21},{8,26},{9,... | collective-permute-start | bytes 393224 | tf_op jit(solution)/shard_map/ppermute | solution.py:374

commit v6 on v5

--- a/solution.py
+++ b/solution.py
@@ -123,7 +123,7 @@
 
 
 def unpack_kernel(_, g_ref, x_ref, d_ref, ids_ref, in_s):
-    in_s[...] = g_ref[...].reshape(F * STEP, 128).astype(F32)
+    in_s[0:F * STEP] = g_ref[...].reshape(F * STEP, 128).astype(F32)
     for q in range(4):
         ref = (x_ref, d_ref)[q // 2]
         for j in range(8):
@@ -133,14 +133,14 @@
 
 def tail_kernel(g_ref, ids_ref, score_ref, table_ref, in_s, out_s):
     y_hi = lax.axis_index("tp") >> 1
-    in_s[...] = g_ref[...].astype(F32)
+    in_s[0:F * 24] = g_ref[...].astype(F32)
     for p in range(2):
         for j in range(8):
             rows = in_s[pl.ds(p * 8 + j, F, stride=24), :]
             out_s[pl.ds(128 * j + p, F, stride=2), :] = flip_rows(rows, y_hi)
     for j in range(8):
         score_ref[:, 128 * j:128 * j + 128] = out_s[128 * j:128 * j + 128].astype(BF)
-    total = jnp.sum(in_s[...].reshape(F, 24, 128)[:, 16:24], axis=0)
+    total = jnp.sum(in_s[0:F * 24].reshape(F, 24, 128)[:, 16:24], axis=0)
     cols = jnp.concatenate([total[:, 0:64], total[:, 64:128]], axis=0)
     ids = ids_ref[:, 0:1]
     onehot = (ids == lax.broadcasted_iota(jnp.int32, (F, CONCEPTS), 1).astype(F32)).astype(F32)
@@ -353,7 +353,7 @@
         for p in range(2):
             for i in range(2):
                 out_s[pl.ds(8 * p + 2 * j + i, F, stride=16), :] = score[64 * p:64 * p + 64, 128 * i:128 * i + 128]
-    score_ref[...] = out_s[...].astype(BF)
+    score_ref[...] = out_s[0:F * 16].astype(BF)
 
 
 def finish_kernel(score_ref, a_ref, b_ref, c_ref, o_ref, out_s):
@@ -381,8 +381,8 @@
         in_specs=[hbm, hbm, pl.BlockSpec(memory_space=pl.ANY)],
         out_specs=hbm,
         scratch_shapes=[
-            vmem((2 * F, W), BF), vmem((2 * F, W), BF), pltpu.SMEM((1,), jnp.int32), vmem((4 * F * 8, 128), F32),
-            vmem((F * STEP, 128), F32), vmem((F, 9, 4, 128), BF), pltpu.SemaphoreType.DMA((7,))],
+            vmem((2 * F, W), BF), vmem((2 * F, W), BF), pltpu.SMEM((1,), jnp.int32), vmem((4 * F * 8 + 8, 128), F32),
+            vmem((F * STEP + 40, 128), F32), vmem((F, 9, 4, 128), BF), pltpu.SemaphoreType.DMA((7,))],
         compiler_params=pltpu.CompilerParams(vmem_limit_bytes=8 * 1024 * 1024),
         name="pack",
     )(*[pltpu.with_memory_space_constraint(v.reshape(2 * F, W), pltpu.HBM) for v in (latent, direction)], concept)
@@ -405,7 +405,7 @@
 
     half = ((2, F, W), BF)
     x0, d0, ids = local_call(
-        unpack_kernel, (token, got), (half, half, ((F, 2 * W), BF)), (vmem((F * STEP, 128), F32),), 8, "unpack")
+        unpack_kernel, (token, got), (half, half, ((F, 2 * W), BF)), (vmem((F * STEP + 40, 128), F32),), 8, "unpack")
 
     steps = ((0.25 + 1.75 * timestep.astype(F32) / STEPS) / math.sqrt(HD)).reshape(F, 1)
     weights, back_late, mod = local_call(
@@ -442,7 +442,7 @@
          vmem((4, F, W), BF)), 20, "tangent", 1 << 34)
     beside = swap_core(u1)
     score, = local_call(
-        score_kernel, (u0, beside, got_first, got_rest, x0, mod, stat), (((F * 16, 128), BF),), (vmem((F * 16, 128), F32),), 6, "score")
+        score_kernel, (u0, beside, got_first, got_rest, x0, mod, stat), (((F * 16, 128), BF),), (vmem((F * 16 + 16, 128), F32),), 6, "score")
     v_far, v_near = swap_core(v3), swap_core(v1)
     v_sum, = local_call(add_kernel, (got_rest, v2, v_far), (terms,), (), 4, "add")
     v_chip = swap_chip(v_sum)
@@ -452,7 +452,7 @@
     back = lax.all_to_all(ready, "seq", split_axis=0, concat_axis=0, tiled=True)
     score_field, table = local_call(
         tail_kernel, (back, ids_late), (((2 * F, W), BF), ((16, CONCEPTS), F32)),
-        (vmem((F * 24, 128), F32), vmem((2 * F * 8, 128), F32)), 8, "tail")
+        (vmem((F * 24 + 24, 128), F32), vmem((2 * F * 8 + 8, 128), F32)), 8, "tail")
     return (score_field.reshape(1, 2 * F, W), table.T)
 
 

time: 92.9 us -> 92.9 us (level)
  transfers between devices with their start and end apart: 16 -> 16, of which waited for: 8 -> 7; matrix products, arithmetic and copies ran while one was open for 1% -> 1% of each run, Pallas kernels for 24% -> 24%
where the time goes in v6:
time: 92.9 us; the launch traced here: 92.6 us
  blocking collectives  23.8 us (26%)
  starting transfers between devices  23.5 us (25%)
  Pallas kernels  23.4 us (25%)
  waiting for transfers between devices  16.4 us (18%)
  local copies, waits for them, and re-layouts  3.35 us (4%)
  between operations  1.47 us (2%)
    all_to_all x1, blocking collectives, body(): back = lax.all_to_all(ready, 'seq', split_axis=0, concat_axis=0, tiled=True)  23.8 us
    pallas_call x14, Pallas kernels, local_call(): pl.pallas_call(kernel, out_shape=tuple((jax.ShapeDtypeStruct(s, t) for s,...  16.3 us
    all_to_all x1, starting transfers between devices, body(): got = lax.all_to_all(sent, 'seq', split_axis=0, concat_axis=0, tiled=True)  13.4 us
    all_to_all x1, waiting for transfers between devices, body(): got = lax.all_to_all(sent, 'seq', split_axis=0, concat_axis=0, tiled=True)  9.09 us
    ppermute x6, starting transfers between devices, body(): swap_chip = lambda v: lax.ppermute(v, ('seq', 'tp'), cross)  7.52 us
    ppermute x6, waiting for transfers between devices, body(): swap_chip = lambda v: lax.ppermute(v, ('seq', 'tp'), cross)  5.83 us
    pallas_call x1, Pallas kernels, body(): pl.pallas_call(turn_kernel, out_shape=(jax.ShapeDtypeStruct((4, W, W), BF...  4.87 us
    unnamed x2, local copies, waits for them, and re-layouts  3.25 us
  transfers between devices with their start and end apart: 16, of which 7 were waited for; matrix products, arithmetic and copies ran while one was open for 1% of the time, Pallas kernels for 24%

profile of v6, /device:TPU:8, one launch (start us, length us, event | category | flops | bytes accessed | tf_op | source)
XLA Modules:
  0.0 92.6 jit_solution(7845915635559017575)
XLA Ops:
  0.6 1.7 %collective-permute-start.2 = (bf16[256,1024]{1,0:T(8,128)(2,1)}, bf16[256,1024]{1,0:T(8,128)(2,1)S(1)}, u32[]{:S(2)}, u32[]{:S(2)}) collective-permute-start(bf16[256,1024]{1,0:T(8,128)(2,1)} %table_ref.1), channel_id=1, source_target_pairs={{0,18},{1,19},{2,16},{3,17},{4,22},{5,23},{6,20},{7,21},{8,26},{9,... | collective-permute-start | bytes 1572872 | tf_op jit(solution)/shard_map/ppermute | solution.py:374
  2.9 2.2 %pack.1 = bf16[64,9,4,128]{3,2,1,0:T(4,128)(2,1)} custom-call(bf16[128,1024]{1,0:T(8,128)(2,1)} %bitcast.10, bf16[128,1024]{1,0:T(8,128)(2,1)} %bitcast.11, s32[1]{0:T(128)S(6)} %copy.10.concept_ref), custom_call_target="tpu_custom_call" | custom-call | tf_op jit(solution)/shard_map/pack/pallas_call | solution.py:378
  5.2 13.4 %all-to-all-start = ((bf16[64,9,4,128]{3,2,1,0:T(4,128)(2,1)}), bf16[64,9,4,128]{3,2,1,0:T(4,128)(2,1)S(1)}, u32[]{:S(2)}, u32[]{:S(2)}) async-start(bf16[64,9,4,128]{3,2,1,0:T(4,128)(2,1)} %pack.1), calls=%async_computation | async-start | bytes 1179648 | tf_op jit(solution)/shard_map/all_to_all | solution.py:389
  18.5 0.1 collective-permute-start.1
  18.7 0.7 multiply_bitcast_fusion
  19.3 0.1 copy.9.steps_ref
  19.4 0.0 collective-permute-done.2.t2
  19.4 0.6 collective-permute-start.3
  20.0 4.9 %turn.1 = (bf16[4,1024,1024]{2,1,0:T(8,128)(2,1)S(1)}, f32[8,128]{1,0:T(8,128)S(1)}) custom-call(bf16[4096,512]{1,0:T(8,128)(2,1)} %wq_ref.3, bf16[4096,512]{1,0:T(8,128)(2,1)} %wk_ref.3), custom_call_target="tpu_custom_call" | custom-call | flops 8589934592 | bytes 16777216 | tf_op jit(solution)/shard_map/turn/pallas_call | solution.py:391
  24.9 0.0 copy-start
  24.9 3.3 %copy-done = bf16[4,1024,1024]{2,1,0:T(8,128)(2,1)} copy-done((bf16[4,1024,1024]{2,1,0:T(8,128)(2,1)}, bf16[4,1024,1024]{2,1,0:T(8,128)(2,1)S(1)}, u32[]{:S(2)}) %copy-start) | copy-done | bytes 8388632
  28.1 9.1 %all-to-all-done.g_ref = bf16[64,9,4,128]{3,2,1,0:T(4,128)(2,1)S(1)} async-done(((bf16[64,9,4,128]{3,2,1,0:T(4,128)(2,1)}), bf16[64,9,4,128]{3,2,1,0:T(4,128)(2,1)S(1)}, u32[]{:S(2)}, u32[]{:S(2)}) %all-to-all-start) | async-done | bytes 589856 | tf_op jit(solution)/shard_map/all_to_all | solution.py:389
  37.2 0.4 unpack.1
  37.6 0.1 collective-permute-start
  37.7 0.0 collective-permute-done.1.t1
  37.7 0.0 collective-permute-done.3.t3
  37.7 5.8 %prepare.1 = (bf16[4,1024,1024]{2,1,0:T(8,128)(2,1)S(1)}, bf16[3,1024,1024]{2,1,0:T(8,128)(2,1)S(1)}, f32[5,64,1024]{2,1,0:T(8,128)S(1)}) custom-call(bf16[4096,512]{1,0:T(8,128)(2,1)} %wq_ref.3, bf16[4096,512]{1,0:T(8,128)(2,1)} %wk_ref.3, bf16[4,1024,1024]{2,1,0:T(8,128)(2,1)} %copy-done, bf16[256,1024]{1,0:T(8,128)(2,1)} %table_ref.1, ...), custom_call_target="tpu_custom_call" | custom-call | flops 4294967296 | bytes 4096 | tf_op jit(solution)/shard_map/prepare/pallas_call | solution.py:301
  43.5 0.6 collective-permute-done.b_ref._.x2
  44.1 0.1 collective-permute-start.4
  44.2 1.5 %collective-permute-start.10 = (bf16[2,64,1024]{2,1,0:T(8,128)(2,1)S(1)}, bf16[2,64,1024]{2,1,0:T(8,128)(2,1)S(1)}, u32[]{:S(2)}, u32[]{:S(2)}) collective-permute-start(bf16[2,64,1024]{2,1,0:T(8,128)(2,1)S(1)} %relay.2._), channel_id=1, source_target_pairs={{0,18},{1,19},{2,16},{3,17},{4,22},{5,23},{6,20},{7,21},{8,26},{9,... | collective-permute-start | bytes 786440 | tf_op jit(solution)/shard_map/ppermute | solution.py:374
  45.7 0.3 collective-permute-done.4.xn
  46.1 2.7 %latents.1 = (bf16[144,1024]{1,0:T(8,128)(2,1)S(1)}, bf16[64,1024]{1,0:T(8,128)(2,1)S(1)}, bf16[80,1024]{1,0:T(8,128)(2,1)S(1)}, bf16[128,1024]{1,0:T(8,128)(2,1...) custom-call(bf16[2,64,1024]{2,1,0:T(8,128)(2,1)S(1)} %get-tuple-element.31.a_ref.x0.x_ref, ...), custom_call_target="tpu_custom_call" | custom-call | flops 1073741824 | bytes 4096 | tf_op jit(solution)/shard_map/latents/pallas_call | solution.py:301
  48.8 0.2 collective-permute-start.6
  49.0 0.4 collective-permute-start.5
  49.4 1.1 %collective-permute-done.5.low_ref = bf16[64,1024]{1,0:T(8,128)(2,1)S(1)} collective-permute-done((bf16[64,1024]{1,0:T(8,128)(2,1)S(1)}, bf16[64,1024]{1,0:T(8,128)(2,1)S(1)}, u32[]{:S(2)}, u32[]{:S(2)}) %collective-permute-start.5) | collective-permute-done | bytes 131104 | tf_op jit(solution)/shard_map/ppermute | solution.py:373
  50.5 0.0 collective-permute-done.6.high_ref
  50.5 0.1 merge.1
  50.5 1.7 %collective-permute-start.8 = (bf16[32,1024]{1,0:T(8,128)(2,1)S(1)}, bf16[32,1024]{1,0:T(8,128)(2,1)S(1)}, u32[]{:S(2)}, u32[]{:S(2)}) collective-permute-start(bf16[32,1024]{1,0:T(8,128)(2,1)S(1)} %get-tuple-element.40._), channel_id=1, source_target_pairs={{0,18},{1,19},{2,16},{3,17},{4,22},{5,23},{6,20},{7,21},{8,26},{9,... | collective-permute-start | bytes 196616 | tf_op jit(solution)/shard_map/ppermute | solution.py:374
  52.3 2.1 %others.1 = (bf16[1024,1024]{1,0:T(8,128)(2,1)S(1)}, bf16[144,1024]{1,0:T(8,128)(2,1)S(1)}, bf16[144,1024]{1,0:T(8,128)(2,1)S(1)}) custom-call(bf16[4,1024,1024]{2,1,0:T(8,128)(2,1)} %copy-done, bf16[32,1024]{1,0:T(8,128)(2,1)S(1)} %get-tuple-element.40._, bf16[128,1024]{1,0:T(8,128)(2,1)S(1)} %get-tuple-element.41.grad_ref, ...), custom_call_target="tpu_custom_call" | custom-call | flops 4096 | bytes 4096 | tf_op jit(solution)/shard_map/others/pallas_call | solution.py:301
  54.3 0.1 collective-permute-start.7
  54.4 0.0 collective-permute-done.10.b_ref.d2
  54.5 0.6 collective-permute-start.11
  55.0 0.1 collective-permute-done.8._.first_ref
  55.1 1.5 %collective-permute-start.9 = (bf16[112,1024]{1,0:T(8,128)(2,1)S(1)}, bf16[112,1024]{1,0:T(8,128)(2,1)S(1)}, u32[]{:S(2)}, u32[]{:S(2)}) collective-permute-start(bf16[112,1024]{1,0:T(8,128)(2,1)S(1)} %relay.3), channel_id=1, source_target_pairs={{0,18},{1,19},{2,16},{3,17},{4,22},{5,23},{6,20},{7,21},{8,26},{9,... | collective-permute-start | bytes 688136 | tf_op jit(solution)/shard_map/ppermute | solution.py:374
  56.6 0.1 collective-permute-done.11.dn
  56.7 3.8 %tangent.1 = (bf16[64,1024]{1,0:T(8,128)(2,1)S(1)}, bf16[64,1024]{1,0:T(8,128)(2,1)S(1)}, bf16[64,1024]{1,0:T(8,128)(2,1)S(1)}, bf16[64,1024]{1,0:T(8,128)(2,1)S(1)}, f32[64,128]{1,0:T(8,128)S(1)}) custom-call(bf16[2,64,1024]{2,1,0:T(8,128)(2,1)S(1)} %get-tuple-element.31.a_ref.x0.x_ref, bf16[2,64,1024]{2,1,0:T(8,128)(2,1)S(1)} %collective-permute-done.b_ref._.x2, ...), custom_call_target="tpu_custom_call" | custom-call | flops 17179869184 | bytes 4096 | tf_op jit(solution)/shard_map/tangent/pallas_call | solution.py:301
  60.6 0.3 collective-permute-start.13
  60.9 0.3 collective-permute-start.12
  61.2 1.5 %collective-permute-done.9.rest_ref._ = bf16[112,1024]{1,0:T(8,128)(2,1)S(1)} collective-permute-done((bf16[112,1024]{1,0:T(8,128)(2,1)S(1)}, bf16[112,1024]{1,0:T(8,128)(2,1)S(1)}, u32[]{:S(2)}, u32[]{:S(2)}) %collective-permute-start.9) | collective-permute-done | bytes 229408 | tf_op jit(solution)/shard_map/ppermute | solution.py:374
  62.7 0.0 collective-permute-done.13.b_ref
  62.7 1.0 %collective-permute-start.14 = (bf16[64,1024]{1,0:T(8,128)(2,1)S(1)}, bf16[64,1024]{1,0:T(8,128)(2,1)S(1)}, u32[]{:S(2)}, u32[]{:S(2)}) collective-permute-start(bf16[64,1024]{1,0:T(8,128)(2,1)S(1)} %add.11), channel_id=1, source_target_pairs={{0,18},{1,19},{2,16},{3,17},{4,22},{5,23},{6,20},{7,21},{8,26},{9,... | collective-permute-start | bytes 393224 | tf_op jit(solution)/shard_map/ppermute | solution.py:374
  63.7 0.0 collective-permute-done.7.b_ref
  63.7 0.4 score.1.score_ref
  64.1 0.0 collective-permute-done.12.b_ref
  64.1 3.7 %collective-permute-done.14.c_ref = bf16[64,1024]{1,0:T(8,128)(2,1)S(1)} collective-permute-done((bf16[64,1024]{1,0:T(8,128)(2,1)S(1)}, bf16[64,1024]{1,0:T(8,128)(2,1)S(1)}, u32[]{:S(2)}, u32[]{:S(2)}) %collective-permute-start.14) | collective-permute-done | bytes 131104 | tf_op jit(solution)/shard_map/ppermute | solution.py:374
  67.8 0.1 finish.1
  67.8 23.8 %all_to_all.16 = bf16[64,24,128]{2,1,0:T(8,128)(2,1)S(1)} all-to-all(bf16[64,24,128]{2,1,0:T(8,128)(2,1)S(1)} %bitcast.9), channel_id=1, replica_groups=mesh['seq'=64,'tp'=4] {'seq'}, dimensions={0} | all-to-all | bytes 786432 | tf_op jit(solution)/shard_map/all_to_all | solution.py:452
  91.6 1.0 %tail.1 = (bf16[128,1024]{1,0:T(8,128)(2,1)}, f32[16,256]{1,0:T(8,128)}) custom-call(bf16[1536,128]{1,0:T(8,128)(2,1)S(1)} %bitcast.8, f32[64,128]{1,0:T(8,128)S(1)} %get-tuple-element.53.ids_ref), custom_call_target="tpu_custom_call" | custom-call | flops 4096 | bytes 4096 | tf_op jit(solution)/shard_map/tail/pallas_call | solution.py:301
  (5 shorter events, 0.1 us)
Async XLA Ops:
  0.6 18.8 %collective-permute-start.2 = (bf16[256,1024]{1,0:T(8,128)(2,1)}, bf16[256,1024]{1,0:T(8,128)(2,1)S(1)}, u32[]{:S(2)}, u32[]{:S(2)}) collective-permute-start(bf16[256,1024]{1,0:T(8,128)(2,1)} %table_ref.1), channel_id=1, source_target_pairs={{0,18},{1,19},{2,16},{3,17},{4,22},{5,23},{6,20},{7,21},{8,26},{9,... | collective-permute-start | bytes 1572872 | tf_op jit(solution)/shard_map/ppermute | solution.py:374
  5.2 32.1 %all-to-all-start = ((bf16[64,9,4,128]{3,2,1,0:T(4,128)(2,1)}), bf16[64,9,4,128]{3,2,1,0:T(4,128)(2,1)S(1)}, u32[]{:S(2)}, u32[]{:S(2)}) async-start(bf16[64,9,4,128]{3,2,1,0:T(4,128)(2,1)} %pack.1), calls=%async_computation | async-start | bytes 1179648 | tf_op jit(solution)/shard_map/all_to_all | solution.py:389
  18.5 19.1 %collective-permute-start.1 = (bf16[256,1024]{1,0:T(8,128)(2,1)}, bf16[256,1024]{1,0:T(8,128)(2,1)S(1)}, u32[]{:S(2)}, u32[]{:S(2)}) collective-permute-start(bf16[256,1024]{1,0:T(8,128)(2,1)} %table_ref.1), channel_id=1, source_target_pairs={{0,1},{1,0},{2,3},{3,2},{4,5},{5,4},{6,7},{7,6},{8,9},{9,8},{10,11... | collective-permute-start | bytes 1572872 | tf_op jit(solution)/shard_map/ppermute | solution.py:373
  19.4 18.3 %collective-permute-start.3 = (bf16[256,1024]{1,0:T(8,128)(2,1)S(1)}, bf16[256,1024]{1,0:T(8,128)(2,1)S(1)}, u32[]{:S(2)}, u32[]{:S(2)}) collective-permute-start(bf16[256,1024]{1,0:T(8,128)(2,1)S(1)} %collective-permute-done.2.t2), channel_id=1, source_target_pairs={{0,1},{1,0},{2,3},{3,2},{4,5},{5,4},{6,7},{7,6},{8,9},{9,8},{10,11... | collective-permute-start | bytes 1572872 | tf_op jit(solution)/shard_map/ppermute | solution.py:373
  24.9 3.3 %copy-start = (bf16[4,1024,1024]{2,1,0:T(8,128)(2,1)}, bf16[4,1024,1024]{2,1,0:T(8,128)(2,1)S(1)}, u32[]{:S(2)}) copy-start(bf16[4,1024,1024]{2,1,0:T(8,128)(2,1)S(1)} %get-tuple-element.29.turned_ref) | copy-start | bytes 25165828
  37.6 6.5 %collective-permute-start = (bf16[2,64,1024]{2,1,0:T(8,128)(2,1)S(1)}, bf16[2,64,1024]{2,1,0:T(8,128)(2,1)S(1)}, u32[]{:S(2)}, u32[]{:S(2)}) collective-permute-start(bf16[2,64,1024]{2,1,0:T(8,128)(2,1)S(1)} %get-tuple-element.31.a_ref.x0.x_ref), channel_id=1, source_target_pairs={{0,18},{1,19},{2,16},{3,17},{4,22},{5,23},{6,20},{7,21},{8,26},{9,... | collective-permute-start | bytes 786440 | tf_op jit(solution)/shard_map/ppermute | solution.py:374
  44.1 2.0 %collective-permute-start.4 = (bf16[4,64,1024]{2,1,0:T(8,128)(2,1)S(1)}, bf16[4,64,1024]{2,1,0:T(8,128)(2,1)S(1)}, u32[]{:S(2)}, u32[]{:S(2)}) collective-permute-start(bf16[4,64,1024]{2,1,0:T(8,128)(2,1)S(1)} %join.2), channel_id=1, source_target_pairs={{0,1},{1,0},{2,3},{3,2},{4,5},{5,4},{6,7},{7,6},{8,9},{9,8},{10,11... | collective-permute-start | bytes 1572872 | tf_op jit(solution)/shard_map/ppermute | solution.py:373
  44.2 10.2 %collective-permute-start.10 = (bf16[2,64,1024]{2,1,0:T(8,128)(2,1)S(1)}, bf16[2,64,1024]{2,1,0:T(8,128)(2,1)S(1)}, u32[]{:S(2)}, u32[]{:S(2)}) collective-permute-start(bf16[2,64,1024]{2,1,0:T(8,128)(2,1)S(1)} %relay.2._), channel_id=1, source_target_pairs={{0,18},{1,19},{2,16},{3,17},{4,22},{5,23},{6,20},{7,21},{8,26},{9,... | collective-permute-start | bytes 786440 | tf_op jit(solution)/shard_map/ppermute | solution.py:374
  48.8 1.7 %collective-permute-start.6 = (bf16[80,1024]{1,0:T(8,128)(2,1)S(1)}, bf16[80,1024]{1,0:T(8,128)(2,1)S(1)}, u32[]{:S(2)}, u32[]{:S(2)}) collective-permute-start(bf16[80,1024]{1,0:T(8,128)(2,1)S(1)} %get-tuple-element.39.u3_high), channel_id=1, source_target_pairs={{0,1},{1,0},{2,3},{3,2},{4,5},{5,4},{6,7},{7,6},{8,9},{9,8},{10,11... | collective-permute-start | bytes 491528 | tf_op jit(solution)/shard_map/ppermute | solution.py:373
  49.0 1.4 %collective-permute-start.5 = (bf16[64,1024]{1,0:T(8,128)(2,1)S(1)}, bf16[64,1024]{1,0:T(8,128)(2,1)S(1)}, u32[]{:S(2)}, u32[]{:S(2)}) collective-permute-start(bf16[64,1024]{1,0:T(8,128)(2,1)S(1)} %get-tuple-element.38.u3_low), channel_id=1, source_target_pairs={{0,1},{1,0},{2,3},{3,2},{4,5},{5,4},{6,7},{7,6},{8,9},{9,8},{10,11... | collective-permute-start | bytes 393224 | tf_op jit(solution)/shard_map/ppermute | solution.py:373
  50.5 4.5 %collective-permute-start.8 = (bf16[32,1024]{1,0:T(8,128)(2,1)S(1)}, bf16[32,1024]{1,0:T(8,128)(2,1)S(1)}, u32[]{:S(2)}, u32[]{:S(2)}) collective-permute-start(bf16[32,1024]{1,0:T(8,128)(2,1)S(1)} %get-tuple-element.40._), channel_id=1, source_target_pairs={{0,18},{1,19},{2,16},{3,17},{4,22},{5,23},{6,20},{7,21},{8,26},{9,... | collective-permute-start | bytes 196616 | tf_op jit(solution)/shard_map/ppermute | solution.py:374
  54.3 9.4 %collective-permute-start.7 = (bf16[144,1024]{1,0:T(8,128)(2,1)S(1)}, bf16[144,1024]{1,0:T(8,128)(2,1)S(1)}, u32[]{:S(2)}, u32[]{:S(2)}) collective-permute-start(bf16[144,1024]{1,0:T(8,128)(2,1)S(1)} %get-tuple-element.43.u1), channel_id=1, source_target_pairs={{0,1},{1,0},{2,3},{3,2},{4,5},{5,4},{6,7},{7,6},{8,9},{9,8},{10,11... | collective-permute-start | bytes 884744 | tf_op jit(solution)/shard_map/ppermute | solution.py:373
  54.5 2.3 %collective-permute-start.11 = (bf16[4,64,1024]{2,1,0:T(8,128)(2,1)S(1)}, bf16[4,64,1024]{2,1,0:T(8,128)(2,1)S(1)}, u32[]{:S(2)}, u32[]{:S(2)}) collective-permute-start(bf16[4,64,1024]{2,1,0:T(8,128)(2,1)S(1)} %join.3), channel_id=1, source_target_pairs={{0,1},{1,0},{2,3},{3,2},{4,5},{5,4},{6,7},{7,6},{8,9},{9,8},{10,11... | collective-permute-start | bytes 1572872 | tf_op jit(solution)/shard_map/ppermute | solution.py:373
  55.1 7.6 %collective-permute-start.9 = (bf16[112,1024]{1,0:T(8,128)(2,1)S(1)}, bf16[112,1024]{1,0:T(8,128)(2,1)S(1)}, u32[]{:S(2)}, u32[]{:S(2)}) collective-permute-start(bf16[112,1024]{1,0:T(8,128)(2,1)S(1)} %relay.3), channel_id=1, source_target_pairs={{0,18},{1,19},{2,16},{3,17},{4,22},{5,23},{6,20},{7,21},{8,26},{9,... | collective-permute-start | bytes 688136 | tf_op jit(solution)/shard_map/ppermute | solution.py:374
  60.6 2.1 %collective-permute-start.13 = (bf16[64,1024]{1,0:T(8,128)(2,1)S(1)}, bf16[64,1024]{1,0:T(8,128)(2,1)S(1)}, u32[]{:S(2)}, u32[]{:S(2)}) collective-permute-start(bf16[64,1024]{1,0:T(8,128)(2,1)S(1)} %get-tuple-element.52), channel_id=1, source_target_pairs={{0,1},{1,0},{2,3},{3,2},{4,5},{5,4},{6,7},{7,6},{8,9},{9,8},{10,11... | collective-permute-start | bytes 393224 | tf_op jit(solution)/shard_map/ppermute | solution.py:373
  60.9 3.2 %collective-permute-start.12 = (bf16[64,1024]{1,0:T(8,128)(2,1)S(1)}, bf16[64,1024]{1,0:T(8,128)(2,1)S(1)}, u32[]{:S(2)}, u32[]{:S(2)}) collective-permute-start(bf16[64,1024]{1,0:T(8,128)(2,1)S(1)} %get-tuple-element.50), channel_id=1, source_target_pairs={{0,1},{1,0},{2,3},{3,2},{4,5},{5,4},{6,7},{7,6},{8,9},{9,8},{10,11... | collective-permute-start | bytes 393224 | tf_op jit(solution)/shard_map/ppermute | solution.py:373
  62.7 5.1 %collective-permute-start.14 = (bf16[64,1024]{1,0:T(8,128)(2,1)S(1)}, bf16[64,1024]{1,0:T(8,128)(2,1)S(1)}, u32[]{:S(2)}, u32[]{:S(2)}) collective-permute-start(bf16[64,1024]{1,0:T(8,128)(2,1)S(1)} %add.11), channel_id=1, source_target_pairs={{0,18},{1,19},{2,16},{3,17},{4,22},{5,23},{6,20},{7,21},{8,26},{9,... | collective-permute-start | bytes 393224 | tf_op jit(solution)/shard_map/ppermute | solution.py:374
